TPU v7x, 128 devices: a whole 4x4x4 slice. The times are simulated.
128 devices in a mesh: dp: 32 (over y, x, core), seq: 4 (over z).
Axes of the slice: x: 4, y: 4, z: 4, core: 2. Of those that a mesh axis runs over, the one named last changes fastest.
Arguments:
- token_rows: bfloat16 [163840, 5120], P(('dp', 'seq')), may hold values from -6 to 6
- key_rows: bfloat16 [163840, 128], P(('dp', 'seq')), may hold values from -1.8 to 1.8
- query_rows: bfloat16 [163840, 128], P(('dp', 'seq')), may hold values from -0.1796875 to 0.1796875
- step_rows: bfloat16 [163840, 80], P(('dp', 'seq')), may hold values from -6 to 1000
- decay_log: float32 [80], replicated, may hold values from -9.3 to -1.8
- skip_gain: float32 [80], replicated, may hold values from 0.5 to 1.5
- source_rows: int32 [32, 5120], P('dp', 'seq'), may hold values from 0 to 163839, as said below
- document_starts: int32 [32, 6], P('dp'), may hold values from 0 to 5119, as said below
Outputs:
- layer_result_rows: bfloat16 [32, 5120, 5120], P('dp', 'seq')
Inputs may be any that keep to these rules, and one draw needn't show every extreme that they name: `source_rows`: every loaded row is placed exactly once. The row at position p of a packed sequence is held by a device whose seq index is p // 1280. Positions come in aligned runs of 8 that hold consecutive rows of one device. A device takes at most 48 of its positions from any one device, and in every seq index some pair of devices reaches that number. `document_starts`: each row is strictly increasing and begins with 0.
All inputs are finite; a program needn't handle non-finite values.
Results may differ from a plain program's by a relative error of at most 0.0065.
Values may be sent and summed in bfloat16 or wider, within the bound.
No kernel may reach another device: no remote copies, remote signals or barrier semaphores. Data moves between devices by JAX's collectives and lax.ppermute only.
A program may use at most 192 MiB of HBM per device.

v0:
```python
import jax
import jax.numpy as jnp
from jax import lax
from jax.sharding import PartitionSpec as P

SPAN = 256
SEG = 8


highest = lax.Precision.HIGHEST


def shifted(block, axis, distance):
    devices = range(lax.axis_size(axis))
    route = [(i - distance, i) for i in devices if i - distance in devices]
    return lax.ppermute(block, axis, route)


def span_pass(
    carried,
    values_heads,
    keys_span,
    query_span,
    scores,
    steps_heads,
    restart,
    decay_rate,
    skip_part,
):
    log_decay = -steps_heads * decay_rate[:, None]
    running_total = jnp.cumsum(log_decay, axis=1)
    document = jnp.cumsum(restart.astype(jnp.int32))
    position = jnp.arange(restart.shape[0])
    linked = (document[:, None] == document[None, :]) & (position[None, :] <= position[:, None])
    decay_gap = running_total[:, :, None] - running_total[:, None, :]
    masked_gap = jnp.where(linked[None], decay_gap, -jnp.inf)
    weights = (scores[None] * jnp.exp(masked_gap) * steps_heads[:, None, :]).astype(jnp.bfloat16)
    within = jnp.einsum("hts,hsp->htp", weights, values_heads, preferred_element_type=jnp.float32)
    entry_decay = jnp.where((document == 0)[None, :], jnp.exp(running_total), 0.0)
    from_state = (
        jnp.einsum("tn,hnp->htp", query_span.astype(jnp.float32), carried, precision=highest)
        * entry_decay[:, :, None]
    )
    to_end = running_total[:, -1:] - running_total
    end_weight = jnp.where((document == document[-1])[None, :], jnp.exp(to_end), 0.0) * steps_heads
    scaled_values = (values_heads.astype(jnp.float32) * end_weight[:, :, None]).astype(jnp.bfloat16)
    added_state = jnp.einsum(
        "sn,hsp->hnp", keys_span, scaled_values, preferred_element_type=jnp.float32
    )
    retained = jnp.where(document[-1] == 0, jnp.exp(running_total[:, -1]), 0.0)
    carried = retained[:, None, None] * carried + added_state
    result = within + from_state + skip_part[:, None, None] * values_heads.astype(jnp.float32)
    return (carried, result)


def on_device(
    token_rows, key_rows, query_rows, step_rows, decay_log, skip_gain, source_rows, document_starts
):
    tokens = token_rows.shape[0]
    packing_peers = lax.axis_size("dp")
    sequence_shards = lax.axis_size("seq")
    head_count = decay_log.shape[0]
    head_width = token_rows.shape[1] // head_count
    state_width = key_rows.shape[1]
    span_count = tokens // SPAN
    wanted = source_rows[0]
    device_of = wanted // tokens
    source_group = device_of // sequence_shards
    local_row = wanted % tokens
    onehot = (source_group[:, None] == jnp.arange(packing_peers)[None, :]).astype(jnp.int32)
    ranking = jnp.sum((jnp.cumsum(onehot, axis=0) - 1) * onehot, axis=1)
    capacity = SEG * (tokens // (SEG * packing_peers) + 1)
    pick_index = source_group * capacity + ranking
    slot_match = pick_index[:, None] == jnp.arange(packing_peers * capacity)[None, :]
    requests = jnp.sum(jnp.where(slot_match, local_row[:, None], 0), axis=0)
    requests = requests.reshape(packing_peers, capacity)
    asked_rows = lax.all_to_all(requests, "dp", split_axis=0, concat_axis=0, tiled=True)

    def arrange(received):
        flat = received.reshape((received.shape[0] * received.shape[1],) + received.shape[2:])
        return jnp.take(flat, pick_index, axis=0)

    arrived = (
        lax.all_to_all(
            jnp.take(token_rows, asked_rows, axis=0), "dp", split_axis=0, concat_axis=0, tiled=True
        ),
        lax.all_to_all(
            jnp.take(key_rows, asked_rows, axis=0), "dp", split_axis=0, concat_axis=0, tiled=True
        ),
        lax.all_to_all(
            jnp.take(query_rows, asked_rows, axis=0), "dp", split_axis=0, concat_axis=0, tiled=True
        ),
        lax.all_to_all(
            jnp.take(step_rows, asked_rows, axis=0), "dp", split_axis=0, concat_axis=0, tiled=True
        ),
    )
    packed_values = arrange(arrived[0])
    packed_keys = arrange(arrived[1])
    packed_query = arrange(arrived[2])
    packed_step = arrange(arrived[3])
    position = lax.axis_index("seq") * tokens + jnp.arange(tokens)
    restart = jnp.any(position[:, None] == document_starts[0][None, :], axis=1)
    restarts_seen = jnp.cumsum(restart.astype(jnp.int32))
    steps_heads_all = jax.nn.softplus(packed_step.astype(jnp.float32)).T
    key_spans = packed_keys.reshape(span_count, SPAN, state_width)
    query_spans = packed_query.reshape(span_count, SPAN, state_width)
    scores = jnp.einsum("ctn,csn->cts", query_spans, key_spans, preferred_element_type=jnp.float32)
    query_float = packed_query.astype(jnp.float32)
    decay_rate = jnp.exp(decay_log)
    values_heads = packed_values.reshape(tokens, head_count, head_width).transpose(1, 0, 2)
    final_state = jnp.zeros((head_count, state_width, head_width), jnp.float32)
    span_results = []
    for span_number in range(span_count):
        low = span_number * SPAN
        final_state, span_out = span_pass(
            final_state,
            values_heads[:, low : low + SPAN],
            key_spans[span_number],
            query_spans[span_number],
            scores[span_number],
            steps_heads_all[:, low : low + SPAN],
            restart[low : low + SPAN],
            decay_rate,
            skip_gain,
        )
        span_results.append(span_out)
    local_part = jnp.concatenate(span_results, axis=1)
    running_total = jnp.cumsum(-steps_heads_all * decay_rate[:, None], axis=1)
    entry_decay = jnp.where((restarts_seen == 0)[None, :], jnp.exp(running_total), 0.0)
    through = jnp.where(restarts_seen[-1] == 0, jnp.exp(running_total[:, -1]), 0.0)
    incoming = jnp.zeros_like(final_state)
    for link_step in range(sequence_shards - 1):
        outgoing = through[:, None, None] * incoming + final_state
        incoming = shifted(outgoing.astype(jnp.bfloat16), "seq", 1).astype(outgoing.dtype)
    correction = (
        jnp.einsum("tn,hnp->htp", query_float, incoming, precision=highest)
        * entry_decay[:, :, None]
    )
    combined = (local_part + correction).astype(jnp.bfloat16)
    layer_result_rows = combined.transpose(1, 0, 2).reshape(tokens, head_count * head_width)
    return layer_result_rows[None]


def solution(mesh):
    in_specs = (
        P(("dp", "seq"), None),
        P(("dp", "seq"), None),
        P(("dp", "seq"), None),
        P(("dp", "seq"), None),
        P(),
        P(),
        P("dp", "seq"),
        P("dp", None),
    )
    out_specs = P("dp", "seq", None)
    return jax.shard_map(
        on_device, mesh=mesh, in_specs=in_specs, out_specs=out_specs, check_vma=False
    )
```

profile of v0, /device:TPU:44, one launch (start us, length us, event | category | flops | bytes accessed | tf_op | source)
XLA Modules:
  0.0 505.0 jit_solution(11372786426406007385)
XLA Ops:
  1.6 9.1 %reduce-window.96 = s32[32,10,128]{2,1,0:T(8,128)S(1)} reduce-window(s32[32,10,128]{2,1,0:T(8,128)S(1)} %fusion.101, s32[]{:T(128)} %constant.135.clone.1), window={size=1x1x128 pad=0_0x0_0x127_0}, to_apply=%region_0.1 | reduce-window | flops 5201920 | bytes 327684 | tf_op jit(solution)/shard_map/reduce-window
  13.0 7.5 %all-to-all-start = ((s32[32,1,48]{2,1,0:T(1,128)}), s32[32,1,48]{2,1,0:T(1,128)S(1)}, u32[]{:S(2)}, u32[]{:S(2)}) async-start(s32[32,1,48]{2,1,0:T(1,128)} %all_to_all.22), calls=%async_computation | async-start | bytes 32768 | tf_op jit(solution)/shard_map/all_to_all | solution.py:77
  25.0 3.2 gather_fusion
  29.2 6.8 %all-to-all-start.3 = ((bf16[32,48,80]{2,1,0:T(8,128)(2,1)}), bf16[32,48,80]{2,1,0:T(8,128)(2,1)S(1)}, u32[]{:S(2)}, u32[]{:S(2)}) async-start(bf16[32,48,80]{2,1,0:T(8,128)(2,1)} %broadcast_select_fusion.3), calls=%async_computation.3 | async-start | bytes 786432 | tf_op jit(solution)/shard_map/all_to_all | solution.py:93
  39.3 3.2 gather_fusion.4
  43.7 7.4 %all-to-all-start.2 = ((bf16[32,48,128]{2,1,0:T(8,128)(2,1)}), bf16[32,48,128]{2,1,0:T(8,128)(2,1)S(1)}, u32[]{:S(2)}, u32[]{:S(2)}) async-start(bf16[32,48,128]{2,1,0:T(8,128)(2,1)} %get-tuple-element.51), calls=%async_computation.2 | async-start | bytes 786432 | tf_op jit(solution)/shard_map/all_to_all | solution.py:87
  51.1 33.8 %gather_fusion.2 = bf16[1536,5120]{1,0:T(8,128)(2,1)} fusion(bf16[1280,5120]{1,0:T(8,128)(2,1)} %param.12, s32[2048]{0:T(1024)S(1)} %get-tuple-element.62), kind=kCustom, calls=%fused_computation.6 | custom fusion | bytes 31463424 | tf_op jit(solution)/shard_map/jit(_take)/gather | solution.py:85
  85.0 7.4 %all-to-all-start.1 = ((bf16[32,48,128]{2,1,0:T(8,128)(2,1)}), bf16[32,48,128]{2,1,0:T(8,128)(2,1)S(1)}, u32[]{:S(2)}, u32[]{:S(2)}) async-start(bf16[32,48,128]{2,1,0:T(8,128)(2,1)} %get-tuple-element.52), calls=%async_computation.1 | async-start | bytes 786432 | tf_op jit(solution)/shard_map/all_to_all | solution.py:90
  92.4 13.6 %broadcast_select_fusion = bf16[32,48,5120]{2,1,0:T(8,128)(2,1)} fusion(bf16[32,48,5120]{2,1,0:T(8,128)(2,1)} %bitcast.232, pred[32,48]{1,0:T(8,128)(4,1)S(1)} %compare_and_fusion.1), kind=kLoop, calls=%fused_computation.15 | loop fusion | flops 7864320 | bytes 31458816 | tf_op jit(solution)/shard_map/jit(_take)/select_n | solution.py:85
  106.0 7.6 %all-to-all-start.4 = ((bf16[32,48,5120]{2,1,0:T(8,128)(2,1)}), bf16[32,48,5120]{2,1,0:T(8,128)(2,1)}, u32[]{:S(2)}, u32[]{:S(2)}) async-start(bf16[32,48,5120]{2,1,0:T(8,128)(2,1)} %broadcast_select_fusion), calls=%async_computation.4 | async-start | bytes 31457280 | tf_op jit(solution)/shard_map/all_to_all | solution.py:84
  162.6 22.7 %reduce-window.160 = f32[80,10,128]{2,1,0:T(8,128)S(1)} reduce-window(f32[80,10,128]{2,1,0:T(8,128)S(1)} %copy.218, f32[]{:T(128)} %constant.146.clone.1), window={size=1x1x128 pad=0_0x0_0x127_0}, to_apply=%region_27.30 | reduce-window | flops 13004800 | bytes 819204 | tf_op jit(solution)/shard_map/reduce-window.24
  194.5 113.9 %all-to-all-done.4 = bf16[32,48,5120]{2,1,0:T(8,128)(2,1)} async-done(((bf16[32,48,5120]{2,1,0:T(8,128)(2,1)}), bf16[32,48,5120]{2,1,0:T(8,128)(2,1)}, u32[]{:S(2)}, u32[]{:S(2)}) %all-to-all-start.4) | async-done | bytes 15728672 | tf_op jit(solution)/shard_map/all_to_all | solution.py:84
  308.4 30.8 %gather_fusion.3 = bf16[1280,5120]{1,0:T(8,128)(2,1)} fusion(bf16[1536,5120]{1,0:T(8,128)(2,1)} %bitcast.21, s32[2048]{0:T(1024)S(1)} %copy-done.26), kind=kCustom, calls=%fused_computation.7 | custom fusion | bytes 26219520 | tf_op jit(solution)/shard_map/jit(_take)/gather | solution.py:81
  339.2 17.6 %copy.187 = bf16[1280,5120]{0,1:T(8,128)(2,1)} copy(bf16[1280,5120]{1,0:T(8,128)(2,1)} %gather_fusion.3) | data formatting | bytes 26214400 | tf_op jit(solution)/shard_map/jit(_take)/gather | solution.py:81
  356.8 6.6 %select_bitcast_fusion = bf16[80,1280,64]{1,2,0:T(8,128)(2,1)S(1)} fusion(bf16[1280,80,64]{0,2,1:T(8,128)(2,1)} %bitcast.234, pred[1280]{0:T(1024)(128)(4,1)S(1)} %copy-done.34), kind=kLoop, calls=%fused_computation.16 | loop fusion | flops 6553600 | bytes 26215680 | tf_op jit(solution)/shard_map/transpose | solution.py:110
  368.0 3.8 collective-permute-start
  371.9 7.3 %fusion.1 = f32[80,256,64]{1,2,0:T(8,128)} fusion(f32[80,256]{1,0:T(8,128)S(1)} %copy-done.19, f32[80,256]{1,0:T(8,128)S(1)} %copy-done.6, f32[256,256]{1,0:T(8,128)S(1)} %get-tuple-element.29, pred[256,256]{1,0:T(8,128)(4,1)S(1)} %copy-done.31, bf16[80,1280,64]{1,2,0:T(8,128)(2,1)S(1)} %select_bitcast_fusion), kind=kOutput, calls=%fused_computation.17 | convolution fusion | flops 697303040 | bytes 8437760 | tf_op jit(solution)/shard_map/hts,hsp->htp/dot_general | solution.py:38
  379.2 5.4 %fusion.2 = f32[80,256,64]{1,2,0:T(8,128)S(1)} fusion(f32[80,256]{1,0:T(8,128)S(1)} %copy-done.20, f32[80,256]{1,0:T(8,128)S(1)} %copy-done.8, f32[256,256]{1,0:T(8,128)S(1)} %get-tuple-element.28, pred[256,256]{1,0:T(8,128)(4,1)S(1)} %copy-done.30, bf16[80,1280,64]{1,2,0:T(8,128)(2,1)S(1)} %select_bitcast_fusion), kind=kOutput, calls=%fused_computation.18 | convolution fusion | flops 697303040 | bytes 8437760 | tf_op jit(solution)/shard_map/hts,hsp->htp/dot_general | solution.py:38
  384.7 7.1 %fusion.3 = f32[80,256,64]{1,2,0:T(8,128)} fusion(f32[80,256]{1,0:T(8,128)S(1)} %copy-done.22, f32[80,256]{1,0:T(8,128)S(1)} %copy-done.10, f32[256,256]{1,0:T(8,128)S(1)} %get-tuple-element.27, pred[256,256]{1,0:T(8,128)(4,1)S(1)} %copy-done.29, bf16[80,1280,64]{1,2,0:T(8,128)(2,1)S(1)} %select_bitcast_fusion), kind=kOutput, calls=%fused_computation.19 | convolution fusion | flops 697303040 | bytes 8437760 | tf_op jit(solution)/shard_map/hts,hsp->htp/dot_general | solution.py:38
  391.7 7.5 %fusion.37 = f32[80,1280,64]{1,2,0:T(8,128)} fusion(f32[80,256,64]{1,2,0:T(8,128)} %fusion.1, f32[80]{0:T(128)S(1)} %copy-done.35, f32[80,256]{1,0:T(8,128)S(1)} %copy-done.11, bf16[80,1280,64]{1,2,0:T(8,128)(2,1)S(1)} %select_bitcast_fusion, bf16[1280,128]{1,0:T(8,128)(2,1)S(1)} %get-tuple-element.59), kind=kOutput, calls=%fused_computation.65 | convolution fusion | flops 2019819520 | bytes 13255168 | tf_op jit(solution)/shard_map/tn,hnp->htp/dot_general | solution.py:41
  399.2 7.1 %fusion.4 = f32[80,256,64]{1,2,0:T(8,128)} fusion(f32[80,256]{1,0:T(8,128)S(1)} %copy-done.23, f32[80,256]{1,0:T(8,128)S(1)} %copy_bitcast_fusion.2, f32[256,256]{1,0:T(8,128)S(1)} %get-tuple-element.26, pred[256,256]{1,0:T(8,128)(4,1)S(1)} %copy-done.28, bf16[80,1280,64]{1,2,0:T(8,128)(2,1)S(1)} %select_bitcast_fusion), kind=kOutput, calls=%fused_computation.20 | convolution fusion | flops 697303040 | bytes 8437760 | tf_op jit(solution)/shard_map/hts,hsp->htp/dot_general | solution.py:38
  407.8 3.7 collective-permute-start.1
  411.6 4.4 fusion.40
  416.0 7.1 %fusion.5 = f32[80,256,64]{1,2,0:T(8,128)} fusion(f32[80,256]{1,0:T(8,128)S(1)} %copy-done.21, f32[80,256]{1,0:T(8,128)S(1)} %copy-done.4, f32[256,256]{1,0:T(8,128)S(1)} %copy-done.18, pred[256,256]{1,0:T(8,128)(4,1)S(1)} %copy-done.27, bf16[80,1280,64]{1,2,0:T(8,128)(2,1)S(1)} %select_bitcast_fusion), kind=kOutput, calls=%fused_computation.21 | convolution fusion | flops 697303040 | bytes 8437760 | tf_op jit(solution)/shard_map/hts,hsp->htp/dot_general | solution.py:38
  423.1 17.0 %collective-permute-done.1 = bf16[80,128,64]{1,2,0:T(8,128)(2,1)S(1)} collective-permute-done((bf16[80,128,64]{1,2,0:T(8,128)(2,1)}, bf16[80,128,64]{1,2,0:T(8,128)(2,1)S(1)}, u32[]{:S(2)}, u32[]{:S(2)}) %collective-permute-start.1) | collective-permute-done | bytes 1310752 | tf_op jit(solution)/shard_map/ppermute | solution.py:16
  440.6 3.9 collective-permute-start.2
  444.5 5.0 fusion.43
  449.6 7.5 %fusion.46 = f32[80,1280,64]{1,2,0:T(8,128)} fusion(f32[80,1280,64]{1,2,0:T(8,128)} %fusion.43, f32[80,256,64]{1,2,0:T(8,128)} %fusion.4, f32[80,256]{1,0:T(8,128)S(1)} %copy-done.16, f32[80]{0:T(128)S(1)} %copy-done.35, f32[80,128,64]{1,2,0:T(8,128)S(1)} %bitcast_add_fusion.8, bf16[80,1280,64]{1,2,0:T(8,128)(2,1)S(1)} %select_bitcast_fusion, ...), kind=kOutput, calls=%fused_computation.74 | convolution fusion | flops 2019819520 | bytes 15876608 | tf_op jit(solution)/shard_map/tn,hnp->htp/dot_general | solution.py:41
  457.1 5.1 %fusion.49 = f32[80,1280,64]{1,2,0:T(8,128)} fusion(f32[80,1280,64]{1,2,0:T(8,128)} %fusion.46, f32[80,256,64]{1,2,0:T(8,128)S(1)} %bitcast.242, f32[80,256]{1,0:T(8,128)S(1)} %copy-done.17, f32[80]{0:T(128)S(1)} %copy-done.35, f32[80,128,64]{1,2,0:T(8,128)S(1)} %bitcast_add_fusion.7, bf16[80,1280,64]{1,2,0:T(8,128)(2,1)S(1)} %select_bitcast_fusion, ...), kind=kOutput, calls=%fused_computation.77 | convolution fusion | flops 2019819520 | bytes 15876608 | tf_op jit(solution)/shard_map/tn,hnp->htp/dot_general | solution.py:41
  462.2 9.5 %collective-permute-done.2 = bf16[80,128,64]{1,2,0:T(8,128)(2,1)S(1)} collective-permute-done((bf16[80,128,64]{1,2,0:T(8,128)(2,1)S(1)}, bf16[80,128,64]{1,2,0:T(8,128)(2,1)S(1)}, u32[]{:S(2)}, u32[]{:S(2)}) %collective-permute-start.2) | collective-permute-done | bytes 1310752 | tf_op jit(solution)/shard_map/ppermute | solution.py:16
  471.7 15.2 %fusion = bf16[80,1280,64]{1,2,0:T(8,128)(2,1)} fusion(f32[80,1280,64]{1,2,0:T(8,128)} %fusion.49, bf16[80,128,64]{1,2,0:T(8,128)(2,1)S(1)} %collective-permute-done.2, f32[80,1280]{1,0:T(8,128)S(1)} %copy.224, bf16[1280,128]{1,0:T(8,128)(2,1)S(1)} %get-tuple-element.59), kind=kOutput, calls=%fused_computation.9 | convolution fusion | flops 1697382400 | bytes 41369600 | tf_op jit(solution)/shard_map/tn,hnp->htp/dot_general | solution.py:136
  486.9 17.6 %copy.225 = bf16[1,1280,5120]{2,1,0:T(8,128)(2,1)} copy(bf16[1,1280,5120]{1,2,0:T(8,128)(2,1)} %bitcast.233) | data formatting | bytes 26214400 | tf_op jit(solution)/shard_map/broadcast_in_dim;reshape | solution.py:141
  (275 shorter events, 74.2 us)
Async XLA Ops:
  0.0 36.1 %copy-start = (bf16[1280,128]{1,0:T(8,128)(2,1)S(1)}, bf16[1280,128]{1,0:T(8,128)(2,1)}, u32[]{:S(2)}) copy-start(bf16[1280,128]{1,0:T(8,128)(2,1)} %param.13) | copy-start | bytes 983044
  11.0 28.3 %copy-start.2 = (bf16[1280,128]{1,0:T(8,128)(2,1)S(1)}, bf16[1280,128]{1,0:T(8,128)(2,1)}, u32[]{:S(2)}) copy-start(bf16[1280,128]{1,0:T(8,128)(2,1)} %param.14) | copy-start | bytes 983044
  13.0 11.8 %all-to-all-start = ((s32[32,1,48]{2,1,0:T(1,128)}), s32[32,1,48]{2,1,0:T(1,128)S(1)}, u32[]{:S(2)}, u32[]{:S(2)}) async-start(s32[32,1,48]{2,1,0:T(1,128)} %all_to_all.22), calls=%async_computation | async-start | bytes 32768 | tf_op jit(solution)/shard_map/all_to_all | solution.py:77
  29.2 14.5 %all-to-all-start.3 = ((bf16[32,48,80]{2,1,0:T(8,128)(2,1)}), bf16[32,48,80]{2,1,0:T(8,128)(2,1)S(1)}, u32[]{:S(2)}, u32[]{:S(2)}) async-start(bf16[32,48,80]{2,1,0:T(8,128)(2,1)} %broadcast_select_fusion.3), calls=%async_computation.3 | async-start | bytes 786432 | tf_op jit(solution)/shard_map/all_to_all | solution.py:93
  43.7 41.3 %all-to-all-start.2 = ((bf16[32,48,128]{2,1,0:T(8,128)(2,1)}), bf16[32,48,128]{2,1,0:T(8,128)(2,1)S(1)}, u32[]{:S(2)}, u32[]{:S(2)}) async-start(bf16[32,48,128]{2,1,0:T(8,128)(2,1)} %get-tuple-element.51), calls=%async_computation.2 | async-start | bytes 786432 | tf_op jit(solution)/shard_map/all_to_all | solution.py:87
  85.0 21.0 %all-to-all-start.1 = ((bf16[32,48,128]{2,1,0:T(8,128)(2,1)}), bf16[32,48,128]{2,1,0:T(8,128)(2,1)S(1)}, u32[]{:S(2)}, u32[]{:S(2)}) async-start(bf16[32,48,128]{2,1,0:T(8,128)(2,1)} %get-tuple-element.52), calls=%async_computation.1 | async-start | bytes 786432 | tf_op jit(solution)/shard_map/all_to_all | solution.py:90
  106.0 21.8 %copy-start.32 = (s32[1,1280]{1,0:T(1,128)S(1)}, s32[1,1280]{1,0:T(1,128)}, u32[]{:S(2)}) copy-start(s32[1,1280]{1,0:T(1,128)} %param.18) | copy-start | bytes 15364
  106.0 202.4 %all-to-all-start.4 = ((bf16[32,48,5120]{2,1,0:T(8,128)(2,1)}), bf16[32,48,5120]{2,1,0:T(8,128)(2,1)}, u32[]{:S(2)}, u32[]{:S(2)}) async-start(bf16[32,48,5120]{2,1,0:T(8,128)(2,1)} %broadcast_select_fusion), calls=%async_computation.4 | async-start | bytes 31457280 | tf_op jit(solution)/shard_map/all_to_all | solution.py:84
  127.9 9.0 %copy-start.25 = (s32[2048]{0:T(1024)}, s32[2048]{0:T(1024)S(1)}, u32[]{:S(2)}) copy-start(s32[2048]{0:T(1024)S(1)} %pad_clamp_fusion) | copy-start | bytes 24580
  140.3 12.1 %copy-start.39 = (pred[256]{0:T(512)(128)(4,1)S(1)}, pred[256]{0:T(512)(128)(4,1)}, u32[]{:S(2)}) copy-start(pred[256]{0:T(512)(128)(4,1)} %get-tuple-element.64) | copy-start | bytes 772
  140.3 12.1 %copy-start.40 = (pred[256]{0:T(512)(128)(4,1)S(1)}, pred[256]{0:T(512)(128)(4,1)}, u32[]{:S(2)}) copy-start(pred[256]{0:T(512)(128)(4,1)} %get-tuple-element.65) | copy-start | bytes 772
  140.3 12.1 %copy-start.41 = (pred[256]{0:T(512)(128)(4,1)S(1)}, pred[256]{0:T(512)(128)(4,1)}, u32[]{:S(2)}) copy-start(pred[256]{0:T(512)(128)(4,1)} %get-tuple-element.66) | copy-start | bytes 772
  140.3 12.1 %copy-start.42 = (pred[256]{0:T(512)(128)(4,1)S(1)}, pred[256]{0:T(512)(128)(4,1)}, u32[]{:S(2)}) copy-start(pred[256]{0:T(512)(128)(4,1)} %get-tuple-element.67) | copy-start | bytes 772
  140.3 16.3 %copy-start.38 = (pred[256]{0:T(512)(128)(4,1)S(1)}, pred[256]{0:T(512)(128)(4,1)}, u32[]{:S(2)}) copy-start(pred[256]{0:T(512)(128)(4,1)} %get-tuple-element.15) | copy-start | bytes 772
  141.3 20.0 %copy-start.37 = (pred[256]{0:T(512)(128)(4,1)S(1)}, pred[256]{0:T(512)(128)(4,1)}, u32[]{:S(2)}) copy-start(pred[256]{0:T(512)(128)(4,1)} %get-tuple-element.11) | copy-start | bytes 772
  144.3 8.0 %copy-start.5 = (f32[80,256]{1,0:T(8,128)}, f32[80,256]{1,0:T(8,128)S(1)}, u32[]{:S(2)}) copy-start(f32[80,256]{1,0:T(8,128)S(1)} %copy_bitcast_fusion.5) | copy-start | bytes 245764
  156.6 30.1 %copy-start.36 = (pred[1280]{0:T(1024)(128)(4,1)S(1)}, pred[1280]{0:T(1024)(128)(4,1)}, u32[]{:S(2)}) copy-start(pred[1280]{0:T(1024)(128)(4,1)} %get-tuple-element.9) | copy-start | bytes 3844
  162.2 25.2 %copy-start.24 = (s32[2048]{0:T(1024)S(1)}, s32[2048]{0:T(1024)}, u32[]{:S(2)}) copy-start(s32[2048]{0:T(1024)} %pad_clamp_fusion.2) | copy-start | bytes 24580
  187.5 120.9 %copy-start.26 = (s32[2048]{0:T(1024)S(1)}, s32[2048]{0:T(1024)}, u32[]{:S(2)}) copy-start(s32[2048]{0:T(1024)} %copy-done.25) | copy-start | bytes 24580
  368.0 38.3 %collective-permute-start = (bf16[80,128,64]{1,2,0:T(8,128)(2,1)S(1)}, bf16[80,128,64]{1,2,0:T(8,128)(2,1)S(1)}, u32[]{:S(2)}, u32[]{:S(2)}) collective-permute-start(bf16[80,128,64]{1,2,0:T(8,128)(2,1)S(1)} %get-tuple-element.60), channel_id=1, source_target_pairs={{0,1},{1,2},{2,3},{4,5},{5,6},{6,7},{8,9},{9,10},{10,11},{12,13},{... | collective-permute-start | bytes 3932168 | tf_op jit(solution)/shard_map/ppermute | solution.py:16
  407.8 8.2 %copy-start.4 = (f32[80,256]{1,0:T(8,128)S(1)}, f32[80,256]{1,0:T(8,128)}, u32[]{:S(2)}) copy-start(f32[80,256]{1,0:T(8,128)} %copy-done.3) | copy-start | bytes 245764
  407.8 8.2 %copy-start.18 = (f32[256,256]{1,0:T(8,128)S(1)}, f32[256,256]{1,0:T(8,128)}, u32[]{:S(2)}) copy-start(f32[256,256]{1,0:T(8,128)} %get-tuple-element.25) | copy-start | bytes 786436
  407.8 8.2 %copy-start.21 = (f32[80,256]{1,0:T(8,128)S(1)}, f32[80,256]{1,0:T(8,128)}, u32[]{:S(2)}) copy-start(f32[80,256]{1,0:T(8,128)} %copy.213) | copy-start | bytes 245764
  407.8 8.2 %copy-start.27 = (pred[256,256]{1,0:T(8,128)(4,1)S(1)}, pred[256,256]{1,0:T(8,128)(4,1)}, u32[]{:S(2)}) copy-start(pred[256,256]{1,0:T(8,128)(4,1)} %fusion.96) | copy-start | bytes 196612
  407.8 32.3 %collective-permute-start.1 = (bf16[80,128,64]{1,2,0:T(8,128)(2,1)}, bf16[80,128,64]{1,2,0:T(8,128)(2,1)S(1)}, u32[]{:S(2)}, u32[]{:S(2)}) collective-permute-start(bf16[80,128,64]{1,2,0:T(8,128)(2,1)} %add_convert_fusion.1), channel_id=1, source_target_pairs={{0,1},{1,2},{2,3},{4,5},{5,6},{6,7},{8,9},{9,10},{10,11},{12,13},{... | collective-permute-start | bytes 3932168 | tf_op jit(solution)/shard_map/ppermute | solution.py:16
  411.5 32.9 %slice-start = ((s8[5242880]{0:T(1024)(128)(4,1)}), s8[1048576]{0:T(1024)(128)(4,1)S(1)}, s32[]{:S(2)}) async-start(s8[5242880]{0:T(1024)(128)(4,1)} %bitcast.239), calls=%async_computation.5 | async-start | bytes 2097152
  416.0 28.5 %slice-start.1 = ((s8[5242880]{0:T(1024)(128)(4,1)}), s8[4194304]{0:T(1024)(128)(4,1)S(1)}, s32[]{:S(2)}) async-start(s8[5242880]{0:T(1024)(128)(4,1)} %bitcast.239), calls=%async_computation.6 | async-start | bytes 8388608
  423.1 21.4 %copy-start.15 = (f32[80,256]{1,0:T(8,128)S(1)}, f32[80,256]{1,0:T(8,128)}, u32[]{:S(2)}) copy-start(f32[80,256]{1,0:T(8,128)} %copy.203) | copy-start | bytes 245764
  440.5 9.0 %copy-start.16 = (f32[80,256]{1,0:T(8,128)S(1)}, f32[80,256]{1,0:T(8,128)}, u32[]{:S(2)}) copy-start(f32[80,256]{1,0:T(8,128)} %copy.210) | copy-start | bytes 245764
  440.6 31.1 %collective-permute-start.2 = (bf16[80,128,64]{1,2,0:T(8,128)(2,1)S(1)}, bf16[80,128,64]{1,2,0:T(8,128)(2,1)S(1)}, u32[]{:S(2)}, u32[]{:S(2)}) collective-permute-start(bf16[80,128,64]{1,2,0:T(8,128)(2,1)S(1)} %add_convert_fusion), channel_id=1, source_target_pairs={{0,1},{1,2},{2,3},{4,5},{5,6},{6,7},{8,9},{9,10},{10,11},{12,13},{... | collective-permute-start | bytes 3932168 | tf_op jit(solution)/shard_map/ppermute | solution.py:16
  444.5 12.5 %slice-start.2 = ((s8[5242880]{0:T(1024)(128)(4,1)}), s8[4194304]{0:T(1024)(128)(4,1)S(1)}, s32[]{:S(2)}) async-start(s8[5242880]{0:T(1024)(128)(4,1)} %bitcast.241), calls=%async_computation.7 | async-start | bytes 8388608
  486.9 17.7 %copy-start.1 = (bf16[1280,128]{1,0:T(8,128)(2,1)S(1)}, bf16[1280,128]{1,0:T(8,128)(2,1)}, u32[]{:S(2)}) copy-start(bf16[1280,128]{1,0:T(8,128)(2,1)} %param.13) | copy-start | bytes 983044
  (25 other events, 146.5 us)
where the time goes:
time: 515 us; the launch traced here: 505 us
  waiting for transfers between devices  144 us (28%)
  local copies, waits for them, and re-layouts  142 us (28%)
  matrix products  83.5 us (16%)
  other arithmetic  82.6 us (16%)
  starting transfers between devices  48.1 us (9%)
  between operations  5.3 us (1%)
    all_to_all x1, waiting for transfers between devices, on_device(): lax.all_to_all(jnp.take(token_rows, asked_rows, axis=0), 'dp', split_axis...  114 us
    gather x5, local copies, waits for them, and re-layouts, arrange(): return jnp.take(flat, pick_index, axis=0)  56.9 us
    another operation x32, other arithmetic  37.9 us
    dot_general x5, matrix products, span_pass(): jnp.einsum('hts,hsp->htp', weights, values_heads, preferred_element_type=...  33.9 us
    gather x1, local copies, waits for them, and re-layouts, on_device(): jnp.take(token_rows, asked_rows, axis=0)  33.8 us
    dot_general x5, matrix products, span_pass(): jnp.einsum('tn,hnp->htp', query_span.astype(jnp.float32), carried, precis...  29.5 us
    ppermute x3, waiting for transfers between devices, shifted(): return lax.ppermute(block, axis, route)  26.5 us
    another operation x1, local copies, waits for them, and re-layouts, on_device(): return layer_result_rows[None]  17.6 us
  transfers between devices with their start and end apart: 8, of which 4 were waited for; matrix products, arithmetic and copies ran while one was open for 39% of the time, Pallas kernels for 0%

commit v1 on v0

v1 whole, which is shorter than its diff:
```python
import functools
import math

import jax
import jax.numpy as jnp
from jax import lax
from jax.experimental import pallas as pl
from jax.experimental.pallas import tpu as pltpu
from jax.sharding import PartitionSpec as P

SPAN = 256
SEG = 8
LANES = 128
AUX = 3 * LANES
GROUP = 16
LOG2E = math.log2(math.e)
CEILING = 64.0

f32 = jnp.float32
bf16 = jnp.bfloat16


def params(mib, *semantics):
    return pltpu.CompilerParams(vmem_limit_bytes=mib * 2**20, dimension_semantics=semantics or None)


def estimate(flops, moved, exps=0):
    return pl.CostEstimate(flops=int(flops), bytes_accessed=int(moved), transcendentals=int(exps))


def pick_runs(ids, source, first, width, extra=None):
    count = ids.shape[0]
    more = 0 if extra is None else extra.shape[2]
    sources = (source,) if extra is None else (source, extra)

    def kernel(ids_ref, *refs):
        out_ref, sem = refs[-2:]

        @pl.loop(0, count)
        def _(i):
            run = ids_ref[i]
            pltpu.make_async_copy(
                refs[0].at[run, :, pl.ds(first, width)], out_ref.at[i, :, pl.ds(0, width)], sem
            ).start()
            if more:
                pltpu.make_async_copy(
                    refs[1].at[run], out_ref.at[i, :, pl.ds(width, more)], sem
                ).start()

        pltpu.make_async_copy(out_ref, out_ref, sem).wait()

    total = width + more
    return pl.pallas_call(
        kernel,
        out_shape=jax.ShapeDtypeStruct((count, SEG, total), source.dtype),
        grid_spec=pltpu.PrefetchScalarGridSpec(
            num_scalar_prefetch=1,
            grid=(1,),
            in_specs=[pl.BlockSpec(memory_space=pl.ANY)] * len(sources),
            out_specs=pl.BlockSpec(memory_space=pl.ANY),
            scratch_shapes=[pltpu.SemaphoreType.DMA],
        ),
        cost_estimate=estimate(0, 4 * count * SEG * total),
    )(ids, *sources)


def side_rows(key_rows, query_rows, step_rows):
    tokens, heads = step_rows.shape

    def kernel(k_ref, q_ref, st_ref, out_ref):
        out_ref[:, 0:LANES] = k_ref[...]
        out_ref[:, LANES : 2 * LANES] = q_ref[...]
        steps = st_ref[...].astype(f32)
        steps = jnp.concatenate([steps, jnp.zeros((LANES - heads, tokens), f32)], axis=0)
        out_ref[:, 2 * LANES : AUX] = jnp.transpose(steps).astype(bf16)

    return pl.pallas_call(
        kernel,
        out_shape=jax.ShapeDtypeStruct((tokens, AUX), bf16),
        compiler_params=params(32),
        cost_estimate=estimate(0, 4 * tokens * AUX),
    )(key_rows, query_rows, step_rows.T)


def prepare(packed, columns, decay_row, scalars):
    tokens = packed.shape[0]
    spans = tokens // SPAN
    starts = scalars.shape[0] - 1

    def kernel(
        sc_ref, k_ref, q_ref, st_ref, dec_ref,
        cum_ref, rt_ref, score_ref, kt_ref, endw_ref, entry_ref, entd_ref, ret_ref, thru_ref, pref,
    ):
        j = pl.program_id(0)

        @pl.when(j == 0)
        def _():
            pref[...] = jnp.ones_like(pref)

        raw = st_ref[...].astype(f32)
        step = jnp.maximum(raw, 0.0) + jnp.log1p(jnp.exp(-jnp.abs(raw)))
        decay = step * (jnp.exp(dec_ref[...]) * (-LOG2E))
        row = lax.broadcasted_iota(jnp.int32, (SPAN, SPAN), 0)
        col = lax.broadcasted_iota(jnp.int32, (SPAN, SPAN), 1)
        tri = (col <= row).astype(f32)
        cum = jnp.dot(tri, decay, precision=lax.Precision.HIGHEST, preferred_element_type=f32)
        begin = sc_ref[starts] + j * SPAN
        doc_row = jnp.zeros((SPAN, SPAN), jnp.int32)
        doc_col = jnp.zeros((SPAN, SPAN), jnp.int32)
        doc_tok = jnp.zeros((SPAN, LANES), jnp.int32)
        token = lax.broadcasted_iota(jnp.int32, (SPAN, LANES), 0)
        doc_end = jnp.int32(0)
        for d in range(starts):
            at = sc_ref[d] - begin
            at = jnp.where(at < 0, SPAN, at)
            doc_row += (at <= row).astype(jnp.int32)
            doc_col += (at <= col).astype(jnp.int32)
            doc_tok += (at <= token).astype(jnp.int32)
            doc_end += (at < SPAN).astype(jnp.int32)
        linked = (doc_row == doc_col) & (col <= row)
        scores = lax.dot_general(
            q_ref[...], k_ref[...], (((1,), (1,)), ((), ())), preferred_element_type=f32
        )
        score_ref[0] = jnp.where(linked, scores, 0.0)
        last = cum[SPAN - 1 : SPAN, :]
        cum_ref[...] = cum
        rt_ref[0] = jnp.transpose(cum - jnp.log(step) * LOG2E)
        kt_ref[0] = jnp.transpose(k_ref[...].astype(f32)).astype(bf16)
        endw_ref[...] = jnp.where(doc_tok == doc_end, jnp.exp2(last - cum), 0.0) * step
        entry = jnp.where(doc_tok == 0, jnp.exp2(cum), 0.0)
        entry_ref[...] = entry
        entd_ref[...] = entry * pref[0:1, :]
        kept = jnp.where(doc_end == 0, jnp.exp2(last), 0.0)
        kept = jnp.broadcast_to(kept, (8, LANES))
        ret_ref[0] = kept
        pref[...] = pref[...] * kept
        thru_ref[...] = pref[...]

    block = columns // LANES
    span_rows = pl.BlockSpec((SPAN, LANES), lambda j, s: (j, 0))
    rows = jax.ShapeDtypeStruct((tokens, LANES), f32)
    return pl.pallas_call(
        kernel,
        out_shape=(
            rows,
            jax.ShapeDtypeStruct((spans, LANES, SPAN), f32),
            jax.ShapeDtypeStruct((spans, SPAN, SPAN), f32),
            jax.ShapeDtypeStruct((spans, LANES, SPAN), bf16),
            rows,
            rows,
            rows,
            jax.ShapeDtypeStruct((spans, 8, LANES), f32),
            jax.ShapeDtypeStruct((8, LANES), f32),
        ),
        grid_spec=pltpu.PrefetchScalarGridSpec(
            num_scalar_prefetch=1,
            grid=(spans,),
            in_specs=[
                pl.BlockSpec((SPAN, LANES), lambda j, s: (j, block)),
                pl.BlockSpec((SPAN, LANES), lambda j, s: (j, block + 1)),
                pl.BlockSpec((SPAN, LANES), lambda j, s: (j, block + 2)),
                pl.BlockSpec((1, LANES), lambda j, s: (0, 0)),
            ],
            out_specs=[
                span_rows,
                pl.BlockSpec((1, LANES, SPAN), lambda j, s: (j, 0, 0)),
                pl.BlockSpec((1, SPAN, SPAN), lambda j, s: (j, 0, 0)),
                pl.BlockSpec((1, LANES, SPAN), lambda j, s: (j, 0, 0)),
                span_rows,
                span_rows,
                span_rows,
                pl.BlockSpec((1, 8, LANES), lambda j, s: (j, 0, 0)),
                pl.BlockSpec((8, LANES), lambda j, s: (0, 0)),
            ],
            scratch_shapes=[pltpu.VMEM((8, LANES), f32)],
        ),
        compiler_params=params(32, "arbitrary"),
        cost_estimate=estimate(spans * 2 * SPAN * SPAN * LANES * 7, 6 * 2**20),
    )(scalars, packed, packed, packed, decay_row)


def roll_heads(table, first_head):
    return pltpu.roll(table, lax.rem(LANES - first_head, LANES), 1)


def spreader(width, head_width):
    lane = lax.broadcasted_iota(jnp.int32, (2 * LANES, width), 1) // head_width
    source = lax.rem(lax.broadcasted_iota(jnp.int32, (2 * LANES, width), 0), LANES)
    return (lane == source).astype(bf16)


def halves(x):
    high = x.astype(bf16)
    return high, (x - high.astype(f32)).astype(bf16)


def spread(table, matrix):
    return jnp.dot(jnp.concatenate(halves(table), axis=1), matrix, preferred_element_type=f32)


def states(packed, width, first_head, head_width, kt, endw, ret, thru):
    tokens = packed.shape[0]
    spans = tokens // SPAN
    step_width = GROUP * head_width
    groups = width // step_width

    def kernel(v_ref, kt_ref, endw_ref, ret_ref, thru_ref, final_ref, enter_ref, state, matrix):
        g, j = pl.program_id(0), pl.program_id(1)
        head = first_head + g * GROUP

        @pl.when((g == 0) & (j == 0))
        def _():
            matrix[...] = spreader(step_width, head_width)

        @pl.when(j == 0)
        def _():
            state[...] = jnp.zeros_like(state)

        repeat = matrix[...]
        weight = spread(roll_heads(endw_ref[...], head), repeat)
        scaled = (v_ref[...].astype(f32) * weight).astype(bf16)
        added = jnp.dot(kt_ref[0], scaled, preferred_element_type=f32)
        kept = spread(roll_heads(ret_ref[0], head), repeat)[0:1, :]
        old = state[...]
        high, low = halves(old)
        enter_ref[0, 0:LANES, :] = high
        enter_ref[0, LANES : 2 * LANES, :] = low
        new = kept * old + added
        state[...] = new
        final_ref[0:LANES, :] = new.astype(bf16)
        through = spread(roll_heads(thru_ref[...], head), repeat)
        high, low = halves(through)
        final_ref[LANES : LANES + 16, :] = jnp.concatenate([high, low], axis=0)

    return pl.pallas_call(
        kernel,
        out_shape=(
            jax.ShapeDtypeStruct((LANES + 16, width), bf16),
            jax.ShapeDtypeStruct((spans, 2 * LANES, width), bf16),
        ),
        grid=(groups, spans),
        in_specs=[
            pl.BlockSpec((SPAN, step_width), lambda g, j: (j, g)),
            pl.BlockSpec((1, LANES, SPAN), lambda g, j: (j, 0, 0)),
            pl.BlockSpec((SPAN, LANES), lambda g, j: (j, 0)),
            pl.BlockSpec((1, 8, LANES), lambda g, j: (j, 0, 0)),
            pl.BlockSpec((8, LANES), lambda g, j: (0, 0)),
        ],
        out_specs=[
            pl.BlockSpec((LANES + 16, step_width), lambda g, j: (0, g)),
            pl.BlockSpec((1, 2 * LANES, step_width), lambda g, j: (j, 0, g)),
        ],
        scratch_shapes=[
            pltpu.VMEM((LANES, step_width), f32),
            pltpu.VMEM((2 * LANES, step_width), bf16),
        ],
        compiler_params=params(32, "arbitrary", "arbitrary"),
        cost_estimate=estimate(2 * tokens * width * 2.5 * LANES, 5 * tokens * width),
    )(packed, kt, endw, ret, thru)


def local_results(
    packed, width, first_head, head_width, whole_width, query_at, aux, cum, rt, scores, entry, enter, skip_row, result
):
    tokens = packed.shape[0]
    spans = tokens // SPAN
    step_width = GROUP * head_width
    groups = width // step_width
    first_group = first_head // GROUP
    half = SPAN // 2

    def kernel(v_ref, q_ref, cum_ref, rt_ref, score_ref, entry_ref, enter_ref, skip_ref, *rest):
        out_ref, matrix = rest[-2:]
        j, g = pl.program_id(0), pl.program_id(1)
        head = first_head + g * GROUP

        @pl.when((g == 0) & (j == 0))
        def _():
            matrix[...] = spreader(step_width, head_width)

        query = q_ref[...]
        base = jnp.dot(
            jnp.concatenate([query, query], axis=1), enter_ref[0], preferred_element_type=f32
        )
        base = base * spread(roll_heads(entry_ref[...], head), matrix[...])
        base = base + skip_ref[...] * v_ref[...].astype(f32)
        total = roll_heads(cum_ref[...], head)
        lane = lax.broadcasted_iota(jnp.int32, (half, 2 * head_width), 1)
        first_row = pl.multiple_of(head, 8)
        for pair in range(GROUP // 2):
            at = pair * 2 * head_width
            values = v_ref[:, at : at + 2 * head_width]
            for part in range(2):
                reach = (part + 1) * half
                rows = slice(part * half, reach)
                outs = []
                for h in (2 * pair, 2 * pair + 1):
                    from_row = rt_ref[0, pl.ds(first_row + 8 * (h // 8), 8), 0:reach][h % 8 : h % 8 + 1, :]
                    gap = total[rows, h : h + 1] - from_row
                    weights = score_ref[0, rows, 0:reach] * jnp.exp2(jnp.minimum(gap, CEILING))
                    outs.append(
                        jnp.dot(weights.astype(bf16), values[0:reach], preferred_element_type=f32)
                    )
                within = jnp.where(lane < head_width, outs[0], outs[1])
                out_ref[rows, at : at + 2 * head_width] = (
                    within + base[rows, at : at + 2 * head_width]
                ).astype(out_ref.dtype)

    rows = pl.BlockSpec((SPAN, LANES), lambda j, g: (j, 0))
    earlier = [] if result is None else [result]
    return pl.pallas_call(
        kernel,
        out_shape=jax.ShapeDtypeStruct((tokens, whole_width), bf16),
        grid=(spans, groups),
        in_specs=[
            pl.BlockSpec((SPAN, step_width), lambda j, g: (j, g)),
            pl.BlockSpec((SPAN, LANES), lambda j, g: (j, query_at)),
            rows,
            pl.BlockSpec((1, LANES, SPAN), lambda j, g: (j, 0, 0)),
            pl.BlockSpec((1, SPAN, SPAN), lambda j, g: (j, 0, 0)),
            rows,
            pl.BlockSpec((1, 2 * LANES, step_width), lambda j, g: (j, 0, g)),
            pl.BlockSpec((1, step_width), lambda j, g: (0, first_group + g)),
        ]
        + [pl.BlockSpec(memory_space=pl.ANY)] * len(earlier),
        out_specs=pl.BlockSpec((SPAN, step_width), lambda j, g: (j, first_group + g)),
        scratch_shapes=[pltpu.VMEM((2 * LANES, step_width), bf16)],
        input_output_aliases={8: 0} if earlier else {},
        compiler_params=params(48, "arbitrary", "arbitrary"),
        cost_estimate=estimate(
            2 * tokens * width * 4 * SPAN, 6 * tokens * width, tokens * SPAN * width // head_width
        ),
    )(packed, aux, cum, rt, scores, entry, enter, skip_row, *earlier)


def add_entering(result, width, first_head, head_width, query_at, aux, entd, arrived):
    tokens = result.shape[0]
    spans = tokens // SPAN
    step_width = GROUP * head_width
    groups = width // step_width
    first_group = first_head // GROUP

    def kernel(q_ref, entd_ref, *rest):
        froms = rest[: len(arrived)]
        in_ref, out_ref, matrix, state = rest[len(arrived) :]
        g, j = pl.program_id(0), pl.program_id(1)
        head = first_head + g * GROUP

        @pl.when((g == 0) & (j == 0))
        def _():
            matrix[...] = spreader(step_width, head_width)

        @pl.when(j == 0)
        def _():
            incoming = froms[-1][0:LANES, :].astype(f32)
            for ref in reversed(froms[:-1]):
                factor = ref[LANES : LANES + 16, :].astype(f32)
                incoming = ref[0:LANES, :].astype(f32) + (factor[0:1, :] + factor[8:9, :]) * incoming
            state[...] = incoming.astype(bf16)

        part = jnp.dot(q_ref[...], state[...], preferred_element_type=f32)
        part = part * spread(roll_heads(entd_ref[...], head), matrix[...])
        out_ref[...] = (in_ref[...].astype(f32) + part).astype(out_ref.dtype)

    place = pl.BlockSpec((SPAN, step_width), lambda g, j: (j, first_group + g))
    return pl.pallas_call(
        kernel,
        out_shape=jax.ShapeDtypeStruct(result.shape, result.dtype),
        grid=(groups, spans),
        in_specs=[
            pl.BlockSpec((SPAN, LANES), lambda g, j: (j, query_at)),
            pl.BlockSpec((SPAN, LANES), lambda g, j: (j, 0)),
        ]
        + [pl.BlockSpec((LANES + 16, step_width), lambda g, j: (0, g))] * len(arrived)
        + [place],
        out_specs=place,
        scratch_shapes=[
            pltpu.VMEM((2 * LANES, step_width), bf16),
            pltpu.VMEM((LANES, step_width), bf16),
        ],
        input_output_aliases={2 + len(arrived): 0},
        compiler_params=params(32, "arbitrary", "arbitrary"),
        cost_estimate=estimate(2 * tokens * width * 3 * LANES, 4 * tokens * width),
    )(aux, entd, *arrived, result)


def shifted(block, distance):
    count = lax.axis_size("seq")
    return lax.ppermute(block, "seq", [(i, i + distance) for i in range(count - distance)])


def on_device(
    token_rows, key_rows, query_rows, step_rows, decay_log, skip_gain, source_rows, document_starts
):
    tokens, whole_width = token_rows.shape
    peers = lax.axis_size("dp")
    shards = lax.axis_size("seq")
    heads = decay_log.shape[0]
    head_width = whole_width // heads
    runs = tokens // SEG
    capacity = runs // peers + 1

    first_rows = source_rows[0].reshape(runs, SEG)[:, 0]
    peer = first_rows // (tokens * shards)
    run = (first_rows % tokens) // SEG
    order = jnp.arange(runs)
    earlier = (peer[:, None] == peer[None, :]) & (order[None, :] < order[:, None])
    slot = peer * capacity + jnp.sum(earlier.astype(jnp.int32), axis=1)
    asked = jnp.sum(
        jnp.where(slot[None, :] == jnp.arange(peers * capacity)[:, None], run[None, :], 0), axis=1
    )
    wanted = lax.all_to_all(
        asked.reshape(peers, capacity), "dp", split_axis=0, concat_axis=0, tiled=True
    ).reshape(peers * capacity)

    aux_rows = side_rows(key_rows, query_rows, step_rows).reshape(runs, SEG, AUX)
    token_runs = token_rows.reshape(runs, SEG, whole_width)

    def exchange(block):
        rows = block.reshape(peers, capacity * SEG, block.shape[2])
        rows = lax.all_to_all(rows, "dp", split_axis=0, concat_axis=0, tiled=True)
        return rows.reshape(block.shape)

    last_width = GROUP * head_width
    main_width = whole_width - last_width
    main_heads = heads - GROUP
    sent_main = pick_runs(wanted, token_runs, 0, main_width, aux_rows)
    got_main = exchange(sent_main)
    wanted, sent_main = lax.optimization_barrier((wanted, sent_main))
    sent_last = pick_runs(wanted, token_runs, main_width, last_width)
    got_main, sent_last = lax.optimization_barrier((got_main, sent_last))
    got_last = exchange(sent_last)

    packed_main = pick_runs(slot, got_main, 0, main_width + AUX).reshape(tokens, main_width + AUX)
    scalars = jnp.concatenate(
        [document_starts[0], (lax.axis_index("seq") * tokens).astype(jnp.int32)[None]]
    )
    decay_row = jnp.pad(decay_log, (0, LANES - heads))[None, :]
    skip_row = jnp.repeat(skip_gain, head_width)[None, :]
    cum, rt, scores, kt, endw, entry, entd, ret, thru = prepare(
        packed_main, main_width, decay_row, scalars
    )
    query_at = main_width // LANES + 1
    distances = range(1, shards)

    final_main, enter_main = states(packed_main, main_width, 0, head_width, kt, endw, ret, thru)
    arrived_main = [shifted(final_main, d) for d in distances]
    packed_last = pick_runs(slot, got_last, 0, last_width).reshape(tokens, last_width)
    final_last, enter_last = states(
        packed_last, last_width, main_heads, head_width, kt, endw, ret, thru
    )
    arrived_last = [shifted(final_last, d) for d in distances]

    result = local_results(
        packed_main, main_width, 0, head_width, whole_width, query_at, packed_main, cum, rt, scores,
        entry, enter_main, skip_row, None,
    )
    result = local_results(
        packed_last, last_width, main_heads, head_width, whole_width, query_at, packed_main, cum, rt,
        scores, entry, enter_last, skip_row, result,
    )
    result = add_entering(
        result, main_width, 0, head_width, query_at, packed_main, entd, arrived_main
    )
    result = add_entering(
        result, last_width, main_heads, head_width, query_at, packed_main, entd, arrived_last
    )
    return result[None]


def solution(mesh):
    in_specs = (
        P(("dp", "seq"), None),
        P(("dp", "seq"), None),
        P(("dp", "seq"), None),
        P(("dp", "seq"), None),
        P(),
        P(),
        P("dp", "seq"),
        P("dp", None),
    )
    out_specs = P("dp", "seq", None)
    return jax.shard_map(
        on_device, mesh=mesh, in_specs=in_specs, out_specs=out_specs, check_vma=False
    )
```

time: 515 us -> 1190 us (2.31)
  the two profiles are of different devices: /device:TPU:44 before, /device:TPU:0 now
where the time goes in v1:
time: 1190 us; the launch traced here: 1180 us
  Pallas kernels  1040 us (87%)
  waiting for transfers between devices  81.3 us (7%)
  starting transfers between devices  33.9 us (3%)
  local copies, waits for them, and re-layouts  26.6 us (2%)
    pallas_call x4, Pallas kernels, pick_runs(): pl.pallas_call(kernel, out_shape=jax.ShapeDtypeStruct((count, SEG, total)...  946 us
    all_to_all x2, waiting for transfers between devices, exchange(): rows = lax.all_to_all(rows, 'dp', split_axis=0, concat_axis=0, tiled=True)  78 us
    pallas_call x2, Pallas kernels, local_results(): pl.pallas_call(kernel, out_shape=jax.ShapeDtypeStruct((tokens, whole_widt...  39.4 us
    pallas_call x2, Pallas kernels, add_entering(): pl.pallas_call(kernel, out_shape=jax.ShapeDtypeStruct(result.shape, resul...  25.5 us
    unnamed x40, local copies, waits for them, and re-layouts  24.4 us
    pallas_call x2, Pallas kernels, states(): pl.pallas_call(kernel, out_shape=(jax.ShapeDtypeStruct((LANES + 16, width...  24.3 us
  transfers between devices with their start and end apart: 9, of which 2 were waited for; matrix products, arithmetic and copies ran while one was open for 0% of the time, Pallas kernels for 52%

profile of v1, /device:TPU:0, one launch (start us, length us, event | category | flops | bytes accessed | tf_op | source)
XLA Modules:
  0.0 1183.8 jit_solution(3686892523303710103)
XLA Ops:
  2.2 7.4 all-to-all-start
  10.6 1.0 copy-done.14
  13.7 3.3 all-to-all-done
  18.7 418.7 %shard_map.83 = bf16[192,8,4480]{2,1,0:T(8,128)(2,1)} custom-call(s32[192]{0:T(256)} %reshape.98.ids_ref, bf16[160,8,5120]{2,1,0:T(8,128)(2,1)} %bitcast.29, bf16[160,8,384]{2,1,0:T(8,128)(2,1)} %bitcast.26), custom_call_target="tpu_custom_call" | custom-call | bytes 27525120 | tf_op jit(solution)/shard_map/pallas_call | solution.py:53
  437.5 5.1 all-to-all-start.1
  442.6 97.2 %shard_map.84 = bf16[192,8,1024]{2,1,0:T(8,128)(2,1)} custom-call(s32[192]{0:T(256)} %reshape.98.ids_ref, bf16[160,8,5120]{2,1,0:T(8,128)(2,1)} %bitcast.30), custom_call_target="tpu_custom_call" | custom-call | bytes 6291456 | tf_op jit(solution)/shard_map/pallas_call | solution.py:53
  539.9 78.0 %all-to-all-done.1 = bf16[32,48,4480]{2,1,0:T(8,128)(2,1)} async-done(((bf16[32,48,4480]{2,1,0:T(8,128)(2,1)}), bf16[32,48,4480]{2,1,0:T(8,128)(2,1)}, u32[]{:S(2)}, u32[]{:S(2)}) %all-to-all-start.1) | async-done | bytes 13762592 | tf_op jit(solution)/shard_map/all_to_all | solution.py:421
  617.9 4.8 all-to-all-start.2
  623.0 349.2 %shard_map.85 = bf16[160,8,4480]{2,1,0:T(8,128)(2,1)} custom-call(s32[160]{0:T(256)} %copy-done.16, bf16[192,8,4480]{2,1,0:T(8,128)(2,1)} %bitcast.5.refs_0_), custom_call_target="tpu_custom_call" | custom-call | bytes 22937600 | tf_op jit(solution)/shard_map/pallas_call | solution.py:53
  972.3 4.2 copy-done
  976.5 3.8 shard_map.86
  980.3 20.7 %shard_map.89 = (bf16[144,4096]{1,0:T(8,128)(2,1)}, bf16[5,256,4096]{2,1,0:T(8,128)(2,1)S(1)}) custom-call(bf16[1280,4480]{1,0:T(8,128)(2,1)} %bitcast.15, bf16[5,128,256]{2,1,0:T(8,128)(2,1)S(1)} %get-tuple-element.25.kt_ref, f32[1280,128]{1,0:T(8,128)S(1)} %get-tuple-element.26.endw_ref, f32[5,8,128]{2,1,0:T(8,128)S(1)} %get-tuple-element.27.ret_ref, ...), custom_call_target="tpu_custom_call" | custom-call | flops 3355443200 | bytes 26214400 | tf_op jit(solution)/shard_map/pallas_call | solution.py:235
  1001.1 4.0 copy-done.4
  1005.0 4.9 collective-permute-start.3
  1009.9 5.5 collective-permute-start.4
  1015.4 2.3 collective-permute-start.5
  1017.7 30.6 %shard_map.90.rest_0_ = bf16[1280,5120]{1,0:T(8,128)(2,1)} custom-call(bf16[1280,4480]{1,0:T(8,128)(2,1)} %bitcast.16, bf16[1280,4480]{1,0:T(8,128)(2,1)} %bitcast.17, f32[1280,128]{1,0:T(8,128)S(1)} %get-tuple-element.31.cum_ref, f32[5,128,256]{2,1,0:T(8,128)S(1)} %get-tuple-element.32.rt_ref, f32[5,256,256]{2,1,0:T(8,128)S(1)} %get-tuple-element.33.score_ref, ...), custom_call_target="tpu_custom_call" | custom-call | flops 10737418240 | bytes 31457280 | tf_op jit(solution)/shard_map/pallas_call | solution.py:311
  1048.4 81.2 %shard_map.87 = bf16[160,8,1024]{2,1,0:T(8,128)(2,1)} custom-call(s32[160]{0:T(256)} %copy-done.16, bf16[192,8,1024]{2,1,0:T(8,128)(2,1)} %bitcast.11.refs_0_), custom_call_target="tpu_custom_call" | custom-call | bytes 5242880 | tf_op jit(solution)/shard_map/pallas_call | solution.py:53
  1129.6 1.7 copy-done.2
  1131.3 1.0 copy-done.12
  1132.3 3.6 shard_map.88
  1136.0 1.5 copy-done.6
  1137.5 1.3 collective-permute-start
  1138.8 1.3 collective-permute-start.1
  1140.1 1.7 copy-done.3
  1141.8 1.1 copy-done.8
  1142.9 1.1 copy-done.10
  1144.0 8.8 shard_map.91.rest_3_
  1152.8 1.3 collective-permute-start.2
  1154.1 4.2 copy-done.1
  1158.4 19.6 %shard_map.92.rest_3_ = bf16[1280,5120]{1,0:T(8,128)(2,1)} custom-call(bf16[1280,4480]{1,0:T(8,128)(2,1)S(1)} %bitcast.22, f32[1280,128]{1,0:T(8,128)S(1)} %get-tuple-element.23.entd_ref, bf16[144,4096]{1,0:T(8,128)(2,1)} %collective-permute-done.3.rest_0_, bf16[144,4096]{1,0:T(8,128)(2,1)} %collective-permute-done.4.rest_1_, ...), custom_call_target="tpu_custom_call", output_to_operand_aliasing={{}: (5, {})} | custom-call | flops 4026531840 | bytes 20971520 | tf_op jit(solution)/shard_map/pallas_call | solution.py:366
  1178.0 5.9 shard_map.93
  (54 shorter events, 7.3 us)
Async XLA Ops:
  1.4 436.1 %copy-start.16 = (s32[160]{0:T(256)}, s32[160]{0:T(256)S(1)}, u32[]{:S(2)}) copy-start(s32[160]{0:T(256)S(1)} %multiply_add_fusion.ids_ref) | copy-start | bytes 1924
  2.2 14.8 %all-to-all-start = ((s32[32,1,6]{2,1,0:T(1,128)}), s32[32,1,6]{2,1,0:T(1,128)S(1)}, u32[]{:S(2)}, u32[]{:S(2)}) async-start(s32[32,1,6]{2,1,0:T(1,128)} %bitcast), calls=%async_computation | async-start | bytes 32768 | tf_op jit(solution)/shard_map/all_to_all | solution.py:412
  9.6 1.0 copy-start.13
  10.6 1.0 copy-start.14
  11.6 0.9 copy-start.15
  12.7 0.9 copy-start.5
  437.5 180.4 %all-to-all-start.1 = ((bf16[32,48,4480]{2,1,0:T(8,128)(2,1)}), bf16[32,48,4480]{2,1,0:T(8,128)(2,1)}, u32[]{:S(2)}, u32[]{:S(2)}) async-start(bf16[32,48,4480]{2,1,0:T(8,128)(2,1)} %bitcast.28), calls=%async_computation.1 | async-start | bytes 27525120 | tf_op jit(solution)/shard_map/all_to_all | solution.py:421
  442.6 180.1 %copy-start.17 = (f32[80]{0:T(128)S(1)}, f32[80]{0:T(128)}, u32[]{:S(2)}) copy-start(f32[80]{0:T(128)} %param.13) | copy-start | bytes 964
  442.6 180.3 %copy-start.18 = (f32[80]{0:T(128)S(1)}, f32[80]{0:T(128)}, u32[]{:S(2)}) copy-start(f32[80]{0:T(128)} %param.12) | copy-start | bytes 964
  442.6 180.3 %copy-start.19 = (s32[1,6]{1,0:T(1,128)S(1)}, s32[1,6]{1,0:T(1,128)}, u32[]{:S(2)}) copy-start(s32[1,6]{1,0:T(1,128)} %param.15) | copy-start | bytes 76
  617.9 430.5 %all-to-all-start.2 = ((bf16[32,48,1024]{2,1,0:T(8,128)(2,1)}), bf16[32,48,1024]{2,1,0:T(8,128)(2,1)}, u32[]{:S(2)}, u32[]{:S(2)}) async-start(bf16[32,48,1024]{2,1,0:T(8,128)(2,1)} %bitcast.31), calls=%async_computation.2 | async-start | bytes 6291456 | tf_op jit(solution)/shard_map/all_to_all | solution.py:421
  972.3 4.3 copy-start
  980.3 20.7 %copy-start.11 = (bf16[5,128,256]{2,1,0:T(8,128)(2,1)}, bf16[5,128,256]{2,1,0:T(8,128)(2,1)S(1)}, u32[]{:S(2)}) copy-start(bf16[5,128,256]{2,1,0:T(8,128)(2,1)S(1)} %get-tuple-element.25.kt_ref) | copy-start | bytes 983044
  980.3 37.4 %copy-start.7 = (f32[5,128,256]{2,1,0:T(8,128)}, f32[5,128,256]{2,1,0:T(8,128)S(1)}, u32[]{:S(2)}) copy-start(f32[5,128,256]{2,1,0:T(8,128)S(1)} %get-tuple-element.32.rt_ref) | copy-start | bytes 1966084
  980.3 37.4 %copy-start.9 = (f32[1280,128]{1,0:T(8,128)}, f32[1280,128]{1,0:T(8,128)S(1)}, u32[]{:S(2)}) copy-start(f32[1280,128]{1,0:T(8,128)S(1)} %get-tuple-element.34.entry_ref) | copy-start | bytes 1966084
  1001.1 4.0 copy-start.4
  1005.0 147.7 %collective-permute-start.3 = (bf16[144,4096]{1,0:T(8,128)(2,1)}, bf16[144,4096]{1,0:T(8,128)(2,1)}, u32[]{:S(2)}, u32[]{:S(2)}) collective-permute-start(bf16[144,4096]{1,0:T(8,128)(2,1)} %get-tuple-element.30), channel_id=1, source_target_pairs={{0,1},{1,2},{2,3},{4,5},{5,6},{6,7},{8,9},{9,10},{10,11},{12,13},{... | collective-permute-start | bytes 3538952 | tf_op jit(solution)/shard_map/ppermute | solution.py:389
  1009.9 144.2 %collective-permute-start.4 = (bf16[144,4096]{1,0:T(8,128)(2,1)}, bf16[144,4096]{1,0:T(8,128)(2,1)}, u32[]{:S(2)}, u32[]{:S(2)}) collective-permute-start(bf16[144,4096]{1,0:T(8,128)(2,1)} %get-tuple-element.30), channel_id=1, source_target_pairs={{0,2},{1,3},{4,6},{5,7},{8,10},{9,11},{12,14},{13,15},{16,18},{17,... | collective-permute-start | bytes 3538952 | tf_op jit(solution)/shard_map/ppermute | solution.py:389
  1015.4 138.7 %collective-permute-start.5 = (bf16[144,4096]{1,0:T(8,128)(2,1)}, bf16[144,4096]{1,0:T(8,128)(2,1)}, u32[]{:S(2)}, u32[]{:S(2)}) collective-permute-start(bf16[144,4096]{1,0:T(8,128)(2,1)} %get-tuple-element.30), channel_id=1, source_target_pairs={{0,3},{4,7},{8,11},{12,15},{16,19},{20,23},{24,27},{28,31},{32,35}... | collective-permute-start | bytes 3538952 | tf_op jit(solution)/shard_map/ppermute | solution.py:389
  1129.6 1.7 copy-start.2
  1131.3 1.0 copy-start.12
  1136.0 1.5 copy-start.6
  1137.5 40.5 %collective-permute-start = (bf16[144,1024]{1,0:T(8,128)(2,1)S(1)}, bf16[144,1024]{1,0:T(8,128)(2,1)S(1)}, u32[]{:S(2)}, u32[]{:S(2)}) collective-permute-start(bf16[144,1024]{1,0:T(8,128)(2,1)S(1)} %get-tuple-element.29), channel_id=1, source_target_pairs={{0,1},{1,2},{2,3},{4,5},{5,6},{6,7},{8,9},{9,10},{10,11},{12,13},{... | collective-permute-start | bytes 884744 | tf_op jit(solution)/shard_map/ppermute | solution.py:389
  1138.8 39.2 %collective-permute-start.1 = (bf16[144,1024]{1,0:T(8,128)(2,1)S(1)}, bf16[144,1024]{1,0:T(8,128)(2,1)S(1)}, u32[]{:S(2)}, u32[]{:S(2)}) collective-permute-start(bf16[144,1024]{1,0:T(8,128)(2,1)S(1)} %get-tuple-element.29), channel_id=1, source_target_pairs={{0,2},{1,3},{4,6},{5,7},{8,10},{9,11},{12,14},{13,15},{16,18},{17,... | collective-permute-start | bytes 884744 | tf_op jit(solution)/shard_map/ppermute | solution.py:389
  1140.1 1.7 copy-start.3
  1141.8 1.1 copy-start.8
  1142.9 1.1 copy-start.10
  1152.8 25.2 %collective-permute-start.2 = (bf16[144,1024]{1,0:T(8,128)(2,1)S(1)}, bf16[144,1024]{1,0:T(8,128)(2,1)S(1)}, u32[]{:S(2)}, u32[]{:S(2)}) collective-permute-start(bf16[144,1024]{1,0:T(8,128)(2,1)S(1)} %get-tuple-element.29), channel_id=1, source_target_pairs={{0,3},{4,7},{8,11},{12,15},{16,19},{20,23},{24,27},{28,31},{32,35}... | collective-permute-start | bytes 884744 | tf_op jit(solution)/shard_map/ppermute | solution.py:389
  1154.1 4.3 copy-start.1

commit v2 on v1

--- a/solution.py
+++ b/solution.py
@@ -13,6 +13,8 @@
 LANES = 128
 AUX = 3 * LANES
 GROUP = 16
+PARTS = (32, 32, 16)
+CHUNK = 16
 LOG2E = math.log2(math.e)
 CEILING = 64.0
 
@@ -32,24 +34,40 @@
     count = ids.shape[0]
     more = 0 if extra is None else extra.shape[2]
     sources = (source,) if extra is None else (source, extra)
+    total = width + more
+    chunk = max(n for n in range(1, CHUNK + 1) if count % n == 0)
+    chunks = count // chunk
 
     def kernel(ids_ref, *refs):
-        out_ref, sem = refs[-2:]
-
-        @pl.loop(0, count)
-        def _(i):
-            run = ids_ref[i]
-            pltpu.make_async_copy(
-                refs[0].at[run, :, pl.ds(first, width)], out_ref.at[i, :, pl.ds(0, width)], sem
-            ).start()
-            if more:
+        out_ref, held, in_sems, out_sems = refs[-4:]
+
+        @pl.loop(0, chunks)
+        def _(c):
+            @pl.loop(0, chunk)
+            def _(i):
+                place = c * chunk + i
+                run = ids_ref[place]
                 pltpu.make_async_copy(
-                    refs[1].at[run], out_ref.at[i, :, pl.ds(width, more)], sem
+                    refs[0].at[run, :, pl.ds(first, width)],
+                    held.at[place, :, pl.ds(0, width)],
+                    in_sems.at[c],
                 ).start()
-
-        pltpu.make_async_copy(out_ref, out_ref, sem).wait()
-
-    total = width + more
+                if more:
+                    pltpu.make_async_copy(
+                        refs[1].at[run], held.at[place, :, pl.ds(width, more)], in_sems.at[c]
+                    ).start()
+
+        @pl.loop(0, chunks)
+        def _(c):
+            part = pl.ds(c * chunk, chunk)
+            pltpu.make_async_copy(held.at[part], held.at[part], in_sems.at[c]).wait()
+            pltpu.make_async_copy(held.at[part], out_ref.at[part], out_sems.at[c]).start()
+
+        @pl.loop(0, chunks)
+        def _(c):
+            part = pl.ds(c * chunk, chunk)
+            pltpu.make_async_copy(held.at[part], out_ref.at[part], out_sems.at[c]).wait()
+
     return pl.pallas_call(
         kernel,
         out_shape=jax.ShapeDtypeStruct((count, SEG, total), source.dtype),
@@ -58,8 +76,13 @@
             grid=(1,),
             in_specs=[pl.BlockSpec(memory_space=pl.ANY)] * len(sources),
             out_specs=pl.BlockSpec(memory_space=pl.ANY),
-            scratch_shapes=[pltpu.SemaphoreType.DMA],
+            scratch_shapes=[
+                pltpu.VMEM((count, SEG, total), source.dtype),
+                pltpu.SemaphoreType.DMA((chunks,)),
+                pltpu.SemaphoreType.DMA((chunks,)),
+            ],
         ),
+        compiler_params=params(56),
         cost_estimate=estimate(0, 4 * count * SEG * total),
     )(ids, *sources)
 
@@ -174,7 +197,7 @@
             ],
             scratch_shapes=[pltpu.VMEM((8, LANES), f32)],
         ),
-        compiler_params=params(32, "arbitrary"),
+        compiler_params=params(56, "arbitrary"),
         cost_estimate=estimate(spans * 2 * SPAN * SPAN * LANES * 7, 6 * 2**20),
     )(scalars, packed, packed, packed, decay_row)
 
@@ -254,7 +277,7 @@
             pltpu.VMEM((LANES, step_width), f32),
             pltpu.VMEM((2 * LANES, step_width), bf16),
         ],
-        compiler_params=params(32, "arbitrary", "arbitrary"),
+        compiler_params=params(56, "arbitrary", "arbitrary"),
         cost_estimate=estimate(2 * tokens * width * 2.5 * LANES, 5 * tokens * width),
     )(packed, kt, endw, ret, thru)
 
@@ -326,7 +349,7 @@
         out_specs=pl.BlockSpec((SPAN, step_width), lambda j, g: (j, first_group + g)),
         scratch_shapes=[pltpu.VMEM((2 * LANES, step_width), bf16)],
         input_output_aliases={8: 0} if earlier else {},
-        compiler_params=params(48, "arbitrary", "arbitrary"),
+        compiler_params=params(56, "arbitrary", "arbitrary"),
         cost_estimate=estimate(
             2 * tokens * width * 4 * SPAN, 6 * tokens * width, tokens * SPAN * width // head_width
         ),
@@ -379,7 +402,7 @@
             pltpu.VMEM((LANES, step_width), bf16),
         ],
         input_output_aliases={2 + len(arrived): 0},
-        compiler_params=params(32, "arbitrary", "arbitrary"),
+        compiler_params=params(56, "arbitrary", "arbitrary"),
         cost_estimate=estimate(2 * tokens * width * 3 * LANES, 4 * tokens * width),
     )(aux, entd, *arrived, result)
 
@@ -421,50 +444,61 @@
         rows = lax.all_to_all(rows, "dp", split_axis=0, concat_axis=0, tiled=True)
         return rows.reshape(block.shape)
 
-    last_width = GROUP * head_width
-    main_width = whole_width - last_width
-    main_heads = heads - GROUP
-    sent_main = pick_runs(wanted, token_runs, 0, main_width, aux_rows)
-    got_main = exchange(sent_main)
-    wanted, sent_main = lax.optimization_barrier((wanted, sent_main))
-    sent_last = pick_runs(wanted, token_runs, main_width, last_width)
-    got_main, sent_last = lax.optimization_barrier((got_main, sent_last))
-    got_last = exchange(sent_last)
-
-    packed_main = pick_runs(slot, got_main, 0, main_width + AUX).reshape(tokens, main_width + AUX)
+    widths = [n * head_width for n in PARTS]
+    firsts = [sum(PARTS[:i]) for i in range(len(PARTS))]
     scalars = jnp.concatenate(
         [document_starts[0], (lax.axis_index("seq") * tokens).astype(jnp.int32)[None]]
     )
     decay_row = jnp.pad(decay_log, (0, LANES - heads))[None, :]
     skip_row = jnp.repeat(skip_gain, head_width)[None, :]
-    cum, rt, scores, kt, endw, entry, entd, ret, thru = prepare(
-        packed_main, main_width, decay_row, scalars
-    )
-    query_at = main_width // LANES + 1
-    distances = range(1, shards)
-
-    final_main, enter_main = states(packed_main, main_width, 0, head_width, kt, endw, ret, thru)
-    arrived_main = [shifted(final_main, d) for d in distances]
-    packed_last = pick_runs(slot, got_last, 0, last_width).reshape(tokens, last_width)
-    final_last, enter_last = states(
-        packed_last, last_width, main_heads, head_width, kt, endw, ret, thru
-    )
-    arrived_last = [shifted(final_last, d) for d in distances]
-
-    result = local_results(
-        packed_main, main_width, 0, head_width, whole_width, query_at, packed_main, cum, rt, scores,
-        entry, enter_main, skip_row, None,
-    )
-    result = local_results(
-        packed_last, last_width, main_heads, head_width, whole_width, query_at, packed_main, cum, rt,
-        scores, entry, enter_last, skip_row, result,
-    )
-    result = add_entering(
-        result, main_width, 0, head_width, query_at, packed_main, entd, arrived_main
-    )
-    result = add_entering(
-        result, last_width, main_heads, head_width, query_at, packed_main, entd, arrived_last
-    )
+    query_at = widths[0] // LANES + 1
+    parts = range(len(PARTS))
+
+    sent = []
+    for i in parts:
+        sent.append(
+            pick_runs(wanted, token_runs, firsts[i] * head_width, widths[i], None if i else aux_rows)
+        )
+        wanted, sent[i] = lax.optimization_barrier((wanted, sent[i]))
+    got, packed, ends, arrived = [], [], [], []
+    aux, tables, result = None, None, None
+
+    def receive(i):
+        nonlocal aux, tables
+        columns = widths[i] if i else widths[i] + AUX
+        packed.append(pick_runs(slot, got[i], 0, columns).reshape(tokens, columns))
+        if not i:
+            aux = packed[0]
+            tables = prepare(aux, widths[0], decay_row, scalars)
+        kt, endw, ret, thru = tables[3], tables[4], tables[7], tables[8]
+        ends.append(states(packed[i], widths[i], firsts[i], head_width, kt, endw, ret, thru))
+        arrived.append([shifted(ends[i][0], d) for d in range(1, shards)])
+
+    def local(i, result):
+        cum, rt, scores, entry = tables[0], tables[1], tables[2], tables[5]
+        return local_results(
+            packed[i], widths[i], firsts[i], head_width, whole_width, query_at, aux, cum, rt, scores,
+            entry, ends[i][1], skip_row, result,
+        )
+
+    def entering(i, result):
+        return add_entering(
+            result, widths[i], firsts[i], head_width, query_at, aux, tables[6], arrived[i]
+        )
+
+    got.append(exchange(sent[0]))
+    got[0], sent[1] = lax.optimization_barrier((got[0], sent[1]))
+    got.append(exchange(sent[1]))
+    receive(0)
+    result = entering(0, local(0, result))
+    got[1], sent[2], result = lax.optimization_barrier((got[1], sent[2], result))
+    got.append(exchange(sent[2]))
+    receive(1)
+    result = local(1, result)
+    receive(2)
+    result = local(2, result)
+    result = entering(1, result)
+    result = entering(2, result)
     return result[None]
 
 

time: 1190 us -> 310 us (0.26)
  Pallas kernels: 1040 us -> 143 us
  starting transfers between devices: 33.9 us -> 51.1 us
  waiting for transfers between devices: 81.3 us -> 97.7 us
  local copies, waits for them, and re-layouts: 26.6 us -> 11.5 us
    pallas_call x4 -> x6, Pallas kernels: 946 us -> 35.4 us  [pick_runs(): pl.pallas_call(kernel, out_shape=jax.ShapeDtypeStruct((count, SEG, total)...]
    all_to_all x2 -> x3, waiting for transfers between devices: 78 us -> 94.4 us  [exchange(): rows = lax.all_to_all(rows, 'dp', split_axis=0, concat_axis=0, tiled=True)]
    unnamed x40 -> x30, local copies, waits for them, and re-layouts: 24.4 us -> 8.15 us
    ppermute x6 -> x9, starting transfers between devices: 16.6 us -> 29.6 us  [shifted(): lax.ppermute(block, 'seq', [(i, i + distance) for i in range(count - dist...]
    pallas_call x2 -> x3, Pallas kernels: 24.3 us -> 29.4 us  [states(): pl.pallas_call(kernel, out_shape=(jax.ShapeDtypeStruct((LANES + 16, width...]
    pallas_call x2 -> x3, Pallas kernels: 39.4 us -> 42.9 us  [local_results(): pl.pallas_call(kernel, out_shape=jax.ShapeDtypeStruct((tokens, whole_widt...]
    pallas_call x2 -> x3, Pallas kernels: 25.5 us -> 28.3 us  [add_entering(): pl.pallas_call(kernel, out_shape=jax.ShapeDtypeStruct(result.shape, resul...]
  transfers between devices with their start and end apart: 9 -> 13, of which waited for: 2 -> 3; matrix products, arithmetic and copies ran while one was open for 0% -> 1% of each run, Pallas kernels for 52% -> 42%
where the time goes in v2:
time: 310 us; the launch traced here: 306 us
  Pallas kernels  143 us (46%)
  waiting for transfers between devices  97.7 us (32%)
  starting transfers between devices  51.1 us (16%)
  local copies, waits for them, and re-layouts  11.5 us (4%)
    all_to_all x3, waiting for transfers between devices, exchange(): rows = lax.all_to_all(rows, 'dp', split_axis=0, concat_axis=0, tiled=True)  94.4 us
    pallas_call x3, Pallas kernels, local_results(): pl.pallas_call(kernel, out_shape=jax.ShapeDtypeStruct((tokens, whole_widt...  42.9 us
    pallas_call x6, Pallas kernels, pick_runs(): pl.pallas_call(kernel, out_shape=jax.ShapeDtypeStruct((count, SEG, total)...  35.4 us
    ppermute x9, starting transfers between devices, shifted(): lax.ppermute(block, 'seq', [(i, i + distance) for i in range(count - dist...  29.6 us
    pallas_call x3, Pallas kernels, states(): pl.pallas_call(kernel, out_shape=(jax.ShapeDtypeStruct((LANES + 16, width...  29.4 us
    pallas_call x3, Pallas kernels, add_entering(): pl.pallas_call(kernel, out_shape=jax.ShapeDtypeStruct(result.shape, resul...  28.3 us
    all_to_all x3, starting transfers between devices, exchange(): rows = lax.all_to_all(rows, 'dp', split_axis=0, concat_axis=0, tiled=True)  14.1 us
    unnamed x30, local copies, waits for them, and re-layouts  8.15 us
  transfers between devices with their start and end apart: 13, of which 3 were waited for; matrix products, arithmetic and copies ran while one was open for 1% of the time, Pallas kernels for 42%

profile of v2, /device:TPU:0, one launch (start us, length us, event | category | flops | bytes accessed | tf_op | source)
XLA Modules:
  0.0 306.0 jit_solution(5684380998498715538)
XLA Ops:
  2.2 7.4 %all-to-all-start = ((s32[32,1,6]{2,1,0:T(1,128)}), s32[32,1,6]{2,1,0:T(1,128)S(1)}, u32[]{:S(2)}, u32[]{:S(2)}) async-start(s32[32,1,6]{2,1,0:T(1,128)} %bitcast), calls=%async_computation | async-start | bytes 32768 | tf_op jit(solution)/shard_map/all_to_all | solution.py:435
  13.7 3.2 %all-to-all-done = s32[32,1,6]{2,1,0:T(1,128)S(1)} async-done(((s32[32,1,6]{2,1,0:T(1,128)}), s32[32,1,6]{2,1,0:T(1,128)S(1)}, u32[]{:S(2)}, u32[]{:S(2)}) %all-to-all-start) | async-done | bytes 800 | tf_op jit(solution)/shard_map/all_to_all | solution.py:435
  18.8 8.2 %shard_map.83 = bf16[192,8,2432]{2,1,0:T(8,128)(2,1)} custom-call(s32[192]{0:T(256)} %reshape.107.ids_ref, bf16[160,8,5120]{2,1,0:T(8,128)(2,1)} %bitcast.31, bf16[160,8,384]{2,1,0:T(8,128)(2,1)} %bitcast.18), custom_call_target="tpu_custom_call" | custom-call | bytes 14942208 | tf_op jit(solution)/shard_map/pallas_call | solution.py:71
  27.0 5.0 %all-to-all-start.1 = ((bf16[32,48,2432]{2,1,0:T(8,128)(2,1)}), bf16[32,48,2432]{2,1,0:T(8,128)(2,1)}, u32[]{:S(2)}, u32[]{:S(2)}) async-start(bf16[32,48,2432]{2,1,0:T(8,128)(2,1)} %bitcast.36), calls=%async_computation.1 | async-start | bytes 14942208 | tf_op jit(solution)/shard_map/all_to_all | solution.py:444
  32.0 6.6 %shard_map.84 = bf16[192,8,2048]{2,1,0:T(8,128)(2,1)} custom-call(s32[192]{0:T(256)} %reshape.107.ids_ref, bf16[160,8,5120]{2,1,0:T(8,128)(2,1)} %bitcast.32), custom_call_target="tpu_custom_call" | custom-call | bytes 12582912 | tf_op jit(solution)/shard_map/pallas_call | solution.py:71
  38.6 87.4 %all-to-all-done.1 = bf16[32,48,2432]{2,1,0:T(8,128)(2,1)} async-done(((bf16[32,48,2432]{2,1,0:T(8,128)(2,1)}), bf16[32,48,2432]{2,1,0:T(8,128)(2,1)}, u32[]{:S(2)}, u32[]{:S(2)}) %all-to-all-start.1) | async-done | bytes 7471136 | tf_op jit(solution)/shard_map/all_to_all | solution.py:444
  126.0 5.0 %all-to-all-start.2 = ((bf16[32,48,2048]{2,1,0:T(8,128)(2,1)}), bf16[32,48,2048]{2,1,0:T(8,128)(2,1)}, u32[]{:S(2)}, u32[]{:S(2)}) async-start(bf16[32,48,2048]{2,1,0:T(8,128)(2,1)} %bitcast.37), calls=%async_computation.2 | async-start | bytes 12582912 | tf_op jit(solution)/shard_map/all_to_all | solution.py:444
  132.2 6.2 %shard_map.85 = bf16[160,8,2432]{2,1,0:T(8,128)(2,1)} custom-call(s32[160]{0:T(256)} %copy-done.11, bf16[192,8,2432]{2,1,0:T(8,128)(2,1)} %bitcast.5.refs_0_), custom_call_target="tpu_custom_call" | custom-call | bytes 12451840 | tf_op jit(solution)/shard_map/pallas_call | solution.py:71
  138.4 6.6 %shard_map.86 = (f32[1280,128]{1,0:T(8,128)}, f32[5,128,256]{2,1,0:T(8,128)}, f32[5,256,256]{2,1,0:T(8,128)}, bf16[5,128,256]{2,1,0:T(8,128)(2,1)}, f32[1280,128...) custom-call(s32[7]{0:T(128)} %pad_add_fusion.sc_ref, ...), custom_call_target="tpu_custom_call" | custom-call | flops 587202560 | bytes 6291456 | tf_op jit(solution)/shard_map/pallas_call | solution.py:165
  145.1 11.4 %shard_map.88 = (bf16[144,2048]{1,0:T(8,128)(2,1)}, bf16[5,256,2048]{2,1,0:T(8,128)(2,1)}) custom-call(bf16[1280,2432]{1,0:T(8,128)(2,1)} %bitcast.23, bf16[5,128,256]{2,1,0:T(8,128)(2,1)} %get-tuple-element.38.kt_ref, f32[1280,128]{1,0:T(8,128)} %get-tuple-element.39.endw_ref, f32[5,8,128]{2,1,0:T(8,128)} %get-tuple-element.40.ret_ref, ...), custom_call_target="tpu_custom_call" | custom-call | flops 1677721600 | bytes 13107200 | tf_op jit(solution)/shard_map/pallas_call | solution.py:258
  156.5 3.8 %collective-permute-start = (bf16[144,2048]{1,0:T(8,128)(2,1)}, bf16[144,2048]{1,0:T(8,128)(2,1)S(1)}, u32[]{:S(2)}, u32[]{:S(2)}) collective-permute-start(bf16[144,2048]{1,0:T(8,128)(2,1)} %get-tuple-element.42), channel_id=1, source_target_pairs={{0,1},{1,2},{2,3},{4,5},{5,6},{6,7},{8,9},{9,10},{10,11},{12,13},{... | collective-permute-start | bytes 1769480 | tf_op jit(solution)/shard_map/ppermute | solution.py:412
  160.3 5.5 %collective-permute-start.1 = (bf16[144,2048]{1,0:T(8,128)(2,1)}, bf16[144,2048]{1,0:T(8,128)(2,1)S(1)}, u32[]{:S(2)}, u32[]{:S(2)}) collective-permute-start(bf16[144,2048]{1,0:T(8,128)(2,1)} %get-tuple-element.42), channel_id=1, source_target_pairs={{0,2},{1,3},{4,6},{5,7},{8,10},{9,11},{12,14},{13,15},{16,18},{17,... | collective-permute-start | bytes 1769480 | tf_op jit(solution)/shard_map/ppermute | solution.py:412
  165.8 1.3 collective-permute-start.2
  168.0 5.2 %shard_map.87 = bf16[192,8,1024]{2,1,0:T(8,128)(2,1)} custom-call(s32[192]{0:T(256)} %reshape.107.ids_ref, bf16[160,8,5120]{2,1,0:T(8,128)(2,1)} %bitcast.33), custom_call_target="tpu_custom_call" | custom-call | bytes 6291456 | tf_op jit(solution)/shard_map/pallas_call | solution.py:71
  173.2 16.6 %shard_map.89.rest_3_ = bf16[1280,5120]{1,0:T(8,128)(2,1)} custom-call(bf16[1280,2432]{1,0:T(8,128)(2,1)} %bitcast.24, bf16[1280,2432]{1,0:T(8,128)(2,1)} %bitcast.25, f32[1280,128]{1,0:T(8,128)} %get-tuple-element.43.cum_ref, f32[5,128,256]{2,1,0:T(8,128)} %get-tuple-element.44.rt_ref, f32[5,256,256]{2,1,0:T(8,128)} %get-tuple-element.45.score_ref, ...), custom_call_target="tpu_custom_call" | custom-call | flops 5368709120 | bytes 15728640 | tf_op jit(solution)/shard_map/pallas_call | solution.py:334
  191.0 11.0 %shard_map.90.rest_0_ = bf16[1280,5120]{1,0:T(8,128)(2,1)} custom-call(bf16[1280,2432]{1,0:T(8,128)(2,1)} %bitcast.26, f32[1280,128]{1,0:T(8,128)} %get-tuple-element.34.entd_ref, bf16[144,2048]{1,0:T(8,128)(2,1)} %copy-done.5, bf16[144,2048]{1,0:T(8,128)(2,1)} %copy-done.6, bf16[144,2048]{1,0:T(8,128)(2,1)} %copy-done.7, ...), custom_call_target="tpu_custom_call", output_to_operand_aliasing={{}: (5, {})} | custom-call | flops 2013265920 | bytes 10485760 | tf_op jit(solution)/shard_map/pallas_call | solution.py:389
  201.9 7.0 %all-to-all-done.2 = bf16[32,48,2048]{2,1,0:T(8,128)(2,1)} async-done(((bf16[32,48,2048]{2,1,0:T(8,128)(2,1)}), bf16[32,48,2048]{2,1,0:T(8,128)(2,1)}, u32[]{:S(2)}, u32[]{:S(2)}) %all-to-all-start.2) | async-done | bytes 6291488 | tf_op jit(solution)/shard_map/all_to_all | solution.py:444
  208.9 4.1 %all-to-all-start.3 = ((bf16[32,48,1024]{2,1,0:T(8,128)(2,1)}), bf16[32,48,1024]{2,1,0:T(8,128)(2,1)S(1)}, u32[]{:S(2)}, u32[]{:S(2)}) async-start(bf16[32,48,1024]{2,1,0:T(8,128)(2,1)} %bitcast.12), calls=%async_computation.3 | async-start | bytes 6291456 | tf_op jit(solution)/shard_map/all_to_all | solution.py:444
  213.0 5.4 %shard_map.93 = bf16[160,8,2048]{2,1,0:T(8,128)(2,1)} custom-call(s32[160]{0:T(256)} %copy-done.11, bf16[192,8,2048]{2,1,0:T(8,128)(2,1)} %bitcast.11.refs_0_), custom_call_target="tpu_custom_call" | custom-call | bytes 10485760 | tf_op jit(solution)/shard_map/pallas_call | solution.py:71
  218.4 11.4 %shard_map.94 = (bf16[144,2048]{1,0:T(8,128)(2,1)}, bf16[5,256,2048]{2,1,0:T(8,128)(2,1)}) custom-call(bf16[1280,2048]{1,0:T(8,128)(2,1)} %bitcast.34, bf16[5,128,256]{2,1,0:T(8,128)(2,1)} %get-tuple-element.38.kt_ref, f32[1280,128]{1,0:T(8,128)} %get-tuple-element.39.endw_ref, f32[5,8,128]{2,1,0:T(8,128)} %get-tuple-element.40.ret_ref, ...), custom_call_target="tpu_custom_call" | custom-call | flops 1677721600 | bytes 13107200 | tf_op jit(solution)/shard_map/pallas_call | solution.py:258
  229.8 4.6 %collective-permute-start.6 = (bf16[144,2048]{1,0:T(8,128)(2,1)}, bf16[144,2048]{1,0:T(8,128)(2,1)}, u32[]{:S(2)}, u32[]{:S(2)}) collective-permute-start(bf16[144,2048]{1,0:T(8,128)(2,1)} %get-tuple-element.51), channel_id=1, source_target_pairs={{0,1},{1,2},{2,3},{4,5},{5,6},{6,7},{8,9},{9,10},{10,11},{12,13},{... | collective-permute-start | bytes 1769480 | tf_op jit(solution)/shard_map/ppermute | solution.py:412
  234.4 5.6 %collective-permute-start.7 = (bf16[144,2048]{1,0:T(8,128)(2,1)}, bf16[144,2048]{1,0:T(8,128)(2,1)}, u32[]{:S(2)}, u32[]{:S(2)}) collective-permute-start(bf16[144,2048]{1,0:T(8,128)(2,1)} %get-tuple-element.51), channel_id=1, source_target_pairs={{0,2},{1,3},{4,6},{5,7},{8,10},{9,11},{12,14},{13,15},{16,18},{17,... | collective-permute-start | bytes 1769480 | tf_op jit(solution)/shard_map/ppermute | solution.py:412
  240.0 2.1 collective-permute-start.8
  242.1 16.9 %shard_map.95.rest_0_ = bf16[1280,5120]{1,0:T(8,128)(2,1)} custom-call(bf16[1280,2048]{1,0:T(8,128)(2,1)} %bitcast.35, bf16[1280,2432]{1,0:T(8,128)(2,1)} %bitcast.27, f32[1280,128]{1,0:T(8,128)} %get-tuple-element.43.cum_ref, f32[5,128,256]{2,1,0:T(8,128)} %get-tuple-element.44.rt_ref, ...), custom_call_target="tpu_custom_call", output_to_operand_aliasing={{}: (8, {})} | custom-call | flops 5368709120 | bytes 15728640 | tf_op jit(solution)/shard_map/pallas_call | solution.py:334
  259.0 1.7 copy-done.4
  260.6 3.9 %shard_map.91 = bf16[160,8,1024]{2,1,0:T(8,128)(2,1)} custom-call(s32[160]{0:T(256)} %copy-done.11, bf16[192,8,1024]{2,1,0:T(8,128)(2,1)} %bitcast.40), custom_call_target="tpu_custom_call" | custom-call | bytes 5242880 | tf_op jit(solution)/shard_map/pallas_call | solution.py:71
  264.5 6.5 %shard_map.92 = (bf16[144,1024]{1,0:T(8,128)(2,1)}, bf16[5,256,1024]{2,1,0:T(8,128)(2,1)}) custom-call(bf16[1280,1024]{1,0:T(8,128)(2,1)} %bitcast.38, bf16[5,128,256]{2,1,0:T(8,128)(2,1)} %get-tuple-element.38.kt_ref, f32[1280,128]{1,0:T(8,128)} %get-tuple-element.39.endw_ref, f32[5,8,128]{2,1,0:T(8,128)} %get-tuple-element.40.ret_ref, ...), custom_call_target="tpu_custom_call" | custom-call | flops 838860800 | bytes 6553600 | tf_op jit(solution)/shard_map/pallas_call | solution.py:258
  272.3 3.8 %collective-permute-start.4 = (bf16[144,1024]{1,0:T(8,128)(2,1)}, bf16[144,1024]{1,0:T(8,128)(2,1)S(1)}, u32[]{:S(2)}, u32[]{:S(2)}) collective-permute-start(bf16[144,1024]{1,0:T(8,128)(2,1)} %get-tuple-element.49), channel_id=1, source_target_pairs={{0,2},{1,3},{4,6},{5,7},{8,10},{9,11},{12,14},{13,15},{16,18},{17,... | collective-permute-start | bytes 884744 | tf_op jit(solution)/shard_map/ppermute | solution.py:412
  276.2 1.5 collective-permute-start.5
  277.7 9.4 %shard_map.96.rest_3_ = bf16[1280,5120]{1,0:T(8,128)(2,1)} custom-call(bf16[1280,1024]{1,0:T(8,128)(2,1)} %bitcast.39, bf16[1280,2432]{1,0:T(8,128)(2,1)} %bitcast.28, f32[1280,128]{1,0:T(8,128)} %get-tuple-element.43.cum_ref, f32[5,128,256]{2,1,0:T(8,128)} %get-tuple-element.44.rt_ref, ...), custom_call_target="tpu_custom_call", output_to_operand_aliasing={{}: (8, {})} | custom-call | flops 2684354560 | bytes 7864320 | tf_op jit(solution)/shard_map/pallas_call | solution.py:334
  287.1 11.0 %shard_map.97.rest_3_ = bf16[1280,5120]{1,0:T(8,128)(2,1)} custom-call(bf16[1280,2432]{1,0:T(8,128)(2,1)} %bitcast.29, f32[1280,128]{1,0:T(8,128)} %get-tuple-element.34.entd_ref, bf16[144,2048]{1,0:T(8,128)(2,1)} %collective-permute-done.6.rest_0_, bf16[144,2048]{1,0:T(8,128)(2,1)} %collective-permute-done.7.rest_1_, ...), custom_call_target="tpu_custom_call", output_to_operand_aliasing={{}: (5, {})} | custom-call | flops 2013265920 | bytes 10485760 | tf_op jit(solution)/shard_map/pallas_call | solution.py:389
  299.6 6.4 %shard_map.98 = bf16[1280,5120]{1,0:T(8,128)(2,1)} custom-call(bf16[1280,2432]{1,0:T(8,128)(2,1)} %bitcast.30, f32[1280,128]{1,0:T(8,128)} %get-tuple-element.34.entd_ref, bf16[144,1024]{1,0:T(8,128)(2,1)} %copy-done.8, bf16[144,1024]{1,0:T(8,128)(2,1)} %copy-done.9, bf16[144,1024]{1,0:T(8,128)(2,1)} %copy-done.10, ...), custom_call_target="tpu_custom_call", output_to_operand_aliasing={{}: (5, {})} | custom-call | flops 1006632960 | bytes 5242880 | tf_op jit(solution)/shard_map/pallas_call | solution.py:389
  (57 shorter events, 14.1 us)
Async XLA Ops:
  1.4 25.6 %copy-start.11 = (s32[160]{0:T(256)}, s32[160]{0:T(256)S(1)}, u32[]{:S(2)}) copy-start(s32[160]{0:T(256)S(1)} %multiply_add_fusion.ids_ref) | copy-start | bytes 1924
  2.2 14.7 %all-to-all-start = ((s32[32,1,6]{2,1,0:T(1,128)}), s32[32,1,6]{2,1,0:T(1,128)S(1)}, u32[]{:S(2)}, u32[]{:S(2)}) async-start(s32[32,1,6]{2,1,0:T(1,128)} %bitcast), calls=%async_computation | async-start | bytes 32768 | tf_op jit(solution)/shard_map/all_to_all | solution.py:435
  9.6 1.0 copy-start.1
  10.6 1.0 copy-start.2
  11.6 0.9 copy-start.3
  12.7 1.0 copy-start
  27.0 99.0 %all-to-all-start.1 = ((bf16[32,48,2432]{2,1,0:T(8,128)(2,1)}), bf16[32,48,2432]{2,1,0:T(8,128)(2,1)}, u32[]{:S(2)}, u32[]{:S(2)}) async-start(bf16[32,48,2432]{2,1,0:T(8,128)(2,1)} %bitcast.36), calls=%async_computation.1 | async-start | bytes 14942208 | tf_op jit(solution)/shard_map/all_to_all | solution.py:444
  126.0 5.0 %copy-start.13 = (f32[80]{0:T(128)S(1)}, f32[80]{0:T(128)}, u32[]{:S(2)}) copy-start(f32[80]{0:T(128)} %param.12) | copy-start | bytes 964
  126.0 5.6 %copy-start.14 = (s32[1,6]{1,0:T(1,128)S(1)}, s32[1,6]{1,0:T(1,128)}, u32[]{:S(2)}) copy-start(s32[1,6]{1,0:T(1,128)} %param.15) | copy-start | bytes 76
  126.0 82.9 %all-to-all-start.2 = ((bf16[32,48,2048]{2,1,0:T(8,128)(2,1)}), bf16[32,48,2048]{2,1,0:T(8,128)(2,1)}, u32[]{:S(2)}, u32[]{:S(2)}) async-start(bf16[32,48,2048]{2,1,0:T(8,128)(2,1)} %bitcast.37), calls=%async_computation.2 | async-start | bytes 12582912 | tf_op jit(solution)/shard_map/all_to_all | solution.py:444
  145.1 22.1 %copy-start.12 = (f32[80]{0:T(128)S(1)}, f32[80]{0:T(128)}, u32[]{:S(2)}) copy-start(f32[80]{0:T(128)} %param.13) | copy-start | bytes 964
  156.5 33.3 %collective-permute-start = (bf16[144,2048]{1,0:T(8,128)(2,1)}, bf16[144,2048]{1,0:T(8,128)(2,1)S(1)}, u32[]{:S(2)}, u32[]{:S(2)}) collective-permute-start(bf16[144,2048]{1,0:T(8,128)(2,1)} %get-tuple-element.42), channel_id=1, source_target_pairs={{0,1},{1,2},{2,3},{4,5},{5,6},{6,7},{8,9},{9,10},{10,11},{12,13},{... | collective-permute-start | bytes 1769480 | tf_op jit(solution)/shard_map/ppermute | solution.py:412
  160.3 29.5 %collective-permute-start.1 = (bf16[144,2048]{1,0:T(8,128)(2,1)}, bf16[144,2048]{1,0:T(8,128)(2,1)S(1)}, u32[]{:S(2)}, u32[]{:S(2)}) collective-permute-start(bf16[144,2048]{1,0:T(8,128)(2,1)} %get-tuple-element.42), channel_id=1, source_target_pairs={{0,2},{1,3},{4,6},{5,7},{8,10},{9,11},{12,14},{13,15},{16,18},{17,... | collective-permute-start | bytes 1769480 | tf_op jit(solution)/shard_map/ppermute | solution.py:412
  165.8 24.0 %collective-permute-start.2 = (bf16[144,2048]{1,0:T(8,128)(2,1)}, bf16[144,2048]{1,0:T(8,128)(2,1)S(1)}, u32[]{:S(2)}, u32[]{:S(2)}) collective-permute-start(bf16[144,2048]{1,0:T(8,128)(2,1)} %get-tuple-element.42), channel_id=1, source_target_pairs={{0,3},{4,7},{8,11},{12,15},{16,19},{20,23},{24,27},{28,31},{32,35}... | collective-permute-start | bytes 1769480 | tf_op jit(solution)/shard_map/ppermute | solution.py:412
  189.8 0.8 copy-start.5
  189.8 1.0 copy-start.6
  189.8 1.2 copy-start.7
  208.9 50.0 %all-to-all-start.3 = ((bf16[32,48,1024]{2,1,0:T(8,128)(2,1)}), bf16[32,48,1024]{2,1,0:T(8,128)(2,1)S(1)}, u32[]{:S(2)}, u32[]{:S(2)}) async-start(bf16[32,48,1024]{2,1,0:T(8,128)(2,1)} %bitcast.12), calls=%async_computation.3 | async-start | bytes 6291456 | tf_op jit(solution)/shard_map/all_to_all | solution.py:444
  229.8 46.4 %collective-permute-start.6 = (bf16[144,2048]{1,0:T(8,128)(2,1)}, bf16[144,2048]{1,0:T(8,128)(2,1)}, u32[]{:S(2)}, u32[]{:S(2)}) collective-permute-start(bf16[144,2048]{1,0:T(8,128)(2,1)} %get-tuple-element.51), channel_id=1, source_target_pairs={{0,1},{1,2},{2,3},{4,5},{5,6},{6,7},{8,9},{9,10},{10,11},{12,13},{... | collective-permute-start | bytes 1769480 | tf_op jit(solution)/shard_map/ppermute | solution.py:412
  234.4 52.7 %collective-permute-start.7 = (bf16[144,2048]{1,0:T(8,128)(2,1)}, bf16[144,2048]{1,0:T(8,128)(2,1)}, u32[]{:S(2)}, u32[]{:S(2)}) collective-permute-start(bf16[144,2048]{1,0:T(8,128)(2,1)} %get-tuple-element.51), channel_id=1, source_target_pairs={{0,2},{1,3},{4,6},{5,7},{8,10},{9,11},{12,14},{13,15},{16,18},{17,... | collective-permute-start | bytes 1769480 | tf_op jit(solution)/shard_map/ppermute | solution.py:412
  240.0 47.2 %collective-permute-start.8 = (bf16[144,2048]{1,0:T(8,128)(2,1)}, bf16[144,2048]{1,0:T(8,128)(2,1)}, u32[]{:S(2)}, u32[]{:S(2)}) collective-permute-start(bf16[144,2048]{1,0:T(8,128)(2,1)} %get-tuple-element.51), channel_id=1, source_target_pairs={{0,3},{4,7},{8,11},{12,15},{16,19},{20,23},{24,27},{28,31},{32,35}... | collective-permute-start | bytes 1769480 | tf_op jit(solution)/shard_map/ppermute | solution.py:412
  259.0 1.7 copy-start.4
  271.0 27.1 %collective-permute-start.3 = (bf16[144,1024]{1,0:T(8,128)(2,1)}, bf16[144,1024]{1,0:T(8,128)(2,1)S(1)}, u32[]{:S(2)}, u32[]{:S(2)}) collective-permute-start(bf16[144,1024]{1,0:T(8,128)(2,1)} %get-tuple-element.49), channel_id=1, source_target_pairs={{0,1},{1,2},{2,3},{4,5},{5,6},{6,7},{8,9},{9,10},{10,11},{12,13},{... | collective-permute-start | bytes 884744 | tf_op jit(solution)/shard_map/ppermute | solution.py:412
  272.3 25.8 %collective-permute-start.4 = (bf16[144,1024]{1,0:T(8,128)(2,1)}, bf16[144,1024]{1,0:T(8,128)(2,1)S(1)}, u32[]{:S(2)}, u32[]{:S(2)}) collective-permute-start(bf16[144,1024]{1,0:T(8,128)(2,1)} %get-tuple-element.49), channel_id=1, source_target_pairs={{0,2},{1,3},{4,6},{5,7},{8,10},{9,11},{12,14},{13,15},{16,18},{17,... | collective-permute-start | bytes 884744 | tf_op jit(solution)/shard_map/ppermute | solution.py:412
  276.2 22.0 %collective-permute-start.5 = (bf16[144,1024]{1,0:T(8,128)(2,1)}, bf16[144,1024]{1,0:T(8,128)(2,1)S(1)}, u32[]{:S(2)}, u32[]{:S(2)}) collective-permute-start(bf16[144,1024]{1,0:T(8,128)(2,1)} %get-tuple-element.49), channel_id=1, source_target_pairs={{0,3},{4,7},{8,11},{12,15},{16,19},{20,23},{24,27},{28,31},{32,35}... | collective-permute-start | bytes 884744 | tf_op jit(solution)/shard_map/ppermute | solution.py:412
  298.1 0.7 copy-start.8
  298.1 0.8 copy-start.9
  298.9 0.7 copy-start.10

commit v3 on v2

--- a/solution.py
+++ b/solution.py
@@ -202,14 +202,11 @@
     )(scalars, packed, packed, packed, decay_row)
 
 
-def roll_heads(table, first_head):
-    return pltpu.roll(table, lax.rem(LANES - first_head, LANES), 1)
-
-
-def spreader(width, head_width):
-    lane = lax.broadcasted_iota(jnp.int32, (2 * LANES, width), 1) // head_width
-    source = lax.rem(lax.broadcasted_iota(jnp.int32, (2 * LANES, width), 0), LANES)
-    return (lane == source).astype(bf16)
+def spreader(width, head_width, first_head):
+    lane = lax.broadcasted_iota(jnp.int32, (LANES, width), 1)
+    start = (lax.broadcasted_iota(jnp.int32, (LANES, width), 0) - first_head) * head_width
+    once = ((lane >= start) & (lane < start + head_width)).astype(f32).astype(bf16)
+    return jnp.concatenate([once, once], axis=0)
 
 
 def halves(x):
@@ -217,143 +214,176 @@
     return high, (x - high.astype(f32)).astype(bf16)
 
 
-def spread(table, matrix):
-    return jnp.dot(jnp.concatenate(halves(table), axis=1), matrix, preferred_element_type=f32)
-
-
-def states(packed, width, first_head, head_width, kt, endw, ret, thru):
-    tokens = packed.shape[0]
+def summands(table):
+    return jnp.concatenate(halves(table), axis=1)
+
+
+def spread(pair, matrix):
+    return jnp.dot(pair, matrix, preferred_element_type=f32)
+
+
+def blocks(
+    got, slot, width, first_head, head_width, tables, aux, query_at, skip_row, result, whole_width, with_end, with_local
+):
+    cum, rt, scores, kt, endw, entry, _, ret, thru = tables
+    tokens = slot.shape[0] * SEG
     spans = tokens // SPAN
     step_width = GROUP * head_width
     groups = width // step_width
-
-    def kernel(v_ref, kt_ref, endw_ref, ret_ref, thru_ref, final_ref, enter_ref, state, matrix):
-        g, j = pl.program_id(0), pl.program_id(1)
-        head = first_head + g * GROUP
-
-        @pl.when((g == 0) & (j == 0))
-        def _():
-            matrix[...] = spreader(step_width, head_width)
-
-        @pl.when(j == 0)
-        def _():
-            state[...] = jnp.zeros_like(state)
-
-        repeat = matrix[...]
-        weight = spread(roll_heads(endw_ref[...], head), repeat)
-        scaled = (v_ref[...].astype(f32) * weight).astype(bf16)
-        added = jnp.dot(kt_ref[0], scaled, preferred_element_type=f32)
-        kept = spread(roll_heads(ret_ref[0], head), repeat)[0:1, :]
-        old = state[...]
-        high, low = halves(old)
-        enter_ref[0, 0:LANES, :] = high
-        enter_ref[0, LANES : 2 * LANES, :] = low
-        new = kept * old + added
-        state[...] = new
-        final_ref[0:LANES, :] = new.astype(bf16)
-        through = spread(roll_heads(thru_ref[...], head), repeat)
-        high, low = halves(through)
-        final_ref[LANES : LANES + 16, :] = jnp.concatenate([high, low], axis=0)
-
+    place = first_head * head_width // width
+    half = SPAN // 2
+    runs = SPAN // SEG
+
+    def kernel(slot_ref, *refs):
+        refs = list(refs)
+        got_ref, kt_ref, endw_ref, ret_ref, thru_ref = refs[:5]
+        del refs[:5]
+        if with_local:
+            q_ref, cum_ref, rt_ref, score_ref, entry_ref, skip_ref = refs[:6]
+            del refs[:6]
+            if result is not None:
+                del refs[:1]
+        if with_end:
+            final_ref = refs.pop(0)
+        if with_local:
+            out_ref = refs.pop(0)
+            outs_held, out_sems = refs[-2:]
+        state, matrix, held, sems = refs[:4]
+
+        @pl.loop(0, spans)
+        def _(j):
+            @pl.loop(0, runs, unroll=8)
+            def _(i):
+                pltpu.make_async_copy(
+                    got_ref.at[slot_ref[j * runs + i], :, pl.ds(0, width)], held.at[j, i], sems.at[j]
+                ).start()
+
+        state[...] = jnp.zeros_like(state)
+        for g in range(groups):
+            matrix[g] = spreader(step_width, head_width, first_head + g * GROUP)
+
+        def written(j):
+            return pltpu.make_async_copy(
+                outs_held.at[lax.rem(j, 2)],
+                out_ref.at[pl.ds(pl.multiple_of(j * SPAN, SPAN), SPAN), pl.ds(first_head * head_width, width)],
+                out_sems.at[lax.rem(j, 2)],
+            )
+
+        @pl.loop(0, spans)
+        def _(j):
+            tokens_of = pl.ds(pl.multiple_of(j * SPAN, SPAN), SPAN)
+            end_weight = summands(endw_ref[tokens_of, :])
+            kept_all = summands(ret_ref[j])
+            if with_local:
+                entry_all = summands(entry_ref[tokens_of, :])
+                query = q_ref[tokens_of, :]
+                query = jnp.concatenate([query, query], axis=1)
+                lane = lax.broadcasted_iota(jnp.int32, (half, 2 * head_width), 1)
+
+                @pl.when(j >= 2)
+                def _():
+                    written(j - 2).wait()
+
+            pltpu.make_async_copy(held.at[j], held.at[j], sems.at[j]).wait()
+
+            for g in range(groups):
+                head = first_head + g * GROUP
+                columns = slice(g * step_width, (g + 1) * step_width)
+                block = held[j, :, :, columns].reshape(SPAN, step_width)
+                old = state[:, columns]
+                scaled = block.astype(f32) * spread(end_weight, matrix[g])
+                added = jnp.dot(kt_ref[j], scaled.astype(bf16), preferred_element_type=f32)
+                state[:, columns] = spread(kept_all, matrix[g])[0:1, :] * old + added
+                if not with_local:
+                    continue
+                base = jnp.dot(
+                    query, jnp.concatenate(halves(old), axis=0), preferred_element_type=f32
+                )
+                base = base * spread(entry_all, matrix[g])
+                base = base + skip_ref[:, columns] * block.astype(f32)
+                for pair in range(GROUP // 2):
+                    at = pair * 2 * head_width
+                    values = block[:, at : at + 2 * head_width]
+                    for part in range(2):
+                        reach = (part + 1) * half
+                        rows = slice(part * half, reach)
+                        rows_of = pl.ds(pl.multiple_of(j * SPAN + part * half, half), half)
+                        outs = []
+                        for h in (head + 2 * pair, head + 2 * pair + 1):
+                            gap = cum_ref[rows_of, h : h + 1] - rt_ref[j, h : h + 1, 0:reach]
+                            weights = score_ref[j, rows, 0:reach] * jnp.exp2(
+                                jnp.minimum(gap, CEILING)
+                            )
+                            outs.append(
+                                jnp.dot(
+                                    weights.astype(bf16), values[0:reach], preferred_element_type=f32
+                                )
+                            )
+                        within = jnp.where(lane < head_width, outs[0], outs[1])
+                        to = columns.start + at
+                        outs_held[lax.rem(j, 2), rows, to : to + 2 * head_width] = (
+                            within + base[rows, at : at + 2 * head_width]
+                        ).astype(bf16)
+            if with_local:
+                written(j).start()
+
+        if with_end:
+            through_all = summands(thru_ref[...])
+            for g in range(groups):
+                columns = slice(g * step_width, (g + 1) * step_width)
+                final_ref[0:LANES, columns] = state[:, columns].astype(bf16)
+                high, low = halves(spread(through_all, matrix[g]))
+                final_ref[LANES : LANES + 16, columns] = jnp.concatenate([high, low], axis=0)
+        if with_local:
+            for j in range(max(spans - 2, 0), spans):
+                written(jnp.int32(j)).wait()
+
+    def whole(array, columns=None, at=0):
+        shape = array.shape if columns is None else array.shape[:-1] + (columns,)
+        return pl.BlockSpec(shape, lambda i, s: (0,) * (len(shape) - 1) + (at,))
+
+    anywhere = pl.BlockSpec(memory_space=pl.ANY)
+    operands = [got, kt, endw, ret, thru]
+    in_specs = [anywhere, whole(kt), whole(endw), whole(ret), whole(thru)]
+    out_shape, out_specs, aliases = [], [], {}
+    scratch = [
+        pltpu.VMEM((LANES, width), f32),
+        pltpu.VMEM((groups, 2 * LANES, step_width), bf16),
+        pltpu.VMEM((spans, runs, SEG, width), bf16),
+        pltpu.SemaphoreType.DMA((spans,)),
+    ]
+    if with_end:
+        out_shape.append(jax.ShapeDtypeStruct((LANES + 16, width), bf16))
+        out_specs.append(pl.BlockSpec((LANES + 16, width), lambda i, s: (0, 0)))
+    if with_local:
+        operands += [aux, cum, rt, scores, entry, skip_row]
+        in_specs += [whole(aux, LANES, query_at), whole(cum), whole(rt), whole(scores), whole(entry)]
+        in_specs.append(whole(skip_row, width, place))
+        if result is not None:
+            aliases = {1 + len(operands): len(out_shape)}
+            operands.append(result)
+            in_specs.append(anywhere)
+        out_shape.append(jax.ShapeDtypeStruct((tokens, whole_width), bf16))
+        out_specs.append(anywhere)
+        scratch += [pltpu.VMEM((2, SPAN, width), bf16), pltpu.SemaphoreType.DMA((2,))]
     return pl.pallas_call(
         kernel,
-        out_shape=(
-            jax.ShapeDtypeStruct((LANES + 16, width), bf16),
-            jax.ShapeDtypeStruct((spans, 2 * LANES, width), bf16),
+        out_shape=tuple(out_shape),
+        grid_spec=pltpu.PrefetchScalarGridSpec(
+            num_scalar_prefetch=1,
+            grid=(1,),
+            in_specs=in_specs,
+            out_specs=tuple(out_specs),
+            scratch_shapes=scratch,
         ),
-        grid=(groups, spans),
-        in_specs=[
-            pl.BlockSpec((SPAN, step_width), lambda g, j: (j, g)),
-            pl.BlockSpec((1, LANES, SPAN), lambda g, j: (j, 0, 0)),
-            pl.BlockSpec((SPAN, LANES), lambda g, j: (j, 0)),
-            pl.BlockSpec((1, 8, LANES), lambda g, j: (j, 0, 0)),
-            pl.BlockSpec((8, LANES), lambda g, j: (0, 0)),
-        ],
-        out_specs=[
-            pl.BlockSpec((LANES + 16, step_width), lambda g, j: (0, g)),
-            pl.BlockSpec((1, 2 * LANES, step_width), lambda g, j: (j, 0, g)),
-        ],
-        scratch_shapes=[
-            pltpu.VMEM((LANES, step_width), f32),
-            pltpu.VMEM((2 * LANES, step_width), bf16),
-        ],
-        compiler_params=params(56, "arbitrary", "arbitrary"),
-        cost_estimate=estimate(2 * tokens * width * 2.5 * LANES, 5 * tokens * width),
-    )(packed, kt, endw, ret, thru)
-
-
-def local_results(
-    packed, width, first_head, head_width, whole_width, query_at, aux, cum, rt, scores, entry, enter, skip_row, result
-):
-    tokens = packed.shape[0]
-    spans = tokens // SPAN
-    step_width = GROUP * head_width
-    groups = width // step_width
-    first_group = first_head // GROUP
-    half = SPAN // 2
-
-    def kernel(v_ref, q_ref, cum_ref, rt_ref, score_ref, entry_ref, enter_ref, skip_ref, *rest):
-        out_ref, matrix = rest[-2:]
-        j, g = pl.program_id(0), pl.program_id(1)
-        head = first_head + g * GROUP
-
-        @pl.when((g == 0) & (j == 0))
-        def _():
-            matrix[...] = spreader(step_width, head_width)
-
-        query = q_ref[...]
-        base = jnp.dot(
-            jnp.concatenate([query, query], axis=1), enter_ref[0], preferred_element_type=f32
-        )
-        base = base * spread(roll_heads(entry_ref[...], head), matrix[...])
-        base = base + skip_ref[...] * v_ref[...].astype(f32)
-        total = roll_heads(cum_ref[...], head)
-        lane = lax.broadcasted_iota(jnp.int32, (half, 2 * head_width), 1)
-        first_row = pl.multiple_of(head, 8)
-        for pair in range(GROUP // 2):
-            at = pair * 2 * head_width
-            values = v_ref[:, at : at + 2 * head_width]
-            for part in range(2):
-                reach = (part + 1) * half
-                rows = slice(part * half, reach)
-                outs = []
-                for h in (2 * pair, 2 * pair + 1):
-                    from_row = rt_ref[0, pl.ds(first_row + 8 * (h // 8), 8), 0:reach][h % 8 : h % 8 + 1, :]
-                    gap = total[rows, h : h + 1] - from_row
-                    weights = score_ref[0, rows, 0:reach] * jnp.exp2(jnp.minimum(gap, CEILING))
-                    outs.append(
-                        jnp.dot(weights.astype(bf16), values[0:reach], preferred_element_type=f32)
-                    )
-                within = jnp.where(lane < head_width, outs[0], outs[1])
-                out_ref[rows, at : at + 2 * head_width] = (
-                    within + base[rows, at : at + 2 * head_width]
-                ).astype(out_ref.dtype)
-
-    rows = pl.BlockSpec((SPAN, LANES), lambda j, g: (j, 0))
-    earlier = [] if result is None else [result]
-    return pl.pallas_call(
-        kernel,
-        out_shape=jax.ShapeDtypeStruct((tokens, whole_width), bf16),
-        grid=(spans, groups),
-        in_specs=[
-            pl.BlockSpec((SPAN, step_width), lambda j, g: (j, g)),
-            pl.BlockSpec((SPAN, LANES), lambda j, g: (j, query_at)),
-            rows,
-            pl.BlockSpec((1, LANES, SPAN), lambda j, g: (j, 0, 0)),
-            pl.BlockSpec((1, SPAN, SPAN), lambda j, g: (j, 0, 0)),
-            rows,
-            pl.BlockSpec((1, 2 * LANES, step_width), lambda j, g: (j, 0, g)),
-            pl.BlockSpec((1, step_width), lambda j, g: (0, first_group + g)),
-        ]
-        + [pl.BlockSpec(memory_space=pl.ANY)] * len(earlier),
-        out_specs=pl.BlockSpec((SPAN, step_width), lambda j, g: (j, first_group + g)),
-        scratch_shapes=[pltpu.VMEM((2 * LANES, step_width), bf16)],
-        input_output_aliases={8: 0} if earlier else {},
-        compiler_params=params(56, "arbitrary", "arbitrary"),
+        input_output_aliases=aliases,
+        compiler_params=params(56),
         cost_estimate=estimate(
-            2 * tokens * width * 4 * SPAN, 6 * tokens * width, tokens * SPAN * width // head_width
+            2 * tokens * width * (5 if with_local else 2) * SPAN,
+            6 * tokens * width,
+            tokens * SPAN * width // head_width if with_local else 0,
         ),
-    )(packed, aux, cum, rt, scores, entry, enter, skip_row, *earlier)
+    )(slot, *operands)
 
 
 def add_entering(result, width, first_head, head_width, query_at, aux, entd, arrived):
@@ -361,48 +391,65 @@
     spans = tokens // SPAN
     step_width = GROUP * head_width
     groups = width // step_width
-    first_group = first_head // GROUP
 
     def kernel(q_ref, entd_ref, *rest):
         froms = rest[: len(arrived)]
-        in_ref, out_ref, matrix, state = rest[len(arrived) :]
-        g, j = pl.program_id(0), pl.program_id(1)
-        head = first_head + g * GROUP
-
-        @pl.when((g == 0) & (j == 0))
-        def _():
-            matrix[...] = spreader(step_width, head_width)
-
-        @pl.when(j == 0)
-        def _():
-            incoming = froms[-1][0:LANES, :].astype(f32)
-            for ref in reversed(froms[:-1]):
-                factor = ref[LANES : LANES + 16, :].astype(f32)
-                incoming = ref[0:LANES, :].astype(f32) + (factor[0:1, :] + factor[8:9, :]) * incoming
-            state[...] = incoming.astype(bf16)
-
-        part = jnp.dot(q_ref[...], state[...], preferred_element_type=f32)
-        part = part * spread(roll_heads(entd_ref[...], head), matrix[...])
-        out_ref[...] = (in_ref[...].astype(f32) + part).astype(out_ref.dtype)
-
-    place = pl.BlockSpec((SPAN, step_width), lambda g, j: (j, first_group + g))
+        in_ref, out_ref, matrix, state, held, in_sems, out_sems = rest[len(arrived) :]
+
+        def place(ref, j):
+            first = pl.multiple_of(j * SPAN, SPAN)
+            return ref.at[pl.ds(first, SPAN), pl.ds(first_head * head_width, width)]
+
+        @pl.loop(0, spans)
+        def _(j):
+            pltpu.make_async_copy(place(in_ref, j), held.at[j], in_sems.at[j]).start()
+
+        for g in range(groups):
+            matrix[g] = spreader(step_width, head_width, first_head + g * GROUP)
+        incoming = froms[-1][0:LANES, :].astype(f32)
+        for ref in reversed(froms[:-1]):
+            factor = ref[LANES : LANES + 16, :].astype(f32)
+            incoming = ref[0:LANES, :].astype(f32) + (factor[0:1, :] + factor[8:9, :]) * incoming
+        state[...] = incoming.astype(bf16)
+
+        @pl.loop(0, spans)
+        def _(j):
+            tokens_of = pl.ds(pl.multiple_of(j * SPAN, SPAN), SPAN)
+            entry_all = summands(entd_ref[tokens_of, :])
+            pltpu.make_async_copy(place(in_ref, j), held.at[j], in_sems.at[j]).wait()
+            for g in range(groups):
+                columns = slice(g * step_width, (g + 1) * step_width)
+                part = jnp.dot(
+                    q_ref[tokens_of, :], state[:, columns], preferred_element_type=f32
+                )
+                part = part * spread(entry_all, matrix[g])
+                held[j, :, columns] = (held[j, :, columns].astype(f32) + part).astype(bf16)
+            pltpu.make_async_copy(held.at[j], place(out_ref, j), out_sems.at[j]).start()
+
+        @pl.loop(0, spans)
+        def _(j):
+            pltpu.make_async_copy(held.at[j], place(out_ref, j), out_sems.at[j]).wait()
+
     return pl.pallas_call(
         kernel,
         out_shape=jax.ShapeDtypeStruct(result.shape, result.dtype),
-        grid=(groups, spans),
+        grid=(1,),
         in_specs=[
-            pl.BlockSpec((SPAN, LANES), lambda g, j: (j, query_at)),
-            pl.BlockSpec((SPAN, LANES), lambda g, j: (j, 0)),
+            pl.BlockSpec((tokens, LANES), lambda i: (0, query_at)),
+            pl.BlockSpec((tokens, LANES), lambda i: (0, 0)),
         ]
-        + [pl.BlockSpec((LANES + 16, step_width), lambda g, j: (0, g))] * len(arrived)
-        + [place],
-        out_specs=place,
+        + [pl.BlockSpec((LANES + 16, width), lambda i: (0, 0))] * len(arrived)
+        + [pl.BlockSpec(memory_space=pl.ANY)],
+        out_specs=pl.BlockSpec(memory_space=pl.ANY),
         scratch_shapes=[
-            pltpu.VMEM((2 * LANES, step_width), bf16),
-            pltpu.VMEM((LANES, step_width), bf16),
+            pltpu.VMEM((groups, 2 * LANES, step_width), bf16),
+            pltpu.VMEM((LANES, width), bf16),
+            pltpu.VMEM((spans, SPAN, width), bf16),
+            pltpu.SemaphoreType.DMA((spans,)),
+            pltpu.SemaphoreType.DMA((spans,)),
         ],
         input_output_aliases={2 + len(arrived): 0},
-        compiler_params=params(56, "arbitrary", "arbitrary"),
+        compiler_params=params(56),
         cost_estimate=estimate(2 * tokens * width * 3 * LANES, 4 * tokens * width),
     )(aux, entd, *arrived, result)
 
@@ -451,7 +498,7 @@
     )
     decay_row = jnp.pad(decay_log, (0, LANES - heads))[None, :]
     skip_row = jnp.repeat(skip_gain, head_width)[None, :]
-    query_at = widths[0] // LANES + 1
+    query_at = 1
     parts = range(len(PARTS))
 
     sent = []
@@ -460,26 +507,16 @@
             pick_runs(wanted, token_runs, firsts[i] * head_width, widths[i], None if i else aux_rows)
         )
         wanted, sent[i] = lax.optimization_barrier((wanted, sent[i]))
-    got, packed, ends, arrived = [], [], [], []
-    aux, tables, result = None, None, None
-
-    def receive(i):
-        nonlocal aux, tables
-        columns = widths[i] if i else widths[i] + AUX
-        packed.append(pick_runs(slot, got[i], 0, columns).reshape(tokens, columns))
-        if not i:
-            aux = packed[0]
-            tables = prepare(aux, widths[0], decay_row, scalars)
-        kt, endw, ret, thru = tables[3], tables[4], tables[7], tables[8]
-        ends.append(states(packed[i], widths[i], firsts[i], head_width, kt, endw, ret, thru))
-        arrived.append([shifted(ends[i][0], d) for d in range(1, shards)])
-
-    def local(i, result):
-        cum, rt, scores, entry = tables[0], tables[1], tables[2], tables[5]
-        return local_results(
-            packed[i], widths[i], firsts[i], head_width, whole_width, query_at, aux, cum, rt, scores,
-            entry, ends[i][1], skip_row, result,
+    got, arrived = [], []
+
+    def work(i, result, with_end, with_local):
+        return blocks(
+            got[i], slot, widths[i], firsts[i], head_width, tables, aux, query_at, skip_row, result,
+            whole_width, with_end, with_local,
         )
+
+    def send_end(end):
+        arrived.append([shifted(end, d) for d in range(1, shards)])
 
     def entering(i, result):
         return add_entering(
@@ -489,14 +526,19 @@
     got.append(exchange(sent[0]))
     got[0], sent[1] = lax.optimization_barrier((got[0], sent[1]))
     got.append(exchange(sent[1]))
-    receive(0)
-    result = entering(0, local(0, result))
+    aux = pick_runs(slot, got[0], widths[0], AUX).reshape(tokens, AUX)
+    tables = prepare(aux, 0, decay_row, scalars)
+    end, result = work(0, None, True, True)
+    send_end(end)
+    result = entering(0, result)
     got[1], sent[2], result = lax.optimization_barrier((got[1], sent[2], result))
     got.append(exchange(sent[2]))
-    receive(1)
-    result = local(1, result)
-    receive(2)
-    result = local(2, result)
+    (end,) = work(1, None, True, False)
+    send_end(end)
+    (result,) = work(1, result, False, True)
+    (end,) = work(2, None, True, False)
+    send_end(end)
+    (result,) = work(2, result, False, True)
     result = entering(1, result)
     result = entering(2, result)
     return result[None]

time: 310 us -> 305 us (0.984)
  Pallas kernels: 143 us -> 125 us
  waiting for transfers between devices: 97.7 us -> 109 us
  starting transfers between devices: 51.1 us -> 55 us
    ppermute x9, waiting for transfers between devices: 0.04 us -> 17.4 us  [shifted(): lax.ppermute(block, 'seq', [(i, i + distance) for i in range(count - dist...]
    pallas_call x6 -> x4, Pallas kernels: 35.4 us -> 23.2 us  [pick_runs(): pl.pallas_call(kernel, out_shape=jax.ShapeDtypeStruct((count, SEG, total)...]
    pallas_call x3, Pallas kernels: 28.3 us -> 20.7 us  [add_entering(): pl.pallas_call(kernel, out_shape=jax.ShapeDtypeStruct(result.shape, resul...]
    all_to_all x3, waiting for transfers between devices: 94.4 us -> 88.2 us  [exchange(): rows = lax.all_to_all(rows, 'dp', split_axis=0, concat_axis=0, tiled=True)]
    pallas_call x6 -> x5, Pallas kernels: 72.2 us -> 74.6 us  [blocks(): pl.pallas_call(kernel, out_shape=tuple(out_shape), grid_spec=pltpu.Prefet...]
  transfers between devices with their start and end apart: 13 -> 13, of which waited for: 3 -> 6; matrix products, arithmetic and copies ran while one was open for 1% -> 1% of each run, Pallas kernels for 42% -> 37%
where the time goes in v3:
time: 305 us; the launch traced here: 303 us
  Pallas kernels  125 us (41%)
  waiting for transfers between devices  109 us (36%)
  starting transfers between devices  55 us (18%)
  local copies, waits for them, and re-layouts  11.1 us (4%)
    all_to_all x3, waiting for transfers between devices, exchange(): rows = lax.all_to_all(rows, 'dp', split_axis=0, concat_axis=0, tiled=True)  88.2 us
    pallas_call x5, Pallas kernels, blocks(): pl.pallas_call(kernel, out_shape=tuple(out_shape), grid_spec=pltpu.Prefet...  74.6 us
    ppermute x9, starting transfers between devices, shifted(): lax.ppermute(block, 'seq', [(i, i + distance) for i in range(count - dist...  31.3 us
    pallas_call x4, Pallas kernels, pick_runs(): pl.pallas_call(kernel, out_shape=jax.ShapeDtypeStruct((count, SEG, total)...  23.2 us
    pallas_call x3, Pallas kernels, add_entering(): pl.pallas_call(kernel, out_shape=jax.ShapeDtypeStruct(result.shape, resul...  20.7 us
    ppermute x9, waiting for transfers between devices, shifted(): lax.ppermute(block, 'seq', [(i, i + distance) for i in range(count - dist...  17.4 us
    all_to_all x3, starting transfers between devices, exchange(): rows = lax.all_to_all(rows, 'dp', split_axis=0, concat_axis=0, tiled=True)  16.3 us
    unnamed x30, local copies, waits for them, and re-layouts  7.78 us
  transfers between devices with their start and end apart: 13, of which 6 were waited for; matrix products, arithmetic and copies ran while one was open for 1% of the time, Pallas kernels for 37%

profile of v3, /device:TPU:0, one launch (start us, length us, event | category | flops | bytes accessed | tf_op | source)
XLA Modules:
  0.0 303.4 jit_solution(14291677424242116502)
XLA Ops:
  2.2 7.4 %all-to-all-start = ((s32[32,1,6]{2,1,0:T(1,128)}), s32[32,1,6]{2,1,0:T(1,128)S(1)}, u32[]{:S(2)}, u32[]{:S(2)}) async-start(s32[32,1,6]{2,1,0:T(1,128)} %bitcast), calls=%async_computation | async-start | bytes 32768 | tf_op jit(solution)/shard_map/all_to_all | solution.py:482
  13.7 3.2 %all-to-all-done = s32[32,1,6]{2,1,0:T(1,128)S(1)} async-done(((s32[32,1,6]{2,1,0:T(1,128)}), s32[32,1,6]{2,1,0:T(1,128)S(1)}, u32[]{:S(2)}, u32[]{:S(2)}) %all-to-all-start) | async-done | bytes 800 | tf_op jit(solution)/shard_map/all_to_all | solution.py:482
  18.7 7.5 %shard_map.83 = bf16[192,8,2432]{2,1,0:T(8,128)(2,1)} custom-call(s32[192]{0:T(256)} %reshape.101.ids_ref, bf16[160,8,5120]{2,1,0:T(8,128)(2,1)} %bitcast.18, bf16[160,8,384]{2,1,0:T(8,128)(2,1)} %bitcast.16), custom_call_target="tpu_custom_call" | custom-call | bytes 14942208 | tf_op jit(solution)/shard_map/pallas_call | solution.py:71
  26.3 5.0 %all-to-all-start.1 = ((bf16[32,48,2432]{2,1,0:T(8,128)(2,1)}), bf16[32,48,2432]{2,1,0:T(8,128)(2,1)}, u32[]{:S(2)}, u32[]{:S(2)}) async-start(bf16[32,48,2432]{2,1,0:T(8,128)(2,1)} %bitcast.30), calls=%async_computation.1 | async-start | bytes 14942208 | tf_op jit(solution)/shard_map/all_to_all | solution.py:491
  31.3 6.7 %shard_map.84 = bf16[192,8,2048]{2,1,0:T(8,128)(2,1)} custom-call(s32[192]{0:T(256)} %reshape.101.ids_ref, bf16[160,8,5120]{2,1,0:T(8,128)(2,1)} %bitcast.19), custom_call_target="tpu_custom_call" | custom-call | bytes 12582912 | tf_op jit(solution)/shard_map/pallas_call | solution.py:71
  37.9 87.3 %all-to-all-done.1 = bf16[32,48,2432]{2,1,0:T(8,128)(2,1)} async-done(((bf16[32,48,2432]{2,1,0:T(8,128)(2,1)}), bf16[32,48,2432]{2,1,0:T(8,128)(2,1)}, u32[]{:S(2)}, u32[]{:S(2)}) %all-to-all-start.1) | async-done | bytes 7471136 | tf_op jit(solution)/shard_map/all_to_all | solution.py:491
  125.3 4.9 %all-to-all-start.2 = ((bf16[32,48,2048]{2,1,0:T(8,128)(2,1)}), bf16[32,48,2048]{2,1,0:T(8,128)(2,1)}, u32[]{:S(2)}, u32[]{:S(2)}) async-start(bf16[32,48,2048]{2,1,0:T(8,128)(2,1)} %bitcast.31), calls=%async_computation.2 | async-start | bytes 12582912 | tf_op jit(solution)/shard_map/all_to_all | solution.py:491
  132.2 3.7 %shard_map.85 = bf16[160,8,384]{2,1,0:T(8,128)(2,1)} custom-call(s32[160]{0:T(256)} %copy-done.11, bf16[192,8,2432]{2,1,0:T(8,128)(2,1)} %bitcast.5.refs_0_), custom_call_target="tpu_custom_call" | custom-call | bytes 1966080 | tf_op jit(solution)/shard_map/pallas_call | solution.py:71
  135.9 6.6 %shard_map.86 = (f32[1280,128]{1,0:T(8,128)}, f32[5,128,256]{2,1,0:T(8,128)}, f32[5,256,256]{2,1,0:T(8,128)}, bf16[5,128,256]{2,1,0:T(8,128)(2,1)}, f32[1280,128...) custom-call(s32[7]{0:T(128)} %pad_add_fusion.sc_ref, ...), custom_call_target="tpu_custom_call" | custom-call | flops 587202560 | bytes 6291456 | tf_op jit(solution)/shard_map/pallas_call | solution.py:165
  142.5 22.9 %shard_map.88 = (bf16[144,2048]{1,0:T(8,128)(2,1)}, bf16[1280,5120]{1,0:T(8,128)(2,1)}) custom-call(s32[160]{0:T(256)} %copy-done.11, bf16[192,8,2432]{2,1,0:T(8,128)(2,1)} %bitcast.5.refs_0_, bf16[5,128,256]{2,1,0:T(8,128)(2,1)} %get-tuple-element.34.refs_1_, f32[1280,128]{1,0:T(8,128)} %get-tuple-element.35.refs_2_, ...), custom_call_target="tpu_custom_call" | custom-call | flops 6710886400 | bytes 15728640 | tf_op jit(solution)/shard_map/pallas_call | solution.py:369
  165.4 3.9 %collective-permute-start = (bf16[144,2048]{1,0:T(8,128)(2,1)}, bf16[144,2048]{1,0:T(8,128)(2,1)S(1)}, u32[]{:S(2)}, u32[]{:S(2)}) collective-permute-start(bf16[144,2048]{1,0:T(8,128)(2,1)} %get-tuple-element.42), channel_id=1, source_target_pairs={{0,1},{1,2},{2,3},{4,5},{5,6},{6,7},{8,9},{9,10},{10,11},{12,13},{... | collective-permute-start | bytes 1769480 | tf_op jit(solution)/shard_map/ppermute | solution.py:459
  169.3 5.5 %collective-permute-start.1 = (bf16[144,2048]{1,0:T(8,128)(2,1)}, bf16[144,2048]{1,0:T(8,128)(2,1)S(1)}, u32[]{:S(2)}, u32[]{:S(2)}) collective-permute-start(bf16[144,2048]{1,0:T(8,128)(2,1)} %get-tuple-element.42), channel_id=1, source_target_pairs={{0,2},{1,3},{4,6},{5,7},{8,10},{9,11},{12,14},{13,15},{16,18},{17,... | collective-permute-start | bytes 1769480 | tf_op jit(solution)/shard_map/ppermute | solution.py:459
  174.8 1.3 collective-permute-start.2
  176.1 5.3 %shard_map.87 = bf16[192,8,1024]{2,1,0:T(8,128)(2,1)} custom-call(s32[192]{0:T(256)} %reshape.101.ids_ref, bf16[160,8,5120]{2,1,0:T(8,128)(2,1)} %bitcast.20), custom_call_target="tpu_custom_call" | custom-call | bytes 6291456 | tf_op jit(solution)/shard_map/pallas_call | solution.py:71
  181.4 1.9 collective-permute-done.rest_0_
  183.3 11.8 %collective-permute-done.1.rest_1_ = bf16[144,2048]{1,0:T(8,128)(2,1)S(1)} collective-permute-done((bf16[144,2048]{1,0:T(8,128)(2,1)}, bf16[144,2048]{1,0:T(8,128)(2,1)S(1)}, u32[]{:S(2)}, u32[]{:S(2)}) %collective-permute-start.1) | collective-permute-done | bytes 589856 | tf_op jit(solution)/shard_map/ppermute | solution.py:459
  195.1 3.6 %collective-permute-done.2.rest_2_ = bf16[144,2048]{1,0:T(8,128)(2,1)S(1)} collective-permute-done((bf16[144,2048]{1,0:T(8,128)(2,1)}, bf16[144,2048]{1,0:T(8,128)(2,1)S(1)}, u32[]{:S(2)}, u32[]{:S(2)}) %collective-permute-start.2) | collective-permute-done | bytes 589856 | tf_op jit(solution)/shard_map/ppermute | solution.py:459
  199.6 7.6 %shard_map.89.refs_11_ = bf16[1280,5120]{1,0:T(8,128)(2,1)} custom-call(bf16[1280,384]{1,0:T(8,128)(2,1)} %bitcast.25, f32[1280,128]{1,0:T(8,128)} %get-tuple-element.30.entd_ref, bf16[144,2048]{1,0:T(8,128)(2,1)} %copy-done.5, bf16[144,2048]{1,0:T(8,128)(2,1)} %copy-done.6, bf16[144,2048]{1,0:T(8,128)(2,1)} %copy-done.7, ...), custom_call_target="tpu_custom_call", output_to_operand_aliasing={{}: (5, {})} | custom-call | flops 2013265920 | bytes 10485760 | tf_op jit(solution)/shard_map/pallas_call | solution.py:433
  208.1 6.5 %all-to-all-start.3 = ((bf16[32,48,1024]{2,1,0:T(8,128)(2,1)}), bf16[32,48,1024]{2,1,0:T(8,128)(2,1)S(1)}, u32[]{:S(2)}, u32[]{:S(2)}) async-start(bf16[32,48,1024]{2,1,0:T(8,128)(2,1)} %bitcast.34), calls=%async_computation.3 | async-start | bytes 6291456 | tf_op jit(solution)/shard_map/all_to_all | solution.py:491
  214.6 9.3 %shard_map.91 = bf16[144,2048]{1,0:T(8,128)(2,1)} custom-call(s32[160]{0:T(256)} %copy-done.11, bf16[192,8,2048]{2,1,0:T(8,128)(2,1)} %bitcast.11.refs_0_, bf16[5,128,256]{2,1,0:T(8,128)(2,1)} %get-tuple-element.34.refs_1_, f32[1280,128]{1,0:T(8,128)} %get-tuple-element.35.refs_2_, f32[5,8,128]{2,1,0:T(8,128)} %get-tuple-element.36.refs_3_, ...), custom_call_target="tpu_custom_call" | custom-call | flops 2684354560 | bytes 15728640 | tf_op jit(solution)/shard_map/pallas_call | solution.py:369
  223.8 2.2 collective-permute-start.6
  226.1 7.5 %collective-permute-start.7 = (bf16[144,2048]{1,0:T(8,128)(2,1)}, bf16[144,2048]{1,0:T(8,128)(2,1)}, u32[]{:S(2)}, u32[]{:S(2)}) collective-permute-start(bf16[144,2048]{1,0:T(8,128)(2,1)} %shard_map.91), channel_id=1, source_target_pairs={{0,2},{1,3},{4,6},{5,7},{8,10},{9,11},{12,14},{13,15},{16,18},{17,... | collective-permute-start | bytes 1769480 | tf_op jit(solution)/shard_map/ppermute | solution.py:459
  233.5 2.1 collective-permute-start.8
  235.6 22.1 %shard_map.92.refs_11_ = bf16[1280,5120]{1,0:T(8,128)(2,1)} custom-call(s32[160]{0:T(256)} %copy-done.11, bf16[192,8,2048]{2,1,0:T(8,128)(2,1)} %bitcast.11.refs_0_, bf16[5,128,256]{2,1,0:T(8,128)(2,1)} %get-tuple-element.34.refs_1_, f32[1280,128]{1,0:T(8,128)} %get-tuple-element.35.refs_2_, ...), custom_call_target="tpu_custom_call", output_to_operand_aliasing={{}: (12, {})} | custom-call | flops 6710886400 | bytes 15728640 | tf_op jit(solution)/shard_map/pallas_call | solution.py:369
  257.7 1.6 copy-done.4
  259.4 6.7 %shard_map.90 = bf16[144,1024]{1,0:T(8,128)(2,1)} custom-call(s32[160]{0:T(256)} %copy-done.11, bf16[192,8,1024]{2,1,0:T(8,128)(2,1)} %bitcast.32, bf16[5,128,256]{2,1,0:T(8,128)(2,1)} %get-tuple-element.34.refs_1_, f32[1280,128]{1,0:T(8,128)} %get-tuple-element.35.refs_2_, f32[5,8,128]{2,1,0:T(8,128)} %get-tuple-element.36.refs_3_, ...), custom_call_target="tpu_custom_call" | custom-call | flops 1342177280 | bytes 7864320 | tf_op jit(solution)/shard_map/pallas_call | solution.py:369
  266.1 1.3 collective-permute-start.3
  267.4 6.2 %collective-permute-start.4 = (bf16[144,1024]{1,0:T(8,128)(2,1)}, bf16[144,1024]{1,0:T(8,128)(2,1)S(1)}, u32[]{:S(2)}, u32[]{:S(2)}) collective-permute-start(bf16[144,1024]{1,0:T(8,128)(2,1)} %shard_map.90), channel_id=1, source_target_pairs={{0,2},{1,3},{4,6},{5,7},{8,10},{9,11},{12,14},{13,15},{16,18},{17,... | collective-permute-start | bytes 884744 | tf_op jit(solution)/shard_map/ppermute | solution.py:459
  273.6 1.3 collective-permute-start.5
  274.9 13.6 %shard_map.93.rest_3_ = bf16[1280,5120]{1,0:T(8,128)(2,1)} custom-call(s32[160]{0:T(256)} %copy-done.11, bf16[192,8,1024]{2,1,0:T(8,128)(2,1)} %bitcast.33, bf16[5,128,256]{2,1,0:T(8,128)(2,1)} %get-tuple-element.34.refs_1_, f32[1280,128]{1,0:T(8,128)} %get-tuple-element.35.refs_2_, ...), custom_call_target="tpu_custom_call", output_to_operand_aliasing={{}: (12, {})} | custom-call | flops 3355443200 | bytes 7864320 | tf_op jit(solution)/shard_map/pallas_call | solution.py:369
  288.6 7.6 %shard_map.94.rest_3_ = bf16[1280,5120]{1,0:T(8,128)(2,1)} custom-call(bf16[1280,384]{1,0:T(8,128)(2,1)} %bitcast.28, f32[1280,128]{1,0:T(8,128)} %get-tuple-element.30.entd_ref, bf16[144,2048]{1,0:T(8,128)(2,1)} %collective-permute-done.6.rest_0_, bf16[144,2048]{1,0:T(8,128)(2,1)} %collective-permute-done.7.rest_1_, ...), custom_call_target="tpu_custom_call", output_to_operand_aliasing={{}: (5, {})} | custom-call | flops 2013265920 | bytes 10485760 | tf_op jit(solution)/shard_map/pallas_call | solution.py:433
  297.8 5.5 %shard_map.95 = bf16[1280,5120]{1,0:T(8,128)(2,1)} custom-call(bf16[1280,384]{1,0:T(8,128)(2,1)} %bitcast.29, f32[1280,128]{1,0:T(8,128)} %get-tuple-element.30.entd_ref, bf16[144,1024]{1,0:T(8,128)(2,1)} %copy-done.8, bf16[144,1024]{1,0:T(8,128)(2,1)} %copy-done.9, bf16[144,1024]{1,0:T(8,128)(2,1)} %copy-done.10, ...), custom_call_target="tpu_custom_call", output_to_operand_aliasing={{}: (5, {})} | custom-call | flops 1006632960 | bytes 5242880 | tf_op jit(solution)/shard_map/pallas_call | solution.py:433
  (54 shorter events, 13.3 us)
Async XLA Ops:
  1.4 24.9 %copy-start.11 = (s32[160]{0:T(256)}, s32[160]{0:T(256)S(1)}, u32[]{:S(2)}) copy-start(s32[160]{0:T(256)S(1)} %multiply_add_fusion.ids_ref.slot_ref) | copy-start | bytes 1924
  2.2 14.7 %all-to-all-start = ((s32[32,1,6]{2,1,0:T(1,128)}), s32[32,1,6]{2,1,0:T(1,128)S(1)}, u32[]{:S(2)}, u32[]{:S(2)}) async-start(s32[32,1,6]{2,1,0:T(1,128)} %bitcast), calls=%async_computation | async-start | bytes 32768 | tf_op jit(solution)/shard_map/all_to_all | solution.py:482
  9.6 1.0 copy-start.1
  10.6 1.0 copy-start.2
  11.6 0.9 copy-start.3
  12.7 1.0 copy-start
  26.3 99.0 %all-to-all-start.1 = ((bf16[32,48,2432]{2,1,0:T(8,128)(2,1)}), bf16[32,48,2432]{2,1,0:T(8,128)(2,1)}, u32[]{:S(2)}, u32[]{:S(2)}) async-start(bf16[32,48,2432]{2,1,0:T(8,128)(2,1)} %bitcast.30), calls=%async_computation.1 | async-start | bytes 14942208 | tf_op jit(solution)/shard_map/all_to_all | solution.py:491
  31.2 98.9 %copy-start.12 = (f32[80]{0:T(128)S(1)}, f32[80]{0:T(128)}, u32[]{:S(2)}) copy-start(f32[80]{0:T(128)} %param.13) | copy-start | bytes 964
  31.2 99.7 %copy-start.13 = (f32[80]{0:T(128)S(1)}, f32[80]{0:T(128)}, u32[]{:S(2)}) copy-start(f32[80]{0:T(128)} %param.12) | copy-start | bytes 964
  31.3 100.3 %copy-start.14 = (s32[1,6]{1,0:T(1,128)S(1)}, s32[1,6]{1,0:T(1,128)}, u32[]{:S(2)}) copy-start(s32[1,6]{1,0:T(1,128)} %param.15) | copy-start | bytes 76
  125.3 82.8 %all-to-all-start.2 = ((bf16[32,48,2048]{2,1,0:T(8,128)(2,1)}), bf16[32,48,2048]{2,1,0:T(8,128)(2,1)}, u32[]{:S(2)}, u32[]{:S(2)}) async-start(bf16[32,48,2048]{2,1,0:T(8,128)(2,1)} %bitcast.31), calls=%async_computation.2 | async-start | bytes 12582912 | tf_op jit(solution)/shard_map/all_to_all | solution.py:491
  165.4 17.8 %collective-permute-start = (bf16[144,2048]{1,0:T(8,128)(2,1)}, bf16[144,2048]{1,0:T(8,128)(2,1)S(1)}, u32[]{:S(2)}, u32[]{:S(2)}) collective-permute-start(bf16[144,2048]{1,0:T(8,128)(2,1)} %get-tuple-element.42), channel_id=1, source_target_pairs={{0,1},{1,2},{2,3},{4,5},{5,6},{6,7},{8,9},{9,10},{10,11},{12,13},{... | collective-permute-start | bytes 1769480 | tf_op jit(solution)/shard_map/ppermute | solution.py:459
  169.3 25.8 %collective-permute-start.1 = (bf16[144,2048]{1,0:T(8,128)(2,1)}, bf16[144,2048]{1,0:T(8,128)(2,1)S(1)}, u32[]{:S(2)}, u32[]{:S(2)}) collective-permute-start(bf16[144,2048]{1,0:T(8,128)(2,1)} %get-tuple-element.42), channel_id=1, source_target_pairs={{0,2},{1,3},{4,6},{5,7},{8,10},{9,11},{12,14},{13,15},{16,18},{17,... | collective-permute-start | bytes 1769480 | tf_op jit(solution)/shard_map/ppermute | solution.py:459
  174.8 24.0 %collective-permute-start.2 = (bf16[144,2048]{1,0:T(8,128)(2,1)}, bf16[144,2048]{1,0:T(8,128)(2,1)S(1)}, u32[]{:S(2)}, u32[]{:S(2)}) collective-permute-start(bf16[144,2048]{1,0:T(8,128)(2,1)} %get-tuple-element.42), channel_id=1, source_target_pairs={{0,3},{4,7},{8,11},{12,15},{16,19},{20,23},{24,27},{28,31},{32,35}... | collective-permute-start | bytes 1769480 | tf_op jit(solution)/shard_map/ppermute | solution.py:459
  183.3 15.5 %copy-start.5 = (bf16[144,2048]{1,0:T(8,128)(2,1)}, bf16[144,2048]{1,0:T(8,128)(2,1)S(1)}, u32[]{:S(2)}) copy-start(bf16[144,2048]{1,0:T(8,128)(2,1)S(1)} %collective-permute-done.rest_0_) | copy-start | bytes 1769476
  195.1 3.7 %copy-start.6 = (bf16[144,2048]{1,0:T(8,128)(2,1)}, bf16[144,2048]{1,0:T(8,128)(2,1)S(1)}, u32[]{:S(2)}) copy-start(bf16[144,2048]{1,0:T(8,128)(2,1)S(1)} %collective-permute-done.1.rest_1_) | copy-start | bytes 1769476
  198.7 0.8 copy-start.7
  208.1 49.6 %all-to-all-start.3 = ((bf16[32,48,1024]{2,1,0:T(8,128)(2,1)}), bf16[32,48,1024]{2,1,0:T(8,128)(2,1)S(1)}, u32[]{:S(2)}, u32[]{:S(2)}) async-start(bf16[32,48,1024]{2,1,0:T(8,128)(2,1)} %bitcast.34), calls=%async_computation.3 | async-start | bytes 6291456 | tf_op jit(solution)/shard_map/all_to_all | solution.py:491
  223.8 49.8 %collective-permute-start.6 = (bf16[144,2048]{1,0:T(8,128)(2,1)}, bf16[144,2048]{1,0:T(8,128)(2,1)}, u32[]{:S(2)}, u32[]{:S(2)}) collective-permute-start(bf16[144,2048]{1,0:T(8,128)(2,1)} %shard_map.91), channel_id=1, source_target_pairs={{0,1},{1,2},{2,3},{4,5},{5,6},{6,7},{8,9},{9,10},{10,11},{12,13},{... | collective-permute-start | bytes 1769480 | tf_op jit(solution)/shard_map/ppermute | solution.py:459
  226.1 62.5 %collective-permute-start.7 = (bf16[144,2048]{1,0:T(8,128)(2,1)}, bf16[144,2048]{1,0:T(8,128)(2,1)}, u32[]{:S(2)}, u32[]{:S(2)}) collective-permute-start(bf16[144,2048]{1,0:T(8,128)(2,1)} %shard_map.91), channel_id=1, source_target_pairs={{0,2},{1,3},{4,6},{5,7},{8,10},{9,11},{12,14},{13,15},{16,18},{17,... | collective-permute-start | bytes 1769480 | tf_op jit(solution)/shard_map/ppermute | solution.py:459
  233.5 55.0 %collective-permute-start.8 = (bf16[144,2048]{1,0:T(8,128)(2,1)}, bf16[144,2048]{1,0:T(8,128)(2,1)}, u32[]{:S(2)}, u32[]{:S(2)}) collective-permute-start(bf16[144,2048]{1,0:T(8,128)(2,1)} %shard_map.91), channel_id=1, source_target_pairs={{0,3},{4,7},{8,11},{12,15},{16,19},{20,23},{24,27},{28,31},{32,35}... | collective-permute-start | bytes 1769480 | tf_op jit(solution)/shard_map/ppermute | solution.py:459
  257.7 1.6 copy-start.4
  266.1 30.1 %collective-permute-start.3 = (bf16[144,1024]{1,0:T(8,128)(2,1)}, bf16[144,1024]{1,0:T(8,128)(2,1)S(1)}, u32[]{:S(2)}, u32[]{:S(2)}) collective-permute-start(bf16[144,1024]{1,0:T(8,128)(2,1)} %shard_map.90), channel_id=1, source_target_pairs={{0,1},{1,2},{2,3},{4,5},{5,6},{6,7},{8,9},{9,10},{10,11},{12,13},{... | collective-permute-start | bytes 884744 | tf_op jit(solution)/shard_map/ppermute | solution.py:459
  267.4 28.8 %collective-permute-start.4 = (bf16[144,1024]{1,0:T(8,128)(2,1)}, bf16[144,1024]{1,0:T(8,128)(2,1)S(1)}, u32[]{:S(2)}, u32[]{:S(2)}) collective-permute-start(bf16[144,1024]{1,0:T(8,128)(2,1)} %shard_map.90), channel_id=1, source_target_pairs={{0,2},{1,3},{4,6},{5,7},{8,10},{9,11},{12,14},{13,15},{16,18},{17,... | collective-permute-start | bytes 884744 | tf_op jit(solution)/shard_map/ppermute | solution.py:459
  273.6 22.6 %collective-permute-start.5 = (bf16[144,1024]{1,0:T(8,128)(2,1)}, bf16[144,1024]{1,0:T(8,128)(2,1)S(1)}, u32[]{:S(2)}, u32[]{:S(2)}) collective-permute-start(bf16[144,1024]{1,0:T(8,128)(2,1)} %shard_map.90), channel_id=1, source_target_pairs={{0,3},{4,7},{8,11},{12,15},{16,19},{20,23},{24,27},{28,31},{32,35}... | collective-permute-start | bytes 884744 | tf_op jit(solution)/shard_map/ppermute | solution.py:459
  296.2 0.7 copy-start.8
  296.2 0.8 copy-start.9
  297.0 0.7 copy-start.10

commit v4 on v3

--- a/solution.py
+++ b/solution.py
@@ -230,7 +230,6 @@
     spans = tokens // SPAN
     step_width = GROUP * head_width
     groups = width // step_width
-    place = first_head * head_width // width
     half = SPAN // 2
     runs = SPAN // SEG
 
@@ -300,7 +299,8 @@
                     query, jnp.concatenate(halves(old), axis=0), preferred_element_type=f32
                 )
                 base = base * spread(entry_all, matrix[g])
-                base = base + skip_ref[:, columns] * block.astype(f32)
+                skip = skip_ref[:, head * head_width : head * head_width + step_width]
+                base = base + skip * block.astype(f32)
                 for pair in range(GROUP // 2):
                     at = pair * 2 * head_width
                     values = block[:, at : at + 2 * head_width]
@@ -311,9 +311,8 @@
                         outs = []
                         for h in (head + 2 * pair, head + 2 * pair + 1):
                             gap = cum_ref[rows_of, h : h + 1] - rt_ref[j, h : h + 1, 0:reach]
-                            weights = score_ref[j, rows, 0:reach] * jnp.exp2(
-                                jnp.minimum(gap, CEILING)
-                            )
+                            gap = jnp.minimum(gap, CEILING)
+                            weights = score_ref[j, rows, 0:reach] * jnp.exp2(gap)
                             outs.append(
                                 jnp.dot(
                                     weights.astype(bf16), values[0:reach], preferred_element_type=f32
@@ -358,7 +357,7 @@
     if with_local:
         operands += [aux, cum, rt, scores, entry, skip_row]
         in_specs += [whole(aux, LANES, query_at), whole(cum), whole(rt), whole(scores), whole(entry)]
-        in_specs.append(whole(skip_row, width, place))
+        in_specs.append(whole(skip_row))
         if result is not None:
             aliases = {1 + len(operands): len(out_shape)}
             operands.append(result)
@@ -533,9 +532,8 @@
     result = entering(0, result)
     got[1], sent[2], result = lax.optimization_barrier((got[1], sent[2], result))
     got.append(exchange(sent[2]))
-    (end,) = work(1, None, True, False)
+    end, result = work(1, result, True, True)
     send_end(end)
-    (result,) = work(1, result, False, True)
     (end,) = work(2, None, True, False)
     send_end(end)
     (result,) = work(2, result, False, True)

time: 305 us -> 306 us (level)
  Pallas kernels: 125 us -> 117 us
  waiting for transfers between devices: 109 us -> 116 us
    pallas_call x5 -> x4, Pallas kernels: 74.6 us -> 66 us  [blocks(): pl.pallas_call(kernel, out_shape=tuple(out_shape), grid_spec=pltpu.Prefet...]
    all_to_all x3, waiting for transfers between devices: 88.2 us -> 95.3 us  [exchange(): rows = lax.all_to_all(rows, 'dp', split_axis=0, concat_axis=0, tiled=True)]
  transfers between devices with their start and end apart: 13 -> 13, of which waited for: 6 -> 7; matrix products, arithmetic and copies ran while one was open for 1% -> 1% of each run, Pallas kernels for 37% -> 34%
where the time goes in v4:
time: 306 us; the launch traced here: 304 us
  Pallas kernels  117 us (38%)
  waiting for transfers between devices  116 us (38%)
  starting transfers between devices  56.5 us (18%)
  local copies, waits for them, and re-layouts  11.2 us (4%)
    all_to_all x3, waiting for transfers between devices, exchange(): rows = lax.all_to_all(rows, 'dp', split_axis=0, concat_axis=0, tiled=True)  95.3 us
    pallas_call x4, Pallas kernels, blocks(): pl.pallas_call(kernel, out_shape=tuple(out_shape), grid_spec=pltpu.Prefet...  66 us
    ppermute x9, starting transfers between devices, shifted(): lax.ppermute(block, 'seq', [(i, i + distance) for i in range(count - dist...  32.7 us
    pallas_call x4, Pallas kernels, pick_runs(): pl.pallas_call(kernel, out_shape=jax.ShapeDtypeStruct((count, SEG, total)...  23.7 us
    pallas_call x3, Pallas kernels, add_entering(): pl.pallas_call(kernel, out_shape=jax.ShapeDtypeStruct(result.shape, resul...  20.7 us
    ppermute x9, waiting for transfers between devices, shifted(): lax.ppermute(block, 'seq', [(i, i + distance) for i in range(count - dist...  17.4 us
    all_to_all x3, starting transfers between devices, exchange(): rows = lax.all_to_all(rows, 'dp', split_axis=0, concat_axis=0, tiled=True)  16.4 us
    unnamed x30, local copies, waits for them, and re-layouts  7.78 us
  transfers between devices with their start and end apart: 13, of which 7 were waited for; matrix products, arithmetic and copies ran while one was open for 1% of the time, Pallas kernels for 34%

profile of v4, /device:TPU:0, one launch (start us, length us, event | category | flops | bytes accessed | tf_op | source)
XLA Modules:
  0.0 304.0 jit_solution(14161194722360465351)
XLA Ops:
  2.2 7.4 %all-to-all-start = ((s32[32,1,6]{2,1,0:T(1,128)}), s32[32,1,6]{2,1,0:T(1,128)S(1)}, u32[]{:S(2)}, u32[]{:S(2)}) async-start(s32[32,1,6]{2,1,0:T(1,128)} %bitcast), calls=%async_computation | async-start | bytes 32768 | tf_op jit(solution)/shard_map/all_to_all | solution.py:481
  13.7 3.2 %all-to-all-done = s32[32,1,6]{2,1,0:T(1,128)S(1)} async-done(((s32[32,1,6]{2,1,0:T(1,128)}), s32[32,1,6]{2,1,0:T(1,128)S(1)}, u32[]{:S(2)}, u32[]{:S(2)}) %all-to-all-start) | async-done | bytes 800 | tf_op jit(solution)/shard_map/all_to_all | solution.py:481
  18.8 8.0 %shard_map.83 = bf16[192,8,2432]{2,1,0:T(8,128)(2,1)} custom-call(s32[192]{0:T(256)} %reshape.101.ids_ref, bf16[160,8,5120]{2,1,0:T(8,128)(2,1)} %bitcast.18, bf16[160,8,384]{2,1,0:T(8,128)(2,1)} %bitcast.16), custom_call_target="tpu_custom_call" | custom-call | bytes 14942208 | tf_op jit(solution)/shard_map/pallas_call | solution.py:71
  26.9 4.9 %all-to-all-start.1 = ((bf16[32,48,2432]{2,1,0:T(8,128)(2,1)}), bf16[32,48,2432]{2,1,0:T(8,128)(2,1)}, u32[]{:S(2)}, u32[]{:S(2)}) async-start(bf16[32,48,2432]{2,1,0:T(8,128)(2,1)} %bitcast.30), calls=%async_computation.1 | async-start | bytes 14942208 | tf_op jit(solution)/shard_map/all_to_all | solution.py:490
  31.9 6.7 %shard_map.84 = bf16[192,8,2048]{2,1,0:T(8,128)(2,1)} custom-call(s32[192]{0:T(256)} %reshape.101.ids_ref, bf16[160,8,5120]{2,1,0:T(8,128)(2,1)} %bitcast.19), custom_call_target="tpu_custom_call" | custom-call | bytes 12582912 | tf_op jit(solution)/shard_map/pallas_call | solution.py:71
  38.6 87.3 %all-to-all-done.1 = bf16[32,48,2432]{2,1,0:T(8,128)(2,1)} async-done(((bf16[32,48,2432]{2,1,0:T(8,128)(2,1)}), bf16[32,48,2432]{2,1,0:T(8,128)(2,1)}, u32[]{:S(2)}, u32[]{:S(2)}) %all-to-all-start.1) | async-done | bytes 7471136 | tf_op jit(solution)/shard_map/all_to_all | solution.py:490
  125.8 4.9 %all-to-all-start.2 = ((bf16[32,48,2048]{2,1,0:T(8,128)(2,1)}), bf16[32,48,2048]{2,1,0:T(8,128)(2,1)}, u32[]{:S(2)}, u32[]{:S(2)}) async-start(bf16[32,48,2048]{2,1,0:T(8,128)(2,1)} %bitcast.31), calls=%async_computation.2 | async-start | bytes 12582912 | tf_op jit(solution)/shard_map/all_to_all | solution.py:490
  132.8 3.7 %shard_map.85 = bf16[160,8,384]{2,1,0:T(8,128)(2,1)} custom-call(s32[160]{0:T(256)} %copy-done.11, bf16[192,8,2432]{2,1,0:T(8,128)(2,1)} %bitcast.5.refs_0_), custom_call_target="tpu_custom_call" | custom-call | bytes 1966080 | tf_op jit(solution)/shard_map/pallas_call | solution.py:71
  136.5 6.6 %shard_map.86 = (f32[1280,128]{1,0:T(8,128)}, f32[5,128,256]{2,1,0:T(8,128)}, f32[5,256,256]{2,1,0:T(8,128)}, bf16[5,128,256]{2,1,0:T(8,128)(2,1)}, f32[1280,128...) custom-call(s32[7]{0:T(128)} %pad_add_fusion.sc_ref, ...), custom_call_target="tpu_custom_call" | custom-call | flops 587202560 | bytes 6291456 | tf_op jit(solution)/shard_map/pallas_call | solution.py:165
  143.1 22.8 %shard_map.88 = (bf16[144,2048]{1,0:T(8,128)(2,1)}, bf16[1280,5120]{1,0:T(8,128)(2,1)}) custom-call(s32[160]{0:T(256)} %copy-done.11, bf16[192,8,2432]{2,1,0:T(8,128)(2,1)} %bitcast.5.refs_0_, bf16[5,128,256]{2,1,0:T(8,128)(2,1)} %get-tuple-element.36.refs_1_, f32[1280,128]{1,0:T(8,128)} %get-tuple-element.37.refs_2_, ...), custom_call_target="tpu_custom_call" | custom-call | flops 6710886400 | bytes 15728640 | tf_op jit(solution)/shard_map/pallas_call | solution.py:368
  165.9 3.9 %collective-permute-start = (bf16[144,2048]{1,0:T(8,128)(2,1)}, bf16[144,2048]{1,0:T(8,128)(2,1)S(1)}, u32[]{:S(2)}, u32[]{:S(2)}) collective-permute-start(bf16[144,2048]{1,0:T(8,128)(2,1)} %get-tuple-element.44), channel_id=1, source_target_pairs={{0,1},{1,2},{2,3},{4,5},{5,6},{6,7},{8,9},{9,10},{10,11},{12,13},{... | collective-permute-start | bytes 1769480 | tf_op jit(solution)/shard_map/ppermute | solution.py:458
  169.8 5.5 %collective-permute-start.1 = (bf16[144,2048]{1,0:T(8,128)(2,1)}, bf16[144,2048]{1,0:T(8,128)(2,1)S(1)}, u32[]{:S(2)}, u32[]{:S(2)}) collective-permute-start(bf16[144,2048]{1,0:T(8,128)(2,1)} %get-tuple-element.44), channel_id=1, source_target_pairs={{0,2},{1,3},{4,6},{5,7},{8,10},{9,11},{12,14},{13,15},{16,18},{17,... | collective-permute-start | bytes 1769480 | tf_op jit(solution)/shard_map/ppermute | solution.py:458
  175.3 1.3 collective-permute-start.2
  176.6 5.2 %shard_map.87 = bf16[192,8,1024]{2,1,0:T(8,128)(2,1)} custom-call(s32[192]{0:T(256)} %reshape.101.ids_ref, bf16[160,8,5120]{2,1,0:T(8,128)(2,1)} %bitcast.20), custom_call_target="tpu_custom_call" | custom-call | bytes 6291456 | tf_op jit(solution)/shard_map/pallas_call | solution.py:71
  181.8 1.9 collective-permute-done.rest_0_
  183.8 11.8 %collective-permute-done.1.rest_1_ = bf16[144,2048]{1,0:T(8,128)(2,1)S(1)} collective-permute-done((bf16[144,2048]{1,0:T(8,128)(2,1)}, bf16[144,2048]{1,0:T(8,128)(2,1)S(1)}, u32[]{:S(2)}, u32[]{:S(2)}) %collective-permute-start.1) | collective-permute-done | bytes 589856 | tf_op jit(solution)/shard_map/ppermute | solution.py:458
  195.6 3.7 %collective-permute-done.2.rest_2_ = bf16[144,2048]{1,0:T(8,128)(2,1)S(1)} collective-permute-done((bf16[144,2048]{1,0:T(8,128)(2,1)}, bf16[144,2048]{1,0:T(8,128)(2,1)S(1)}, u32[]{:S(2)}, u32[]{:S(2)}) %collective-permute-start.2) | collective-permute-done | bytes 589856 | tf_op jit(solution)/shard_map/ppermute | solution.py:458
  200.1 7.6 %shard_map.89.refs_11_ = bf16[1280,5120]{1,0:T(8,128)(2,1)} custom-call(bf16[1280,384]{1,0:T(8,128)(2,1)} %bitcast.25, f32[1280,128]{1,0:T(8,128)} %get-tuple-element.32.entd_ref, bf16[144,2048]{1,0:T(8,128)(2,1)} %copy-done.5, bf16[144,2048]{1,0:T(8,128)(2,1)} %copy-done.6, bf16[144,2048]{1,0:T(8,128)(2,1)} %copy-done.7, ...), custom_call_target="tpu_custom_call", output_to_operand_aliasing={{}: (5, {})} | custom-call | flops 2013265920 | bytes 10485760 | tf_op jit(solution)/shard_map/pallas_call | solution.py:432
  208.7 6.6 %all-to-all-start.3 = ((bf16[32,48,1024]{2,1,0:T(8,128)(2,1)}), bf16[32,48,1024]{2,1,0:T(8,128)(2,1)S(1)}, u32[]{:S(2)}, u32[]{:S(2)}) async-start(bf16[32,48,1024]{2,1,0:T(8,128)(2,1)} %bitcast.34), calls=%async_computation.3 | async-start | bytes 6291456 | tf_op jit(solution)/shard_map/all_to_all | solution.py:490
  215.3 22.7 %shard_map.91 = (bf16[144,2048]{1,0:T(8,128)(2,1)}, bf16[1280,5120]{1,0:T(8,128)(2,1)}) custom-call(s32[160]{0:T(256)} %copy-done.11, bf16[192,8,2048]{2,1,0:T(8,128)(2,1)} %bitcast.11.refs_0_, bf16[5,128,256]{2,1,0:T(8,128)(2,1)} %get-tuple-element.36.refs_1_, f32[1280,128]{1,0:T(8,128)} %get-tuple-element.37.refs_2_, ...), custom_call_target="tpu_custom_call", output_to_operand_aliasing={{1}: (12, {})} | custom-call | flops 6710886400 | bytes 15728640 | tf_op jit(solution)/shard_map/pallas_call | solution.py:368
  238.0 2.3 collective-permute-start.6
  240.3 7.4 %collective-permute-start.7 = (bf16[144,2048]{1,0:T(8,128)(2,1)}, bf16[144,2048]{1,0:T(8,128)(2,1)}, u32[]{:S(2)}, u32[]{:S(2)}) collective-permute-start(bf16[144,2048]{1,0:T(8,128)(2,1)} %get-tuple-element.49), channel_id=1, source_target_pairs={{0,2},{1,3},{4,6},{5,7},{8,10},{9,11},{12,14},{13,15},{16,18},{17,... | collective-permute-start | bytes 1769480 | tf_op jit(solution)/shard_map/ppermute | solution.py:458
  247.7 2.1 collective-permute-start.8
  249.8 7.0 %all-to-all-done.3 = bf16[32,48,1024]{2,1,0:T(8,128)(2,1)S(1)} async-done(((bf16[32,48,1024]{2,1,0:T(8,128)(2,1)}), bf16[32,48,1024]{2,1,0:T(8,128)(2,1)S(1)}, u32[]{:S(2)}, u32[]{:S(2)}) %all-to-all-start.3) | async-done | bytes 3145760 | tf_op jit(solution)/shard_map/all_to_all | solution.py:490
  256.9 1.6 copy-done.4
  258.5 6.7 %shard_map.90 = bf16[144,1024]{1,0:T(8,128)(2,1)} custom-call(s32[160]{0:T(256)} %copy-done.11, bf16[192,8,1024]{2,1,0:T(8,128)(2,1)} %bitcast.32, bf16[5,128,256]{2,1,0:T(8,128)(2,1)} %get-tuple-element.36.refs_1_, f32[1280,128]{1,0:T(8,128)} %get-tuple-element.37.refs_2_, f32[5,8,128]{2,1,0:T(8,128)} %get-tuple-element.38.refs_3_, ...), custom_call_target="tpu_custom_call" | custom-call | flops 1342177280 | bytes 7864320 | tf_op jit(solution)/shard_map/pallas_call | solution.py:368
  265.2 1.5 collective-permute-start.3
  266.8 7.4 %collective-permute-start.4 = (bf16[144,1024]{1,0:T(8,128)(2,1)}, bf16[144,1024]{1,0:T(8,128)(2,1)S(1)}, u32[]{:S(2)}, u32[]{:S(2)}) collective-permute-start(bf16[144,1024]{1,0:T(8,128)(2,1)} %shard_map.90), channel_id=1, source_target_pairs={{0,2},{1,3},{4,6},{5,7},{8,10},{9,11},{12,14},{13,15},{16,18},{17,... | collective-permute-start | bytes 884744 | tf_op jit(solution)/shard_map/ppermute | solution.py:458
  274.1 1.3 collective-permute-start.5
  275.5 13.7 %shard_map.92.rest_3_ = bf16[1280,5120]{1,0:T(8,128)(2,1)} custom-call(s32[160]{0:T(256)} %copy-done.11, bf16[192,8,1024]{2,1,0:T(8,128)(2,1)} %bitcast.33, bf16[5,128,256]{2,1,0:T(8,128)(2,1)} %get-tuple-element.36.refs_1_, f32[1280,128]{1,0:T(8,128)} %get-tuple-element.37.refs_2_, ...), custom_call_target="tpu_custom_call", output_to_operand_aliasing={{}: (12, {})} | custom-call | flops 3355443200 | bytes 7864320 | tf_op jit(solution)/shard_map/pallas_call | solution.py:368
  289.1 7.6 %shard_map.93.rest_3_ = bf16[1280,5120]{1,0:T(8,128)(2,1)} custom-call(bf16[1280,384]{1,0:T(8,128)(2,1)} %bitcast.28, f32[1280,128]{1,0:T(8,128)} %get-tuple-element.32.entd_ref, bf16[144,2048]{1,0:T(8,128)(2,1)} %collective-permute-done.6.rest_0_, bf16[144,2048]{1,0:T(8,128)(2,1)} %collective-permute-done.7.rest_1_, ...), custom_call_target="tpu_custom_call", output_to_operand_aliasing={{}: (5, {})} | custom-call | flops 2013265920 | bytes 10485760 | tf_op jit(solution)/shard_map/pallas_call | solution.py:432
  298.3 5.5 %shard_map.94 = bf16[1280,5120]{1,0:T(8,128)(2,1)} custom-call(bf16[1280,384]{1,0:T(8,128)(2,1)} %bitcast.29, f32[1280,128]{1,0:T(8,128)} %get-tuple-element.32.entd_ref, bf16[144,1024]{1,0:T(8,128)(2,1)} %copy-done.8, bf16[144,1024]{1,0:T(8,128)(2,1)} %copy-done.9, bf16[144,1024]{1,0:T(8,128)(2,1)} %copy-done.10, ...), custom_call_target="tpu_custom_call", output_to_operand_aliasing={{}: (5, {})} | custom-call | flops 1006632960 | bytes 5242880 | tf_op jit(solution)/shard_map/pallas_call | solution.py:432
  (53 shorter events, 13.4 us)
Async XLA Ops:
  1.4 25.5 %copy-start.11 = (s32[160]{0:T(256)}, s32[160]{0:T(256)S(1)}, u32[]{:S(2)}) copy-start(s32[160]{0:T(256)S(1)} %multiply_add_fusion.ids_ref.slot_ref) | copy-start | bytes 1924
  2.2 14.7 %all-to-all-start = ((s32[32,1,6]{2,1,0:T(1,128)}), s32[32,1,6]{2,1,0:T(1,128)S(1)}, u32[]{:S(2)}, u32[]{:S(2)}) async-start(s32[32,1,6]{2,1,0:T(1,128)} %bitcast), calls=%async_computation | async-start | bytes 32768 | tf_op jit(solution)/shard_map/all_to_all | solution.py:481
  9.6 1.0 copy-start.1
  10.6 1.0 copy-start.2
  11.6 0.9 copy-start.3
  12.7 0.9 copy-start
  26.9 99.0 %all-to-all-start.1 = ((bf16[32,48,2432]{2,1,0:T(8,128)(2,1)}), bf16[32,48,2432]{2,1,0:T(8,128)(2,1)}, u32[]{:S(2)}, u32[]{:S(2)}) async-start(bf16[32,48,2432]{2,1,0:T(8,128)(2,1)} %bitcast.30), calls=%async_computation.1 | async-start | bytes 14942208 | tf_op jit(solution)/shard_map/all_to_all | solution.py:490
  31.8 98.9 %copy-start.12 = (f32[80]{0:T(128)S(1)}, f32[80]{0:T(128)}, u32[]{:S(2)}) copy-start(f32[80]{0:T(128)} %param.13) | copy-start | bytes 964
  31.8 99.7 %copy-start.13 = (f32[80]{0:T(128)S(1)}, f32[80]{0:T(128)}, u32[]{:S(2)}) copy-start(f32[80]{0:T(128)} %param.12) | copy-start | bytes 964
  31.8 100.3 %copy-start.14 = (s32[1,6]{1,0:T(1,128)S(1)}, s32[1,6]{1,0:T(1,128)}, u32[]{:S(2)}) copy-start(s32[1,6]{1,0:T(1,128)} %param.15) | copy-start | bytes 76
  125.8 82.8 %all-to-all-start.2 = ((bf16[32,48,2048]{2,1,0:T(8,128)(2,1)}), bf16[32,48,2048]{2,1,0:T(8,128)(2,1)}, u32[]{:S(2)}, u32[]{:S(2)}) async-start(bf16[32,48,2048]{2,1,0:T(8,128)(2,1)} %bitcast.31), calls=%async_computation.2 | async-start | bytes 12582912 | tf_op jit(solution)/shard_map/all_to_all | solution.py:490
  165.9 17.8 %collective-permute-start = (bf16[144,2048]{1,0:T(8,128)(2,1)}, bf16[144,2048]{1,0:T(8,128)(2,1)S(1)}, u32[]{:S(2)}, u32[]{:S(2)}) collective-permute-start(bf16[144,2048]{1,0:T(8,128)(2,1)} %get-tuple-element.44), channel_id=1, source_target_pairs={{0,1},{1,2},{2,3},{4,5},{5,6},{6,7},{8,9},{9,10},{10,11},{12,13},{... | collective-permute-start | bytes 1769480 | tf_op jit(solution)/shard_map/ppermute | solution.py:458
  169.8 25.8 %collective-permute-start.1 = (bf16[144,2048]{1,0:T(8,128)(2,1)}, bf16[144,2048]{1,0:T(8,128)(2,1)S(1)}, u32[]{:S(2)}, u32[]{:S(2)}) collective-permute-start(bf16[144,2048]{1,0:T(8,128)(2,1)} %get-tuple-element.44), channel_id=1, source_target_pairs={{0,2},{1,3},{4,6},{5,7},{8,10},{9,11},{12,14},{13,15},{16,18},{17,... | collective-permute-start | bytes 1769480 | tf_op jit(solution)/shard_map/ppermute | solution.py:458
  175.3 24.0 %collective-permute-start.2 = (bf16[144,2048]{1,0:T(8,128)(2,1)}, bf16[144,2048]{1,0:T(8,128)(2,1)S(1)}, u32[]{:S(2)}, u32[]{:S(2)}) collective-permute-start(bf16[144,2048]{1,0:T(8,128)(2,1)} %get-tuple-element.44), channel_id=1, source_target_pairs={{0,3},{4,7},{8,11},{12,15},{16,19},{20,23},{24,27},{28,31},{32,35}... | collective-permute-start | bytes 1769480 | tf_op jit(solution)/shard_map/ppermute | solution.py:458
  183.8 15.5 %copy-start.5 = (bf16[144,2048]{1,0:T(8,128)(2,1)}, bf16[144,2048]{1,0:T(8,128)(2,1)S(1)}, u32[]{:S(2)}) copy-start(bf16[144,2048]{1,0:T(8,128)(2,1)S(1)} %collective-permute-done.rest_0_) | copy-start | bytes 1769476
  195.6 3.7 %copy-start.6 = (bf16[144,2048]{1,0:T(8,128)(2,1)}, bf16[144,2048]{1,0:T(8,128)(2,1)S(1)}, u32[]{:S(2)}) copy-start(bf16[144,2048]{1,0:T(8,128)(2,1)S(1)} %collective-permute-done.1.rest_1_) | copy-start | bytes 1769476
  199.3 0.8 copy-start.7
  208.7 48.2 %all-to-all-start.3 = ((bf16[32,48,1024]{2,1,0:T(8,128)(2,1)}), bf16[32,48,1024]{2,1,0:T(8,128)(2,1)S(1)}, u32[]{:S(2)}, u32[]{:S(2)}) async-start(bf16[32,48,1024]{2,1,0:T(8,128)(2,1)} %bitcast.34), calls=%async_computation.3 | async-start | bytes 6291456 | tf_op jit(solution)/shard_map/all_to_all | solution.py:490
  238.0 36.1 %collective-permute-start.6 = (bf16[144,2048]{1,0:T(8,128)(2,1)}, bf16[144,2048]{1,0:T(8,128)(2,1)}, u32[]{:S(2)}, u32[]{:S(2)}) collective-permute-start(bf16[144,2048]{1,0:T(8,128)(2,1)} %get-tuple-element.49), channel_id=1, source_target_pairs={{0,1},{1,2},{2,3},{4,5},{5,6},{6,7},{8,9},{9,10},{10,11},{12,13},{... | collective-permute-start | bytes 1769480 | tf_op jit(solution)/shard_map/ppermute | solution.py:458
  240.3 48.8 %collective-permute-start.7 = (bf16[144,2048]{1,0:T(8,128)(2,1)}, bf16[144,2048]{1,0:T(8,128)(2,1)}, u32[]{:S(2)}, u32[]{:S(2)}) collective-permute-start(bf16[144,2048]{1,0:T(8,128)(2,1)} %get-tuple-element.49), channel_id=1, source_target_pairs={{0,2},{1,3},{4,6},{5,7},{8,10},{9,11},{12,14},{13,15},{16,18},{17,... | collective-permute-start | bytes 1769480 | tf_op jit(solution)/shard_map/ppermute | solution.py:458
  247.7 41.4 %collective-permute-start.8 = (bf16[144,2048]{1,0:T(8,128)(2,1)}, bf16[144,2048]{1,0:T(8,128)(2,1)}, u32[]{:S(2)}, u32[]{:S(2)}) collective-permute-start(bf16[144,2048]{1,0:T(8,128)(2,1)} %get-tuple-element.49), channel_id=1, source_target_pairs={{0,3},{4,7},{8,11},{12,15},{16,19},{20,23},{24,27},{28,31},{32,35}... | collective-permute-start | bytes 1769480 | tf_op jit(solution)/shard_map/ppermute | solution.py:458
  256.9 1.6 copy-start.4
  265.2 31.5 %collective-permute-start.3 = (bf16[144,1024]{1,0:T(8,128)(2,1)}, bf16[144,1024]{1,0:T(8,128)(2,1)S(1)}, u32[]{:S(2)}, u32[]{:S(2)}) collective-permute-start(bf16[144,1024]{1,0:T(8,128)(2,1)} %shard_map.90), channel_id=1, source_target_pairs={{0,1},{1,2},{2,3},{4,5},{5,6},{6,7},{8,9},{9,10},{10,11},{12,13},{... | collective-permute-start | bytes 884744 | tf_op jit(solution)/shard_map/ppermute | solution.py:458
  266.8 30.0 %collective-permute-start.4 = (bf16[144,1024]{1,0:T(8,128)(2,1)}, bf16[144,1024]{1,0:T(8,128)(2,1)S(1)}, u32[]{:S(2)}, u32[]{:S(2)}) collective-permute-start(bf16[144,1024]{1,0:T(8,128)(2,1)} %shard_map.90), channel_id=1, source_target_pairs={{0,2},{1,3},{4,6},{5,7},{8,10},{9,11},{12,14},{13,15},{16,18},{17,... | collective-permute-start | bytes 884744 | tf_op jit(solution)/shard_map/ppermute | solution.py:458
  274.1 22.6 %collective-permute-start.5 = (bf16[144,1024]{1,0:T(8,128)(2,1)}, bf16[144,1024]{1,0:T(8,128)(2,1)S(1)}, u32[]{:S(2)}, u32[]{:S(2)}) collective-permute-start(bf16[144,1024]{1,0:T(8,128)(2,1)} %shard_map.90), channel_id=1, source_target_pairs={{0,3},{4,7},{8,11},{12,15},{16,19},{20,23},{24,27},{28,31},{32,35}... | collective-permute-start | bytes 884744 | tf_op jit(solution)/shard_map/ppermute | solution.py:458
  296.8 0.7 copy-start.8
  296.8 0.8 copy-start.9
  297.6 0.7 copy-start.10

commit v5 on v4

--- a/solution.py
+++ b/solution.py
@@ -12,8 +12,8 @@
 SEG = 8
 LANES = 128
 AUX = 3 * LANES
-GROUP = 16
-PARTS = (32, 32, 16)
+GROUP = 8
+PARTS = (40, 32, 8)
 CHUNK = 16
 LOG2E = math.log2(math.e)
 CEILING = 64.0
@@ -527,16 +527,17 @@
     got.append(exchange(sent[1]))
     aux = pick_runs(slot, got[0], widths[0], AUX).reshape(tokens, AUX)
     tables = prepare(aux, 0, decay_row, scalars)
-    end, result = work(0, None, True, True)
+    (end,) = work(0, None, True, False)
     send_end(end)
+    (result,) = work(0, None, False, True)
     result = entering(0, result)
     got[1], sent[2], result = lax.optimization_barrier((got[1], sent[2], result))
     got.append(exchange(sent[2]))
-    end, result = work(1, result, True, True)
+    (end,) = work(1, None, True, False)
     send_end(end)
-    (end,) = work(2, None, True, False)
+    (result,) = work(1, result, False, True)
+    end, result = work(2, result, True, True)
     send_end(end)
-    (result,) = work(2, result, False, True)
     result = entering(1, result)
     result = entering(2, result)
     return result[None]

time: 306 us -> 313 us (1.023)
  Pallas kernels: 117 us -> 134 us
  starting transfers between devices: 56.5 us -> 49.6 us
    pallas_call x4 -> x5, Pallas kernels: 66 us -> 82 us  [blocks(): pl.pallas_call(kernel, out_shape=tuple(out_shape), grid_spec=pltpu.Prefet...]
    ppermute x9, waiting for transfers between devices: 17.4 us -> 2.49 us  [shifted(): lax.ppermute(block, 'seq', [(i, i + distance) for i in range(count - dist...]
    all_to_all x3, waiting for transfers between devices: 95.3 us -> 107 us  [exchange(): rows = lax.all_to_all(rows, 'dp', split_axis=0, concat_axis=0, tiled=True)]
    ppermute x9, starting transfers between devices: 32.7 us -> 24.8 us  [shifted(): lax.ppermute(block, 'seq', [(i, i + distance) for i in range(count - dist...]
    unnamed x30 -> x36, local copies, waits for them, and re-layouts: 7.78 us -> 8.25 us
  transfers between devices with their start and end apart: 13 -> 13, of which waited for: 7 -> 4; matrix products, arithmetic and copies ran while one was open for 1% -> 1% of each run, Pallas kernels for 34% -> 39%
where the time goes in v5:
time: 313 us; the launch traced here: 311 us
  Pallas kernels  134 us (43%)
  waiting for transfers between devices  113 us (36%)
  starting transfers between devices  49.6 us (16%)
  local copies, waits for them, and re-layouts  11.6 us (4%)
    all_to_all x3, waiting for transfers between devices, exchange(): rows = lax.all_to_all(rows, 'dp', split_axis=0, concat_axis=0, tiled=True)  107 us
    pallas_call x5, Pallas kernels, blocks(): pl.pallas_call(kernel, out_shape=tuple(out_shape), grid_spec=pltpu.Prefet...  82 us
    ppermute x9, starting transfers between devices, shifted(): lax.ppermute(block, 'seq', [(i, i + distance) for i in range(count - dist...  24.8 us
    pallas_call x4, Pallas kernels, pick_runs(): pl.pallas_call(kernel, out_shape=jax.ShapeDtypeStruct((count, SEG, total)...  24.4 us
    pallas_call x3, Pallas kernels, add_entering(): pl.pallas_call(kernel, out_shape=jax.ShapeDtypeStruct(result.shape, resul...  20.7 us
    all_to_all x3, starting transfers between devices, exchange(): rows = lax.all_to_all(rows, 'dp', split_axis=0, concat_axis=0, tiled=True)  17.4 us
    unnamed x36, local copies, waits for them, and re-layouts  8.25 us
    all_to_all x1, starting transfers between devices, on_device(): lax.all_to_all(asked.reshape(peers, capacity), 'dp', split_axis=0, concat...  7.4 us
  transfers between devices with their start and end apart: 13, of which 4 were waited for; matrix products, arithmetic and copies ran while one was open for 1% of the time, Pallas kernels for 39%

profile of v5, /device:TPU:0, one launch (start us, length us, event | category | flops | bytes accessed | tf_op | source)
XLA Modules:
  0.0 310.8 jit_solution(12519363642644672736)
XLA Ops:
  2.2 7.4 %all-to-all-start = ((s32[32,1,6]{2,1,0:T(1,128)}), s32[32,1,6]{2,1,0:T(1,128)S(1)}, u32[]{:S(2)}, u32[]{:S(2)}) async-start(s32[32,1,6]{2,1,0:T(1,128)} %bitcast), calls=%async_computation | async-start | bytes 32768 | tf_op jit(solution)/shard_map/all_to_all | solution.py:481
  9.6 1.0 copy-done.1
  10.6 1.0 copy-done.2
  13.7 3.2 %all-to-all-done = s32[32,1,6]{2,1,0:T(1,128)S(1)} async-done(((s32[32,1,6]{2,1,0:T(1,128)}), s32[32,1,6]{2,1,0:T(1,128)S(1)}, u32[]{:S(2)}, u32[]{:S(2)}) %all-to-all-start) | async-done | bytes 800 | tf_op jit(solution)/shard_map/all_to_all | solution.py:481
  18.8 8.9 %shard_map.83 = bf16[192,8,2944]{2,1,0:T(8,128)(2,1)} custom-call(s32[192]{0:T(256)} %reshape.101.ids_ref, bf16[160,8,5120]{2,1,0:T(8,128)(2,1)} %bitcast.18, bf16[160,8,384]{2,1,0:T(8,128)(2,1)} %bitcast.16), custom_call_target="tpu_custom_call" | custom-call | bytes 18087936 | tf_op jit(solution)/shard_map/pallas_call | solution.py:71
  27.7 5.0 %all-to-all-start.1 = ((bf16[32,48,2944]{2,1,0:T(8,128)(2,1)}), bf16[32,48,2944]{2,1,0:T(8,128)(2,1)}, u32[]{:S(2)}, u32[]{:S(2)}) async-start(bf16[32,48,2944]{2,1,0:T(8,128)(2,1)} %bitcast.30), calls=%async_computation.1 | async-start | bytes 18087936 | tf_op jit(solution)/shard_map/all_to_all | solution.py:490
  32.7 7.4 %shard_map.84 = bf16[192,8,2048]{2,1,0:T(8,128)(2,1)} custom-call(s32[192]{0:T(256)} %reshape.101.ids_ref, bf16[160,8,5120]{2,1,0:T(8,128)(2,1)} %bitcast.19), custom_call_target="tpu_custom_call" | custom-call | bytes 12582912 | tf_op jit(solution)/shard_map/pallas_call | solution.py:71
  40.1 106.8 %all-to-all-done.1 = bf16[32,48,2944]{2,1,0:T(8,128)(2,1)} async-done(((bf16[32,48,2944]{2,1,0:T(8,128)(2,1)}), bf16[32,48,2944]{2,1,0:T(8,128)(2,1)}, u32[]{:S(2)}, u32[]{:S(2)}) %all-to-all-start.1) | async-done | bytes 9044000 | tf_op jit(solution)/shard_map/all_to_all | solution.py:490
  146.9 4.9 %all-to-all-start.2 = ((bf16[32,48,2048]{2,1,0:T(8,128)(2,1)}), bf16[32,48,2048]{2,1,0:T(8,128)(2,1)}, u32[]{:S(2)}, u32[]{:S(2)}) async-start(bf16[32,48,2048]{2,1,0:T(8,128)(2,1)} %bitcast.31), calls=%async_computation.2 | async-start | bytes 12582912 | tf_op jit(solution)/shard_map/all_to_all | solution.py:490
  153.7 4.3 %shard_map.87 = bf16[192,8,512]{2,1,0:T(8,128)(2,1)} custom-call(s32[192]{0:T(256)} %reshape.101.ids_ref, bf16[160,8,5120]{2,1,0:T(8,128)(2,1)} %bitcast.20), custom_call_target="tpu_custom_call" | custom-call | bytes 3145728 | tf_op jit(solution)/shard_map/pallas_call | solution.py:71
  158.1 3.7 %shard_map.85 = bf16[160,8,384]{2,1,0:T(8,128)(2,1)} custom-call(s32[160]{0:T(256)} %copy-done.14, bf16[192,8,2944]{2,1,0:T(8,128)(2,1)} %bitcast.5.refs_0_), custom_call_target="tpu_custom_call" | custom-call | bytes 1966080 | tf_op jit(solution)/shard_map/pallas_call | solution.py:71
  161.8 6.6 %shard_map.86 = (f32[1280,128]{1,0:T(8,128)}, f32[5,128,256]{2,1,0:T(8,128)}, f32[5,256,256]{2,1,0:T(8,128)}, bf16[5,128,256]{2,1,0:T(8,128)(2,1)}, f32[1280,128...) custom-call(s32[7]{0:T(128)} %pad_add_fusion.sc_ref, ...), custom_call_target="tpu_custom_call" | custom-call | flops 587202560 | bytes 6291456 | tf_op jit(solution)/shard_map/pallas_call | solution.py:165
  168.4 12.2 %shard_map.88 = bf16[144,2560]{1,0:T(8,128)(2,1)} custom-call(s32[160]{0:T(256)} %copy-done.14, bf16[192,8,2944]{2,1,0:T(8,128)(2,1)} %bitcast.5.refs_0_, bf16[5,128,256]{2,1,0:T(8,128)(2,1)} %get-tuple-element.34.refs_1_, f32[1280,128]{1,0:T(8,128)} %get-tuple-element.35.refs_2_, f32[5,8,128]{2,1,0:T(8,128)} %get-tuple-element.36.refs_3_, ...), custom_call_target="tpu_custom_call" | custom-call | flops 3355443200 | bytes 19660800 | tf_op jit(solution)/shard_map/pallas_call | solution.py:368
  180.6 3.8 %collective-permute-start = (bf16[144,2560]{1,0:T(8,128)(2,1)}, bf16[144,2560]{1,0:T(8,128)(2,1)S(1)}, u32[]{:S(2)}, u32[]{:S(2)}) collective-permute-start(bf16[144,2560]{1,0:T(8,128)(2,1)} %shard_map.88), channel_id=1, source_target_pairs={{0,1},{1,2},{2,3},{4,5},{5,6},{6,7},{8,9},{9,10},{10,11},{12,13},{... | collective-permute-start | bytes 2211848 | tf_op jit(solution)/shard_map/ppermute | solution.py:458
  184.4 5.6 %collective-permute-start.1 = (bf16[144,2560]{1,0:T(8,128)(2,1)}, bf16[144,2560]{1,0:T(8,128)(2,1)S(1)}, u32[]{:S(2)}, u32[]{:S(2)}) collective-permute-start(bf16[144,2560]{1,0:T(8,128)(2,1)} %shard_map.88), channel_id=1, source_target_pairs={{0,2},{1,3},{4,6},{5,7},{8,10},{9,11},{12,14},{13,15},{16,18},{17,... | collective-permute-start | bytes 2211848 | tf_op jit(solution)/shard_map/ppermute | solution.py:458
  190.0 1.3 collective-permute-start.2
  191.4 26.4 %shard_map.89.rest_3_ = bf16[1280,5120]{1,0:T(8,128)(2,1)} custom-call(s32[160]{0:T(256)} %copy-done.14, bf16[192,8,2944]{2,1,0:T(8,128)(2,1)} %bitcast.5.refs_0_, bf16[5,128,256]{2,1,0:T(8,128)(2,1)} %get-tuple-element.34.refs_1_, f32[1280,128]{1,0:T(8,128)} %get-tuple-element.35.refs_2_, f32[5,8,128]{2,1,0:T(8,128)} %get-tuple-element.36.refs_3_, ...), custom_call_target="tpu_custom_call" | custom-call | flops 8388608000 | bytes 19660800 | tf_op jit(solution)/shard_map/pallas_call | solution.py:368
  217.8 2.5 collective-permute-done.2.rest_2_
  221.1 8.6 %shard_map.90.refs_11_ = bf16[1280,5120]{1,0:T(8,128)(2,1)} custom-call(bf16[1280,384]{1,0:T(8,128)(2,1)} %bitcast.25, f32[1280,128]{1,0:T(8,128)} %get-tuple-element.30.entd_ref, bf16[144,2560]{1,0:T(8,128)(2,1)} %copy-done.5, bf16[144,2560]{1,0:T(8,128)(2,1)} %copy-done.6, bf16[144,2560]{1,0:T(8,128)(2,1)} %copy-done.7, ...), custom_call_target="tpu_custom_call", output_to_operand_aliasing={{}: (5, {})} | custom-call | flops 2516582400 | bytes 13107200 | tf_op jit(solution)/shard_map/pallas_call | solution.py:432
  229.8 7.5 %all-to-all-start.3 = ((bf16[32,48,512]{2,1,0:T(8,128)(2,1)}), bf16[32,48,512]{2,1,0:T(8,128)(2,1)S(1)}, u32[]{:S(2)}, u32[]{:S(2)}) async-start(bf16[32,48,512]{2,1,0:T(8,128)(2,1)} %bitcast.12), calls=%async_computation.3 | async-start | bytes 3145728 | tf_op jit(solution)/shard_map/all_to_all | solution.py:490
  237.3 10.7 %shard_map.93 = bf16[144,2048]{1,0:T(8,128)(2,1)} custom-call(s32[160]{0:T(256)} %copy-done.14, bf16[192,8,2048]{2,1,0:T(8,128)(2,1)} %bitcast.11.refs_0_, bf16[5,128,256]{2,1,0:T(8,128)(2,1)} %get-tuple-element.34.refs_1_, f32[1280,128]{1,0:T(8,128)} %get-tuple-element.35.refs_2_, f32[5,8,128]{2,1,0:T(8,128)} %get-tuple-element.36.refs_3_, ...), custom_call_target="tpu_custom_call" | custom-call | flops 2684354560 | bytes 15728640 | tf_op jit(solution)/shard_map/pallas_call | solution.py:368
  248.0 1.3 collective-permute-start.6
  249.4 7.6 %collective-permute-start.7 = (bf16[144,2048]{1,0:T(8,128)(2,1)}, bf16[144,2048]{1,0:T(8,128)(2,1)S(1)}, u32[]{:S(2)}, u32[]{:S(2)}) collective-permute-start(bf16[144,2048]{1,0:T(8,128)(2,1)} %shard_map.93), channel_id=1, source_target_pairs={{0,2},{1,3},{4,6},{5,7},{8,10},{9,11},{12,14},{13,15},{16,18},{17,... | collective-permute-start | bytes 1769480 | tf_op jit(solution)/shard_map/ppermute | solution.py:458
  256.9 1.3 collective-permute-start.8
  258.3 22.3 %shard_map.91.refs_11_ = bf16[1280,5120]{1,0:T(8,128)(2,1)} custom-call(s32[160]{0:T(256)} %copy-done.14, bf16[192,8,2048]{2,1,0:T(8,128)(2,1)} %bitcast.11.refs_0_, bf16[5,128,256]{2,1,0:T(8,128)(2,1)} %get-tuple-element.34.refs_1_, f32[1280,128]{1,0:T(8,128)} %get-tuple-element.35.refs_2_, ...), custom_call_target="tpu_custom_call", output_to_operand_aliasing={{}: (12, {})} | custom-call | flops 6710886400 | bytes 15728640 | tf_op jit(solution)/shard_map/pallas_call | solution.py:368
  280.6 1.2 copy-done.4
  281.7 10.4 %shard_map.92 = (bf16[144,512]{1,0:T(8,128)(2,1)}, bf16[1280,5120]{1,0:T(8,128)(2,1)}) custom-call(s32[160]{0:T(256)} %copy-done.14, bf16[192,8,512]{2,1,0:T(8,128)(2,1)} %bitcast.32, bf16[5,128,256]{2,1,0:T(8,128)(2,1)} %get-tuple-element.34.refs_1_, f32[1280,128]{1,0:T(8,128)} %get-tuple-element.35.refs_2_, ...), custom_call_target="tpu_custom_call", output_to_operand_aliasing={{1}: (12, {})} | custom-call | flops 1677721600 | bytes 3932160 | tf_op jit(solution)/shard_map/pallas_call | solution.py:368
  292.1 1.3 collective-permute-start.3
  293.4 1.3 collective-permute-start.4
  294.7 1.3 collective-permute-start.5
  297.1 7.6 %shard_map.94.rest_3_ = bf16[1280,5120]{1,0:T(8,128)(2,1)} custom-call(bf16[1280,384]{1,0:T(8,128)(2,1)} %bitcast.28, f32[1280,128]{1,0:T(8,128)} %get-tuple-element.30.entd_ref, bf16[144,2048]{1,0:T(8,128)(2,1)} %copy-done.8, bf16[144,2048]{1,0:T(8,128)(2,1)} %copy-done.9, bf16[144,2048]{1,0:T(8,128)(2,1)} %copy-done.10, ...), custom_call_target="tpu_custom_call", output_to_operand_aliasing={{}: (5, {})} | custom-call | flops 2013265920 | bytes 10485760 | tf_op jit(solution)/shard_map/pallas_call | solution.py:432
  306.1 4.5 %shard_map.95 = bf16[1280,5120]{1,0:T(8,128)(2,1)} custom-call(bf16[1280,384]{1,0:T(8,128)(2,1)} %bitcast.29, f32[1280,128]{1,0:T(8,128)} %get-tuple-element.30.entd_ref, bf16[144,512]{1,0:T(8,128)(2,1)} %copy-done.11, bf16[144,512]{1,0:T(8,128)(2,1)} %copy-done.12, bf16[144,512]{1,0:T(8,128)(2,1)} %copy-done.13, ...), custom_call_target="tpu_custom_call", output_to_operand_aliasing={{}: (5, {})} | custom-call | flops 503316480 | bytes 2621440 | tf_op jit(solution)/shard_map/pallas_call | solution.py:432
  (60 shorter events, 11.4 us)
Async XLA Ops:
  1.4 26.3 %copy-start.14 = (s32[160]{0:T(256)}, s32[160]{0:T(256)S(1)}, u32[]{:S(2)}) copy-start(s32[160]{0:T(256)S(1)} %multiply_add_fusion.ids_ref.slot_ref) | copy-start | bytes 1924
  2.2 14.7 %all-to-all-start = ((s32[32,1,6]{2,1,0:T(1,128)}), s32[32,1,6]{2,1,0:T(1,128)S(1)}, u32[]{:S(2)}, u32[]{:S(2)}) async-start(s32[32,1,6]{2,1,0:T(1,128)} %bitcast), calls=%async_computation | async-start | bytes 32768 | tf_op jit(solution)/shard_map/all_to_all | solution.py:481
  9.6 1.0 copy-start.1
  10.6 1.0 copy-start.2
  11.6 0.9 copy-start.3
  12.7 0.9 copy-start
  27.7 119.3 %all-to-all-start.1 = ((bf16[32,48,2944]{2,1,0:T(8,128)(2,1)}), bf16[32,48,2944]{2,1,0:T(8,128)(2,1)}, u32[]{:S(2)}, u32[]{:S(2)}) async-start(bf16[32,48,2944]{2,1,0:T(8,128)(2,1)} %bitcast.30), calls=%async_computation.1 | async-start | bytes 18087936 | tf_op jit(solution)/shard_map/all_to_all | solution.py:490
  32.7 119.2 %copy-start.15 = (f32[80]{0:T(128)S(1)}, f32[80]{0:T(128)}, u32[]{:S(2)}) copy-start(f32[80]{0:T(128)} %param.13) | copy-start | bytes 964
  32.7 120.0 %copy-start.16 = (f32[80]{0:T(128)S(1)}, f32[80]{0:T(128)}, u32[]{:S(2)}) copy-start(f32[80]{0:T(128)} %param.12) | copy-start | bytes 964
  32.7 120.5 %copy-start.17 = (s32[1,6]{1,0:T(1,128)S(1)}, s32[1,6]{1,0:T(1,128)}, u32[]{:S(2)}) copy-start(s32[1,6]{1,0:T(1,128)} %param.15) | copy-start | bytes 76
  146.9 82.8 %all-to-all-start.2 = ((bf16[32,48,2048]{2,1,0:T(8,128)(2,1)}), bf16[32,48,2048]{2,1,0:T(8,128)(2,1)}, u32[]{:S(2)}, u32[]{:S(2)}) async-start(bf16[32,48,2048]{2,1,0:T(8,128)(2,1)} %bitcast.31), calls=%async_computation.2 | async-start | bytes 12582912 | tf_op jit(solution)/shard_map/all_to_all | solution.py:490
  180.6 37.1 %collective-permute-start = (bf16[144,2560]{1,0:T(8,128)(2,1)}, bf16[144,2560]{1,0:T(8,128)(2,1)S(1)}, u32[]{:S(2)}, u32[]{:S(2)}) collective-permute-start(bf16[144,2560]{1,0:T(8,128)(2,1)} %shard_map.88), channel_id=1, source_target_pairs={{0,1},{1,2},{2,3},{4,5},{5,6},{6,7},{8,9},{9,10},{10,11},{12,13},{... | collective-permute-start | bytes 2211848 | tf_op jit(solution)/shard_map/ppermute | solution.py:458
  184.4 33.3 %collective-permute-start.1 = (bf16[144,2560]{1,0:T(8,128)(2,1)}, bf16[144,2560]{1,0:T(8,128)(2,1)S(1)}, u32[]{:S(2)}, u32[]{:S(2)}) collective-permute-start(bf16[144,2560]{1,0:T(8,128)(2,1)} %shard_map.88), channel_id=1, source_target_pairs={{0,2},{1,3},{4,6},{5,7},{8,10},{9,11},{12,14},{13,15},{16,18},{17,... | collective-permute-start | bytes 2211848 | tf_op jit(solution)/shard_map/ppermute | solution.py:458
  190.0 30.2 %collective-permute-start.2 = (bf16[144,2560]{1,0:T(8,128)(2,1)}, bf16[144,2560]{1,0:T(8,128)(2,1)S(1)}, u32[]{:S(2)}, u32[]{:S(2)}) collective-permute-start(bf16[144,2560]{1,0:T(8,128)(2,1)} %shard_map.88), channel_id=1, source_target_pairs={{0,3},{4,7},{8,11},{12,15},{16,19},{20,23},{24,27},{28,31},{32,35}... | collective-permute-start | bytes 2211848 | tf_op jit(solution)/shard_map/ppermute | solution.py:458
  217.8 2.5 copy-start.5
  217.8 2.5 copy-start.6
  220.3 0.9 copy-start.7
  229.8 50.8 %all-to-all-start.3 = ((bf16[32,48,512]{2,1,0:T(8,128)(2,1)}), bf16[32,48,512]{2,1,0:T(8,128)(2,1)S(1)}, u32[]{:S(2)}, u32[]{:S(2)}) async-start(bf16[32,48,512]{2,1,0:T(8,128)(2,1)} %bitcast.12), calls=%async_computation.3 | async-start | bytes 3145728 | tf_op jit(solution)/shard_map/all_to_all | solution.py:490
  248.0 46.7 %collective-permute-start.6 = (bf16[144,2048]{1,0:T(8,128)(2,1)}, bf16[144,2048]{1,0:T(8,128)(2,1)S(1)}, u32[]{:S(2)}, u32[]{:S(2)}) collective-permute-start(bf16[144,2048]{1,0:T(8,128)(2,1)} %shard_map.93), channel_id=1, source_target_pairs={{0,1},{1,2},{2,3},{4,5},{5,6},{6,7},{8,9},{9,10},{10,11},{12,13},{... | collective-permute-start | bytes 1769480 | tf_op jit(solution)/shard_map/ppermute | solution.py:458
  249.4 46.7 %collective-permute-start.7 = (bf16[144,2048]{1,0:T(8,128)(2,1)}, bf16[144,2048]{1,0:T(8,128)(2,1)S(1)}, u32[]{:S(2)}, u32[]{:S(2)}) collective-permute-start(bf16[144,2048]{1,0:T(8,128)(2,1)} %shard_map.93), channel_id=1, source_target_pairs={{0,2},{1,3},{4,6},{5,7},{8,10},{9,11},{12,14},{13,15},{16,18},{17,... | collective-permute-start | bytes 1769480 | tf_op jit(solution)/shard_map/ppermute | solution.py:458
  256.9 39.1 %collective-permute-start.8 = (bf16[144,2048]{1,0:T(8,128)(2,1)}, bf16[144,2048]{1,0:T(8,128)(2,1)S(1)}, u32[]{:S(2)}, u32[]{:S(2)}) collective-permute-start(bf16[144,2048]{1,0:T(8,128)(2,1)} %shard_map.93), channel_id=1, source_target_pairs={{0,3},{4,7},{8,11},{12,15},{16,19},{20,23},{24,27},{28,31},{32,35}... | collective-permute-start | bytes 1769480 | tf_op jit(solution)/shard_map/ppermute | solution.py:458
  280.6 1.2 copy-start.4
  292.1 12.6 %collective-permute-start.3 = (bf16[144,512]{1,0:T(8,128)(2,1)}, bf16[144,512]{1,0:T(8,128)(2,1)S(1)}, u32[]{:S(2)}, u32[]{:S(2)}) collective-permute-start(bf16[144,512]{1,0:T(8,128)(2,1)} %get-tuple-element.45), channel_id=1, source_target_pairs={{0,1},{1,2},{2,3},{4,5},{5,6},{6,7},{8,9},{9,10},{10,11},{12,13},{... | collective-permute-start | bytes 442376 | tf_op jit(solution)/shard_map/ppermute | solution.py:458
  293.4 11.3 %collective-permute-start.4 = (bf16[144,512]{1,0:T(8,128)(2,1)}, bf16[144,512]{1,0:T(8,128)(2,1)S(1)}, u32[]{:S(2)}, u32[]{:S(2)}) collective-permute-start(bf16[144,512]{1,0:T(8,128)(2,1)} %get-tuple-element.45), channel_id=1, source_target_pairs={{0,2},{1,3},{4,6},{5,7},{8,10},{9,11},{12,14},{13,15},{16,18},{17,... | collective-permute-start | bytes 442376 | tf_op jit(solution)/shard_map/ppermute | solution.py:458
  294.7 1.4 copy-start.8
  294.7 10.0 %collective-permute-start.5 = (bf16[144,512]{1,0:T(8,128)(2,1)}, bf16[144,512]{1,0:T(8,128)(2,1)S(1)}, u32[]{:S(2)}, u32[]{:S(2)}) collective-permute-start(bf16[144,512]{1,0:T(8,128)(2,1)} %get-tuple-element.45), channel_id=1, source_target_pairs={{0,3},{4,7},{8,11},{12,15},{16,19},{20,23},{24,27},{28,31},{32,35}... | collective-permute-start | bytes 442376 | tf_op jit(solution)/shard_map/ppermute | solution.py:458
  296.1 0.8 copy-start.9
  296.1 1.0 copy-start.10
  304.7 0.7 copy-start.11
  304.7 0.7 copy-start.12
  305.5 0.7 copy-start.13

commit v6 on v3

--- a/solution.py
+++ b/solution.py
@@ -43,7 +43,7 @@
 
         @pl.loop(0, chunks)
         def _(c):
-            @pl.loop(0, chunk)
+            @pl.loop(0, chunk, unroll=chunk)
             def _(i):
                 place = c * chunk + i
                 run = ids_ref[place]
@@ -233,6 +233,8 @@
     place = first_head * head_width // width
     half = SPAN // 2
     runs = SPAN // SEG
+    in_order = got.ndim == 4
+    hand_on = with_end and not with_local
 
     def kernel(slot_ref, *refs):
         refs = list(refs)
@@ -245,6 +247,8 @@
                 del refs[:1]
         if with_end:
             final_ref = refs.pop(0)
+        if hand_on:
+            packed_ref, packed_sems = refs.pop(0), refs[-1]
         if with_local:
             out_ref = refs.pop(0)
             outs_held, out_sems = refs[-2:]
@@ -252,7 +256,11 @@
 
         @pl.loop(0, spans)
         def _(j):
-            @pl.loop(0, runs, unroll=8)
+            if in_order:
+                pltpu.make_async_copy(got_ref.at[j], held.at[j], sems.at[j]).start()
+                return
+
+            @pl.loop(0, runs, unroll=runs)
             def _(i):
                 pltpu.make_async_copy(
                     got_ref.at[slot_ref[j * runs + i], :, pl.ds(0, width)], held.at[j, i], sems.at[j]
@@ -285,6 +293,8 @@
                     written(j - 2).wait()
 
             pltpu.make_async_copy(held.at[j], held.at[j], sems.at[j]).wait()
+            if hand_on:
+                pltpu.make_async_copy(held.at[j], packed_ref.at[j], packed_sems.at[j]).start()
 
             for g in range(groups):
                 head = first_head + g * GROUP
@@ -334,6 +344,12 @@
                 final_ref[0:LANES, columns] = state[:, columns].astype(bf16)
                 high, low = halves(spread(through_all, matrix[g]))
                 final_ref[LANES : LANES + 16, columns] = jnp.concatenate([high, low], axis=0)
+        if hand_on:
+
+            @pl.loop(0, spans)
+            def _(j):
+                pltpu.make_async_copy(held.at[j], packed_ref.at[j], packed_sems.at[j]).wait()
+
         if with_local:
             for j in range(max(spans - 2, 0), spans):
                 written(jnp.int32(j)).wait()
@@ -355,6 +371,10 @@
     if with_end:
         out_shape.append(jax.ShapeDtypeStruct((LANES + 16, width), bf16))
         out_specs.append(pl.BlockSpec((LANES + 16, width), lambda i, s: (0, 0)))
+    if hand_on:
+        out_shape.append(jax.ShapeDtypeStruct((spans, runs, SEG, width), bf16))
+        out_specs.append(anywhere)
+        scratch.append(pltpu.SemaphoreType.DMA((spans,)))
     if with_local:
         operands += [aux, cum, rt, scores, entry, skip_row]
         in_specs += [whole(aux, LANES, query_at), whole(cum), whole(rt), whole(scores), whole(entry)]
@@ -509,9 +529,9 @@
         wanted, sent[i] = lax.optimization_barrier((wanted, sent[i]))
     got, arrived = [], []
 
-    def work(i, result, with_end, with_local):
+    def work(i, result, with_end, with_local, rows=None):
         return blocks(
-            got[i], slot, widths[i], firsts[i], head_width, tables, aux, query_at, skip_row, result,
+            got[i] if rows is None else rows, slot, widths[i], firsts[i], head_width, tables, aux, query_at, skip_row, result,
             whole_width, with_end, with_local,
         )
 
@@ -533,12 +553,12 @@
     result = entering(0, result)
     got[1], sent[2], result = lax.optimization_barrier((got[1], sent[2], result))
     got.append(exchange(sent[2]))
-    (end,) = work(1, None, True, False)
+    end, rows = work(1, None, True, False)
     send_end(end)
-    (result,) = work(1, result, False, True)
-    (end,) = work(2, None, True, False)
+    (result,) = work(1, result, False, True, rows)
+    end, rows = work(2, None, True, False)
     send_end(end)
-    (result,) = work(2, result, False, True)
+    (result,) = work(2, result, False, True, rows)
     result = entering(1, result)
     result = entering(2, result)
     return result[None]

time: 305 us -> 305 us (level)
  no operation moved by 1% of the time
where the time goes in v6:
time: 305 us; the launch traced here: 303 us
  Pallas kernels  125 us (41%)
  waiting for transfers between devices  110 us (36%)
  starting transfers between devices  54 us (18%)
  local copies, waits for them, and re-layouts  11.1 us (4%)
    all_to_all x3, waiting for transfers between devices, exchange(): rows = lax.all_to_all(rows, 'dp', split_axis=0, concat_axis=0, tiled=True)  89.2 us
    pallas_call x5, Pallas kernels, blocks(): pl.pallas_call(kernel, out_shape=tuple(out_shape), grid_spec=pltpu.Prefet...  74.9 us
    ppermute x9, starting transfers between devices, shifted(): lax.ppermute(block, 'seq', [(i, i + distance) for i in range(count - dist...  31.1 us
    pallas_call x4, Pallas kernels, pick_runs(): pl.pallas_call(kernel, out_shape=jax.ShapeDtypeStruct((count, SEG, total)...  22.8 us
    pallas_call x3, Pallas kernels, add_entering(): pl.pallas_call(kernel, out_shape=jax.ShapeDtypeStruct(result.shape, resul...  20.7 us
    ppermute x9, waiting for transfers between devices, shifted(): lax.ppermute(block, 'seq', [(i, i + distance) for i in range(count - dist...  17.5 us
    all_to_all x3, starting transfers between devices, exchange(): rows = lax.all_to_all(rows, 'dp', split_axis=0, concat_axis=0, tiled=True)  15.5 us
    unnamed x30, local copies, waits for them, and re-layouts  7.82 us
  transfers between devices with their start and end apart: 13, of which 6 were waited for; matrix products, arithmetic and copies ran while one was open for 1% of the time, Pallas kernels for 37%

profile of v6, /device:TPU:0, one launch (start us, length us, event | category | flops | bytes accessed | tf_op | source)
XLA Modules:
  0.0 303.5 jit_solution(7154704705060227159)
XLA Ops:
  2.2 7.4 %all-to-all-start = ((s32[32,1,6]{2,1,0:T(1,128)}), s32[32,1,6]{2,1,0:T(1,128)S(1)}, u32[]{:S(2)}, u32[]{:S(2)}) async-start(s32[32,1,6]{2,1,0:T(1,128)} %bitcast), calls=%async_computation | async-start | bytes 32768 | tf_op jit(solution)/shard_map/all_to_all | solution.py:502
  13.7 3.2 %all-to-all-done = s32[32,1,6]{2,1,0:T(1,128)S(1)} async-done(((s32[32,1,6]{2,1,0:T(1,128)}), s32[32,1,6]{2,1,0:T(1,128)S(1)}, u32[]{:S(2)}, u32[]{:S(2)}) %all-to-all-start) | async-done | bytes 800 | tf_op jit(solution)/shard_map/all_to_all | solution.py:502
  18.8 8.2 %shard_map.83 = bf16[192,8,2432]{2,1,0:T(8,128)(2,1)} custom-call(s32[192]{0:T(256)} %reshape.101.ids_ref, bf16[160,8,5120]{2,1,0:T(8,128)(2,1)} %bitcast.18, bf16[160,8,384]{2,1,0:T(8,128)(2,1)} %bitcast.16), custom_call_target="tpu_custom_call" | custom-call | bytes 14942208 | tf_op jit(solution)/shard_map/pallas_call | solution.py:71
  27.0 5.0 %all-to-all-start.1 = ((bf16[32,48,2432]{2,1,0:T(8,128)(2,1)}), bf16[32,48,2432]{2,1,0:T(8,128)(2,1)}, u32[]{:S(2)}, u32[]{:S(2)}) async-start(bf16[32,48,2432]{2,1,0:T(8,128)(2,1)} %bitcast.30), calls=%async_computation.1 | async-start | bytes 14942208 | tf_op jit(solution)/shard_map/all_to_all | solution.py:511
  31.9 6.5 %shard_map.84 = bf16[192,8,2048]{2,1,0:T(8,128)(2,1)} custom-call(s32[192]{0:T(256)} %reshape.101.ids_ref, bf16[160,8,5120]{2,1,0:T(8,128)(2,1)} %bitcast.19), custom_call_target="tpu_custom_call" | custom-call | bytes 12582912 | tf_op jit(solution)/shard_map/pallas_call | solution.py:71
  38.5 87.5 %all-to-all-done.1 = bf16[32,48,2432]{2,1,0:T(8,128)(2,1)} async-done(((bf16[32,48,2432]{2,1,0:T(8,128)(2,1)}), bf16[32,48,2432]{2,1,0:T(8,128)(2,1)}, u32[]{:S(2)}, u32[]{:S(2)}) %all-to-all-start.1) | async-done | bytes 7471136 | tf_op jit(solution)/shard_map/all_to_all | solution.py:511
  126.0 4.9 %all-to-all-start.2 = ((bf16[32,48,2048]{2,1,0:T(8,128)(2,1)}), bf16[32,48,2048]{2,1,0:T(8,128)(2,1)}, u32[]{:S(2)}, u32[]{:S(2)}) async-start(bf16[32,48,2048]{2,1,0:T(8,128)(2,1)} %bitcast.31), calls=%async_computation.2 | async-start | bytes 12582912 | tf_op jit(solution)/shard_map/all_to_all | solution.py:511
  132.8 3.0 shard_map.85
  135.8 6.5 %shard_map.86 = (f32[1280,128]{1,0:T(8,128)}, f32[5,128,256]{2,1,0:T(8,128)}, f32[5,256,256]{2,1,0:T(8,128)}, bf16[5,128,256]{2,1,0:T(8,128)(2,1)}, f32[1280,128...) custom-call(s32[7]{0:T(128)} %pad_add_fusion.sc_ref, ...), custom_call_target="tpu_custom_call" | custom-call | flops 587202560 | bytes 6291456 | tf_op jit(solution)/shard_map/pallas_call | solution.py:165
  142.4 22.9 %shard_map.88 = (bf16[144,2048]{1,0:T(8,128)(2,1)}, bf16[1280,5120]{1,0:T(8,128)(2,1)}) custom-call(s32[160]{0:T(256)} %copy-done.11, bf16[192,8,2432]{2,1,0:T(8,128)(2,1)} %bitcast.5.refs_0_, bf16[5,128,256]{2,1,0:T(8,128)(2,1)} %get-tuple-element.38.refs_1_, f32[1280,128]{1,0:T(8,128)} %get-tuple-element.39.refs_2_, ...), custom_call_target="tpu_custom_call" | custom-call | flops 6710886400 | bytes 15728640 | tf_op jit(solution)/shard_map/pallas_call | solution.py:389
  165.3 3.9 %collective-permute-start = (bf16[144,2048]{1,0:T(8,128)(2,1)}, bf16[144,2048]{1,0:T(8,128)(2,1)S(1)}, u32[]{:S(2)}, u32[]{:S(2)}) collective-permute-start(bf16[144,2048]{1,0:T(8,128)(2,1)} %get-tuple-element.46), channel_id=1, source_target_pairs={{0,1},{1,2},{2,3},{4,5},{5,6},{6,7},{8,9},{9,10},{10,11},{12,13},{... | collective-permute-start | bytes 1769480 | tf_op jit(solution)/shard_map/ppermute | solution.py:479
  169.1 5.5 %collective-permute-start.1 = (bf16[144,2048]{1,0:T(8,128)(2,1)}, bf16[144,2048]{1,0:T(8,128)(2,1)S(1)}, u32[]{:S(2)}, u32[]{:S(2)}) collective-permute-start(bf16[144,2048]{1,0:T(8,128)(2,1)} %get-tuple-element.46), channel_id=1, source_target_pairs={{0,2},{1,3},{4,6},{5,7},{8,10},{9,11},{12,14},{13,15},{16,18},{17,... | collective-permute-start | bytes 1769480 | tf_op jit(solution)/shard_map/ppermute | solution.py:479
  174.6 1.3 collective-permute-start.2
  176.0 5.2 %shard_map.87 = bf16[192,8,1024]{2,1,0:T(8,128)(2,1)} custom-call(s32[192]{0:T(256)} %reshape.101.ids_ref, bf16[160,8,5120]{2,1,0:T(8,128)(2,1)} %bitcast.20), custom_call_target="tpu_custom_call" | custom-call | bytes 6291456 | tf_op jit(solution)/shard_map/pallas_call | solution.py:71
  181.1 2.0 collective-permute-done.rest_0_
  183.1 11.8 %collective-permute-done.1.rest_1_ = bf16[144,2048]{1,0:T(8,128)(2,1)S(1)} collective-permute-done((bf16[144,2048]{1,0:T(8,128)(2,1)}, bf16[144,2048]{1,0:T(8,128)(2,1)S(1)}, u32[]{:S(2)}, u32[]{:S(2)}) %collective-permute-start.1) | collective-permute-done | bytes 589856 | tf_op jit(solution)/shard_map/ppermute | solution.py:479
  194.9 3.7 %collective-permute-done.2.rest_2_ = bf16[144,2048]{1,0:T(8,128)(2,1)S(1)} collective-permute-done((bf16[144,2048]{1,0:T(8,128)(2,1)}, bf16[144,2048]{1,0:T(8,128)(2,1)S(1)}, u32[]{:S(2)}, u32[]{:S(2)}) %collective-permute-start.2) | collective-permute-done | bytes 589856 | tf_op jit(solution)/shard_map/ppermute | solution.py:479
  199.4 7.6 %shard_map.89.refs_11_ = bf16[1280,5120]{1,0:T(8,128)(2,1)} custom-call(bf16[1280,384]{1,0:T(8,128)(2,1)} %bitcast.25, f32[1280,128]{1,0:T(8,128)} %get-tuple-element.34.entd_ref, bf16[144,2048]{1,0:T(8,128)(2,1)} %copy-done.5, bf16[144,2048]{1,0:T(8,128)(2,1)} %copy-done.6, bf16[144,2048]{1,0:T(8,128)(2,1)} %copy-done.7, ...), custom_call_target="tpu_custom_call", output_to_operand_aliasing={{}: (5, {})} | custom-call | flops 2013265920 | bytes 10485760 | tf_op jit(solution)/shard_map/pallas_call | solution.py:453
  207.0 1.8 all-to-all-done.2
  208.8 5.6 %all-to-all-start.3 = ((bf16[32,48,1024]{2,1,0:T(8,128)(2,1)}), bf16[32,48,1024]{2,1,0:T(8,128)(2,1)S(1)}, u32[]{:S(2)}, u32[]{:S(2)}) async-start(bf16[32,48,1024]{2,1,0:T(8,128)(2,1)} %bitcast.12), calls=%async_computation.3 | async-start | bytes 6291456 | tf_op jit(solution)/shard_map/all_to_all | solution.py:511
  214.4 9.4 %shard_map.91 = (bf16[144,2048]{1,0:T(8,128)(2,1)}, bf16[5,32,8,2048]{3,2,1,0:T(8,128)(2,1)}) custom-call(s32[160]{0:T(256)} %copy-done.11, bf16[192,8,2048]{2,1,0:T(8,128)(2,1)} %bitcast.11.refs_0_, bf16[5,128,256]{2,1,0:T(8,128)(2,1)} %get-tuple-element.38.refs_1_, f32[1280,128]{1,0:T(8,128)} %get-tuple-element.39.refs_2_, ...), custom_call_target="tpu_custom_call" | custom-call | flops 2684354560 | bytes 15728640 | tf_op jit(solution)/shard_map/pallas_call | solution.py:389
  223.8 3.1 %collective-permute-start.6 = (bf16[144,2048]{1,0:T(8,128)(2,1)}, bf16[144,2048]{1,0:T(8,128)(2,1)}, u32[]{:S(2)}, u32[]{:S(2)}) collective-permute-start(bf16[144,2048]{1,0:T(8,128)(2,1)} %get-tuple-element.51), channel_id=1, source_target_pairs={{0,1},{1,2},{2,3},{4,5},{5,6},{6,7},{8,9},{9,10},{10,11},{12,13},{... | collective-permute-start | bytes 1769480 | tf_op jit(solution)/shard_map/ppermute | solution.py:479
  226.9 6.6 %collective-permute-start.7 = (bf16[144,2048]{1,0:T(8,128)(2,1)}, bf16[144,2048]{1,0:T(8,128)(2,1)}, u32[]{:S(2)}, u32[]{:S(2)}) collective-permute-start(bf16[144,2048]{1,0:T(8,128)(2,1)} %get-tuple-element.51), channel_id=1, source_target_pairs={{0,2},{1,3},{4,6},{5,7},{8,10},{9,11},{12,14},{13,15},{16,18},{17,... | collective-permute-start | bytes 1769480 | tf_op jit(solution)/shard_map/ppermute | solution.py:479
  233.5 2.1 collective-permute-start.8
  235.6 22.1 %shard_map.92.refs_11_ = bf16[1280,5120]{1,0:T(8,128)(2,1)} custom-call(s32[160]{0:T(256)} %copy-done.11, bf16[5,32,8,2048]{3,2,1,0:T(8,128)(2,1)} %get-tuple-element.53.refs_0_, bf16[5,128,256]{2,1,0:T(8,128)(2,1)} %get-tuple-element.38.refs_1_, f32[1280,128]{1,0:T(8,128)} %get-tuple-element.39.refs_2_, ...), custom_call_target="tpu_custom_call", output_to_operand_aliasing={{}: (12, {})} | custom-call | flops 6710886400 | bytes 15728640 | tf_op jit(solution)/shard_map/pallas_call | solution.py:389
  257.8 1.6 copy-done.4
  259.4 6.8 %shard_map.90 = (bf16[144,1024]{1,0:T(8,128)(2,1)}, bf16[5,32,8,1024]{3,2,1,0:T(8,128)(2,1)}) custom-call(s32[160]{0:T(256)} %copy-done.11, bf16[192,8,1024]{2,1,0:T(8,128)(2,1)} %bitcast.32, bf16[5,128,256]{2,1,0:T(8,128)(2,1)} %get-tuple-element.38.refs_1_, f32[1280,128]{1,0:T(8,128)} %get-tuple-element.39.refs_2_, ...), custom_call_target="tpu_custom_call" | custom-call | flops 1342177280 | bytes 7864320 | tf_op jit(solution)/shard_map/pallas_call | solution.py:389
  267.6 6.0 %collective-permute-start.4 = (bf16[144,1024]{1,0:T(8,128)(2,1)}, bf16[144,1024]{1,0:T(8,128)(2,1)S(1)}, u32[]{:S(2)}, u32[]{:S(2)}) collective-permute-start(bf16[144,1024]{1,0:T(8,128)(2,1)} %get-tuple-element.49), channel_id=1, source_target_pairs={{0,2},{1,3},{4,6},{5,7},{8,10},{9,11},{12,14},{13,15},{16,18},{17,... | collective-permute-start | bytes 884744 | tf_op jit(solution)/shard_map/ppermute | solution.py:479
  273.6 1.3 collective-permute-start.5
  274.9 13.7 %shard_map.93.rest_3_ = bf16[1280,5120]{1,0:T(8,128)(2,1)} custom-call(s32[160]{0:T(256)} %copy-done.11, bf16[5,32,8,1024]{3,2,1,0:T(8,128)(2,1)} %get-tuple-element.52.refs_0_, bf16[5,128,256]{2,1,0:T(8,128)(2,1)} %get-tuple-element.38.refs_1_, f32[1280,128]{1,0:T(8,128)} %get-tuple-element.39.refs_2_, ...), custom_call_target="tpu_custom_call", output_to_operand_aliasing={{}: (12, {})} | custom-call | flops 3355443200 | bytes 7864320 | tf_op jit(solution)/shard_map/pallas_call | solution.py:389
  288.6 7.6 %shard_map.94.rest_3_ = bf16[1280,5120]{1,0:T(8,128)(2,1)} custom-call(bf16[1280,384]{1,0:T(8,128)(2,1)} %bitcast.28, f32[1280,128]{1,0:T(8,128)} %get-tuple-element.34.entd_ref, bf16[144,2048]{1,0:T(8,128)(2,1)} %collective-permute-done.6.rest_0_, bf16[144,2048]{1,0:T(8,128)(2,1)} %collective-permute-done.7.rest_1_, ...), custom_call_target="tpu_custom_call", output_to_operand_aliasing={{}: (5, {})} | custom-call | flops 2013265920 | bytes 10485760 | tf_op jit(solution)/shard_map/pallas_call | solution.py:453
  297.8 5.5 %shard_map.95 = bf16[1280,5120]{1,0:T(8,128)(2,1)} custom-call(bf16[1280,384]{1,0:T(8,128)(2,1)} %bitcast.29, f32[1280,128]{1,0:T(8,128)} %get-tuple-element.34.entd_ref, bf16[144,1024]{1,0:T(8,128)(2,1)} %copy-done.8, bf16[144,1024]{1,0:T(8,128)(2,1)} %copy-done.9, bf16[144,1024]{1,0:T(8,128)(2,1)} %copy-done.10, ...), custom_call_target="tpu_custom_call", output_to_operand_aliasing={{}: (5, {})} | custom-call | flops 1006632960 | bytes 5242880 | tf_op jit(solution)/shard_map/pallas_call | solution.py:453
  (54 shorter events, 13.7 us)
Async XLA Ops:
  1.4 25.6 %copy-start.11 = (s32[160]{0:T(256)}, s32[160]{0:T(256)S(1)}, u32[]{:S(2)}) copy-start(s32[160]{0:T(256)S(1)} %multiply_add_fusion.ids_ref.slot_ref) | copy-start | bytes 1924
  2.2 14.7 %all-to-all-start = ((s32[32,1,6]{2,1,0:T(1,128)}), s32[32,1,6]{2,1,0:T(1,128)S(1)}, u32[]{:S(2)}, u32[]{:S(2)}) async-start(s32[32,1,6]{2,1,0:T(1,128)} %bitcast), calls=%async_computation | async-start | bytes 32768 | tf_op jit(solution)/shard_map/all_to_all | solution.py:502
  9.6 1.0 copy-start.1
  10.6 1.0 copy-start.2
  11.6 0.9 copy-start.3
  12.7 1.0 copy-start
  27.0 99.0 %all-to-all-start.1 = ((bf16[32,48,2432]{2,1,0:T(8,128)(2,1)}), bf16[32,48,2432]{2,1,0:T(8,128)(2,1)}, u32[]{:S(2)}, u32[]{:S(2)}) async-start(bf16[32,48,2432]{2,1,0:T(8,128)(2,1)} %bitcast.30), calls=%async_computation.1 | async-start | bytes 14942208 | tf_op jit(solution)/shard_map/all_to_all | solution.py:511
  38.5 92.4 %copy-start.12 = (f32[80]{0:T(128)S(1)}, f32[80]{0:T(128)}, u32[]{:S(2)}) copy-start(f32[80]{0:T(128)} %param.13) | copy-start | bytes 964
  38.5 93.2 %copy-start.13 = (f32[80]{0:T(128)S(1)}, f32[80]{0:T(128)}, u32[]{:S(2)}) copy-start(f32[80]{0:T(128)} %param.12) | copy-start | bytes 964
  38.5 93.7 %copy-start.14 = (s32[1,6]{1,0:T(1,128)S(1)}, s32[1,6]{1,0:T(1,128)}, u32[]{:S(2)}) copy-start(s32[1,6]{1,0:T(1,128)} %param.15) | copy-start | bytes 76
  126.0 82.8 %all-to-all-start.2 = ((bf16[32,48,2048]{2,1,0:T(8,128)(2,1)}), bf16[32,48,2048]{2,1,0:T(8,128)(2,1)}, u32[]{:S(2)}, u32[]{:S(2)}) async-start(bf16[32,48,2048]{2,1,0:T(8,128)(2,1)} %bitcast.31), calls=%async_computation.2 | async-start | bytes 12582912 | tf_op jit(solution)/shard_map/all_to_all | solution.py:511
  165.3 17.8 %collective-permute-start = (bf16[144,2048]{1,0:T(8,128)(2,1)}, bf16[144,2048]{1,0:T(8,128)(2,1)S(1)}, u32[]{:S(2)}, u32[]{:S(2)}) collective-permute-start(bf16[144,2048]{1,0:T(8,128)(2,1)} %get-tuple-element.46), channel_id=1, source_target_pairs={{0,1},{1,2},{2,3},{4,5},{5,6},{6,7},{8,9},{9,10},{10,11},{12,13},{... | collective-permute-start | bytes 1769480 | tf_op jit(solution)/shard_map/ppermute | solution.py:479
  169.1 25.8 %collective-permute-start.1 = (bf16[144,2048]{1,0:T(8,128)(2,1)}, bf16[144,2048]{1,0:T(8,128)(2,1)S(1)}, u32[]{:S(2)}, u32[]{:S(2)}) collective-permute-start(bf16[144,2048]{1,0:T(8,128)(2,1)} %get-tuple-element.46), channel_id=1, source_target_pairs={{0,2},{1,3},{4,6},{5,7},{8,10},{9,11},{12,14},{13,15},{16,18},{17,... | collective-permute-start | bytes 1769480 | tf_op jit(solution)/shard_map/ppermute | solution.py:479
  174.6 24.0 %collective-permute-start.2 = (bf16[144,2048]{1,0:T(8,128)(2,1)}, bf16[144,2048]{1,0:T(8,128)(2,1)S(1)}, u32[]{:S(2)}, u32[]{:S(2)}) collective-permute-start(bf16[144,2048]{1,0:T(8,128)(2,1)} %get-tuple-element.46), channel_id=1, source_target_pairs={{0,3},{4,7},{8,11},{12,15},{16,19},{20,23},{24,27},{28,31},{32,35}... | collective-permute-start | bytes 1769480 | tf_op jit(solution)/shard_map/ppermute | solution.py:479
  183.1 15.5 %copy-start.5 = (bf16[144,2048]{1,0:T(8,128)(2,1)}, bf16[144,2048]{1,0:T(8,128)(2,1)S(1)}, u32[]{:S(2)}) copy-start(bf16[144,2048]{1,0:T(8,128)(2,1)S(1)} %collective-permute-done.rest_0_) | copy-start | bytes 1769476
  194.9 3.7 %copy-start.6 = (bf16[144,2048]{1,0:T(8,128)(2,1)}, bf16[144,2048]{1,0:T(8,128)(2,1)S(1)}, u32[]{:S(2)}) copy-start(bf16[144,2048]{1,0:T(8,128)(2,1)S(1)} %collective-permute-done.1.rest_1_) | copy-start | bytes 1769476
  198.6 0.8 copy-start.7
  208.8 49.0 %all-to-all-start.3 = ((bf16[32,48,1024]{2,1,0:T(8,128)(2,1)}), bf16[32,48,1024]{2,1,0:T(8,128)(2,1)S(1)}, u32[]{:S(2)}, u32[]{:S(2)}) async-start(bf16[32,48,1024]{2,1,0:T(8,128)(2,1)} %bitcast.12), calls=%async_computation.3 | async-start | bytes 6291456 | tf_op jit(solution)/shard_map/all_to_all | solution.py:511
  223.8 49.8 %collective-permute-start.6 = (bf16[144,2048]{1,0:T(8,128)(2,1)}, bf16[144,2048]{1,0:T(8,128)(2,1)}, u32[]{:S(2)}, u32[]{:S(2)}) collective-permute-start(bf16[144,2048]{1,0:T(8,128)(2,1)} %get-tuple-element.51), channel_id=1, source_target_pairs={{0,1},{1,2},{2,3},{4,5},{5,6},{6,7},{8,9},{9,10},{10,11},{12,13},{... | collective-permute-start | bytes 1769480 | tf_op jit(solution)/shard_map/ppermute | solution.py:479
  226.9 61.7 %collective-permute-start.7 = (bf16[144,2048]{1,0:T(8,128)(2,1)}, bf16[144,2048]{1,0:T(8,128)(2,1)}, u32[]{:S(2)}, u32[]{:S(2)}) collective-permute-start(bf16[144,2048]{1,0:T(8,128)(2,1)} %get-tuple-element.51), channel_id=1, source_target_pairs={{0,2},{1,3},{4,6},{5,7},{8,10},{9,11},{12,14},{13,15},{16,18},{17,... | collective-permute-start | bytes 1769480 | tf_op jit(solution)/shard_map/ppermute | solution.py:479
  233.5 55.1 %collective-permute-start.8 = (bf16[144,2048]{1,0:T(8,128)(2,1)}, bf16[144,2048]{1,0:T(8,128)(2,1)}, u32[]{:S(2)}, u32[]{:S(2)}) collective-permute-start(bf16[144,2048]{1,0:T(8,128)(2,1)} %get-tuple-element.51), channel_id=1, source_target_pairs={{0,3},{4,7},{8,11},{12,15},{16,19},{20,23},{24,27},{28,31},{32,35}... | collective-permute-start | bytes 1769480 | tf_op jit(solution)/shard_map/ppermute | solution.py:479
  257.8 1.6 copy-start.4
  266.3 30.0 %collective-permute-start.3 = (bf16[144,1024]{1,0:T(8,128)(2,1)}, bf16[144,1024]{1,0:T(8,128)(2,1)S(1)}, u32[]{:S(2)}, u32[]{:S(2)}) collective-permute-start(bf16[144,1024]{1,0:T(8,128)(2,1)} %get-tuple-element.49), channel_id=1, source_target_pairs={{0,1},{1,2},{2,3},{4,5},{5,6},{6,7},{8,9},{9,10},{10,11},{12,13},{... | collective-permute-start | bytes 884744 | tf_op jit(solution)/shard_map/ppermute | solution.py:479
  267.6 28.7 %collective-permute-start.4 = (bf16[144,1024]{1,0:T(8,128)(2,1)}, bf16[144,1024]{1,0:T(8,128)(2,1)S(1)}, u32[]{:S(2)}, u32[]{:S(2)}) collective-permute-start(bf16[144,1024]{1,0:T(8,128)(2,1)} %get-tuple-element.49), channel_id=1, source_target_pairs={{0,2},{1,3},{4,6},{5,7},{8,10},{9,11},{12,14},{13,15},{16,18},{17,... | collective-permute-start | bytes 884744 | tf_op jit(solution)/shard_map/ppermute | solution.py:479
  273.6 22.7 %collective-permute-start.5 = (bf16[144,1024]{1,0:T(8,128)(2,1)}, bf16[144,1024]{1,0:T(8,128)(2,1)S(1)}, u32[]{:S(2)}, u32[]{:S(2)}) collective-permute-start(bf16[144,1024]{1,0:T(8,128)(2,1)} %get-tuple-element.49), channel_id=1, source_target_pairs={{0,3},{4,7},{8,11},{12,15},{16,19},{20,23},{24,27},{28,31},{32,35}... | collective-permute-start | bytes 884744 | tf_op jit(solution)/shard_map/ppermute | solution.py:479
  296.2 0.7 copy-start.8
  296.3 0.8 copy-start.9
  297.1 0.7 copy-start.10
